TPU v7x, 32 devices: a whole 2x2x4 slice. The times are simulated.
32 devices in a mesh: shard: 8 (over z, x), ctx: 2 (over y), tensor: 2 (over core).
Axes of the slice: x: 2, y: 2, z: 4, core: 2. Of those that a mesh axis runs over, the one named last changes fastest.
Arguments:
- clip_input: bfloat16 [8, 8, 392, 512], P('shard', 'ctx', None, 'tensor'), may hold values from -6 to 6
- cotangent: bfloat16 [8, 8, 392, 512], P('shard', 'ctx', None, 'tensor'), may hold values from -6 to 6
- gain_one: float32 [512], P('tensor'), may hold values from 0.1 to 1.9
- shift_one: float32 [512], P('tensor'), may hold values from -3 to 3
- w_qkv: bfloat16 [3, 512, 512], P(None, 'shard', 'tensor'), may hold values from -0.25 to 0.25
- b_qv: float32 [2, 512], P(None, 'tensor'), may hold values from -3 to 3
- w_proj: bfloat16 [512, 512], P('tensor', 'shard'), may hold values from -1.5 to 1.5
- b_proj: float32 [512], P('tensor'), may hold values from -3 to 3
- bias_table: float32 [16, 2535], P('tensor'), may hold values from -3 to 3
- gain_two: float32 [512], P('tensor'), may hold values from 0.1 to 1.9
- shift_two: float32 [512], P('tensor'), may hold values from -3 to 3
- w_fc1: bfloat16 [512, 2048], P('shard', 'tensor'), may hold values from -0.25 to 0.25
- b_fc1: float32 [2048], P('tensor'), may hold values from -3 to 3
- w_fc2: bfloat16 [2048, 512], P('tensor', 'shard'), may hold values from -0.125 to 0.125
- b_fc2: float32 [512], P('tensor'), may hold values from -3 to 3
- rel_index: int32 [392, 392], replicated, may hold values from 0 to 2534
- regions: int32 [8, 392], P('ctx'), may hold values from 0 to 3
Outputs:
- block_out: float32 [8, 8, 392, 512], P('shard', 'ctx', None, 'tensor')
- grad_input: float32 [8, 8, 392, 512], P('shard', 'ctx', None, 'tensor')
- grad_gain_one: float32 [512], P('tensor')
- grad_shift_one: float32 [512], P('tensor')
- grad_w_qkv: float32 [3, 512, 512], P(None, 'shard', 'tensor')
- grad_b_qv: float32 [2, 512], P(None, 'tensor')
- grad_w_proj: float32 [512, 512], P('tensor', 'shard')
- grad_b_proj: float32 [512], P('tensor')
- grad_table: float32 [16, 2535], P('tensor')
- grad_gain_two: float32 [512], P('tensor')
- grad_shift_two: float32 [512], P('tensor')
- grad_w_fc1: float32 [512, 2048], P('shard', 'tensor')
- grad_b_fc1: float32 [2048], P('tensor')
- grad_w_fc2: float32 [2048, 512], P('tensor', 'shard')
- grad_b_fc2: float32 [512], P('tensor')
Inputs may be any that keep to these rules, and one draw needn't show every extreme that they name: `rel_index`: a table entry for every pair of a window's tokens.
All inputs are finite; a program needn't handle non-finite values.
Results may differ from a plain program's by a relative error of at most 0.015.
Values may be sent and summed in bfloat16 or wider, within the bound.
No kernel may reach another device: no remote copies, remote signals or barrier semaphores. Data moves between devices by JAX's collectives and lax.ppermute only.
A program may use at most 192 MiB of HBM per device.

v0:
```python
import jax
import jax.numpy as jnp
from jax import lax
from jax.sharding import PartitionSpec as P

D = 512
HD = 32
WT = 8
WH = 7
WW = 7
TABLE = 2535


EPSILON = 1e-05
HIGHEST = lax.Precision.HIGHEST
FINE_COUNT = 64


def partner(value, axis, bit):
    mask = 2**bit
    pairs = [(source, source ^ mask) for source in range(lax.axis_size(axis))]
    return lax.ppermute(value, axis, pairs)


def exact_gelu(values):
    return jax.nn.gelu(values, approximate=False)


def row_sums(first_term, second_term):
    return lax.psum((jnp.sum(first_term, -1), jnp.sum(second_term, -1)), "tensor")


def norm_forward(values, norm_gain, norm_shift):
    total, squares = row_sums(values, values * values)
    center = total / D
    inv_std = lax.rsqrt(squares / D - center * center + EPSILON)
    normed = (values - center[:, None]) * inv_std[:, None]
    return (normed, inv_std, (normed * norm_gain + norm_shift).astype(jnp.bfloat16))


def norm_backward(upstream, normed, inv_std, norm_gain):
    scaled = upstream * norm_gain
    total, along = row_sums(scaled, scaled * normed)
    return inv_std[:, None] * (scaled - total[:, None] / D - normed * along[:, None] / D)


def full_width(half_rows):
    return lax.all_gather(half_rows, "tensor", axis=1, tiled=True)


def tensor_sum(term):
    return lax.psum_scatter(term, "tensor", scatter_dimension=1, tiled=True)


def row_block_size(tokens):
    best = 1
    for candidate in range(1, 33):
        if tokens % candidate == 0:
            best = candidate
    return best


def index_tables(index_block, coarse_count):
    flat_index = index_block.reshape(-1)
    coarse_table = (flat_index[:, None] // FINE_COUNT == jnp.arange(coarse_count)[None, :]).astype(
        jnp.float32
    )
    fine_table = (flat_index[:, None] % FINE_COUNT == jnp.arange(FINE_COUNT)[None, :]).astype(
        jnp.float32
    )
    return (coarse_table, fine_table)


def table_lookup(bias_table, rel_index):
    head_count, table_size = bias_table.shape
    tokens = rel_index.shape[0]
    coarse_count = -(-table_size // FINE_COUNT)
    padded = jnp.pad(bias_table, ((0, 0), (0, coarse_count * FINE_COUNT - table_size)))
    padded = padded.reshape(head_count, coarse_count, FINE_COUNT)
    block_rows = row_block_size(tokens)
    index_blocks = rel_index.reshape(tokens // block_rows, block_rows, tokens)

    def lookup_block(index_block):
        coarse_table, fine_table = index_tables(index_block, coarse_count)
        picked = jnp.einsum("hab,pa->hpb", padded, coarse_table, precision=HIGHEST)
        return jnp.sum(picked * fine_table[None], -1).reshape(head_count, block_rows, tokens)

    looked = lax.map(lookup_block, index_blocks)
    return looked.transpose(1, 0, 2, 3).reshape(head_count, tokens, tokens)


def table_accumulate(pair_grads, rel_index, table_size):
    head_count, tokens, _ = pair_grads.shape
    coarse_count = -(-table_size // FINE_COUNT)
    block_rows = row_block_size(tokens)
    block_count = tokens // block_rows
    index_blocks = rel_index.reshape(block_count, block_rows, tokens)
    grad_blocks = pair_grads.reshape(head_count, block_count, block_rows * tokens).transpose(
        1, 0, 2
    )

    def fold_block(carry, operands):
        index_block, grad_block = operands
        coarse_table, fine_table = index_tables(index_block, coarse_count)
        weighted = grad_block[:, :, None] * fine_table[None]
        return (carry + jnp.einsum("hpb,pa->hab", weighted, coarse_table, precision=HIGHEST), None)

    start = jnp.zeros((head_count, coarse_count, FINE_COUNT), jnp.float32)
    folded, _ = lax.scan(fold_block, start, (index_blocks, grad_blocks))
    return folded.reshape(head_count, coarse_count * FINE_COUNT)[:, :table_size]


def window_roll(flat_rows, clip_count, counts, backward):
    levels = lax.axis_size("ctx").bit_length() - 1
    shaped = flat_rows.reshape((clip_count,) + counts + (WT, WH, WW, flat_rows.shape[-1]))
    for axis_pos in range(3):
        token_axis = 4 + axis_pos
        length = shaped.shape[token_axis]
        border = length - length // 2 if backward else length // 2
        before = lax.slice_in_dim(shaped, 0, border, axis=token_axis)
        after_cut = lax.slice_in_dim(shaped, border, length, axis=token_axis)
        moving = after_cut if backward else before
        if axis_pos < levels:
            moving = partner(moving, "ctx", levels - 1 - axis_pos)
        else:
            moving = jnp.roll(moving, 1 if backward else -1, axis=1 + axis_pos)
        if backward:
            shaped = jnp.concatenate((moving, before), axis=token_axis)
        else:
            shaped = jnp.concatenate((after_cut, moving), axis=token_axis)
    return shaped.reshape(flat_rows.shape)


def on_device(
    clip_input,
    cotangent,
    gain_one,
    shift_one,
    w_qkv,
    b_qv,
    w_proj,
    b_proj,
    bias_table,
    gain_two,
    shift_two,
    w_fc1,
    b_fc1,
    w_fc2,
    b_fc2,
    rel_index,
    regions,
):
    clip_count, window_count, tokens, half_width = clip_input.shape
    head_count = bias_table.shape[0]
    head_width = w_qkv.shape[2]
    levels = lax.axis_size("ctx").bit_length() - 1
    counts = tuple((1 if axis_pos < levels else 2 for axis_pos in range(3)))
    qkv_full, proj_full, fc1_full, fc2_full = (
        lax.all_gather(w_qkv, "shard", axis=1, tiled=True),
        lax.all_gather(w_proj, "shard", axis=1, tiled=True),
        lax.all_gather(w_fc1, "shard", axis=0, tiled=True),
        lax.all_gather(w_fc2, "shard", axis=1, tiled=True),
    )
    scale = HD ** (-0.5)
    rows_in = clip_input.astype(jnp.float32).reshape(-1, half_width)
    normed_one, inv_one, first_norm = norm_forward(rows_in, gain_one, shift_one)
    moved_rows = full_width(window_roll(first_norm, clip_count, counts, False))
    projected = jnp.einsum("rd,cde->rce", moved_rows, qkv_full, preferred_element_type=jnp.float32)
    queries = (projected[:, 0] + b_qv[0]).astype(jnp.bfloat16)
    key_rows = projected[:, 1].astype(jnp.bfloat16)
    values = (projected[:, 2] + b_qv[1]).astype(jnp.bfloat16)
    bias_full = table_lookup(bias_table, rel_index)
    labels = jnp.tile(regions, (clip_count, 1)).reshape(-1, 2, tokens)

    def blocked(flat_rows):
        return flat_rows.reshape(-1, 2, tokens, head_count, HD)

    def scored(query_block, key_block, label_block):
        raw_scores = jnp.einsum(
            "bqhd,bkhd->bhqk", query_block, key_block, preferred_element_type=jnp.float32
        )
        mask_add = jnp.where(label_block[:, :, None] == label_block[:, None, :], 0.0, -100.0)
        return raw_scores * scale + bias_full[None] + mask_add[:, None]

    def attend_block(operands):
        query_block, key_block, value_block, label_block = operands
        scores = scored(query_block, key_block, label_block)
        row_peak = jnp.max(scores, -1, keepdims=True)
        weights_exp = jnp.exp(scores - row_peak)
        row_total = jnp.sum(weights_exp, -1, keepdims=True)
        soft_probs = (weights_exp / row_total).astype(jnp.bfloat16)
        mixed_out = jnp.einsum(
            "bhqk,bkhd->bqhd", soft_probs, value_block, preferred_element_type=jnp.float32
        )
        return (mixed_out.astype(jnp.bfloat16), row_peak[..., 0] + jnp.log(row_total[..., 0]))

    mixed_out, logsum = lax.map(
        attend_block, (blocked(queries), blocked(key_rows), blocked(values), labels)
    )
    attended = mixed_out.reshape(-1, head_width)
    restored = window_roll(attended, clip_count, counts, True)
    branch = tensor_sum(jnp.dot(restored, proj_full, preferred_element_type=jnp.float32)) + b_proj
    middle = rows_in + branch
    normed_two, inv_two, second_norm = norm_forward(middle, gain_two, shift_two)
    second_full = full_width(second_norm)
    hidden = jnp.dot(second_full, fc1_full, preferred_element_type=jnp.float32) + b_fc1
    active, gelu_back = jax.vjp(exact_gelu, hidden)
    active = active.astype(jnp.bfloat16)
    block_out = middle + (
        tensor_sum(jnp.dot(active, fc2_full, preferred_element_type=jnp.float32)) + b_fc2
    )
    upstream = cotangent.reshape(-1, half_width)
    grad_out = upstream.astype(jnp.float32)
    out_full = full_width(upstream)
    grad_fc2 = jnp.einsum("rf,rd->fd", active, out_full, preferred_element_type=jnp.float32)
    grad_active = jnp.einsum("rd,fd->rf", out_full, fc2_full, preferred_element_type=jnp.float32)
    grad_hidden = gelu_back(grad_active)[0].astype(jnp.bfloat16)
    grad_fc1 = jnp.einsum("rd,rf->df", second_full, grad_hidden, preferred_element_type=jnp.float32)
    grad_second = tensor_sum(
        jnp.einsum("rf,df->rd", grad_hidden, fc1_full, preferred_element_type=jnp.float32)
    )
    grad_middle = grad_out + norm_backward(grad_second, normed_two, inv_two, gain_two)
    grad_branch = grad_middle.astype(jnp.bfloat16)
    branch_full = full_width(grad_branch)
    grad_proj = jnp.einsum("re,rd->ed", restored, branch_full, preferred_element_type=jnp.float32)
    grad_restored = jnp.einsum(
        "rd,ed->re", branch_full, proj_full, preferred_element_type=jnp.float32
    )
    grad_attended = window_roll(grad_restored.astype(jnp.bfloat16), clip_count, counts, False)

    def attend_back(pair_total, operands):
        query_block, key_block, value_block, label_block, grad_block, logsum_block = operands
        scores = scored(query_block, key_block, label_block)
        soft_probs = jnp.exp(scores - logsum_block[..., None])
        grad_probs = jnp.einsum(
            "bqhd,bkhd->bhqk", grad_block, value_block, preferred_element_type=jnp.float32
        )
        grad_value = jnp.einsum(
            "bhqk,bqhd->bkhd",
            soft_probs.astype(jnp.bfloat16),
            grad_block,
            preferred_element_type=jnp.float32,
        )
        grad_scores = soft_probs * (
            grad_probs - jnp.sum(grad_probs * soft_probs, -1, keepdims=True)
        )
        grad_scores = grad_scores.astype(jnp.bfloat16)
        grad_query = (
            jnp.einsum(
                "bhqk,bkhd->bqhd", grad_scores, key_block, preferred_element_type=jnp.float32
            )
            * scale
        )
        grad_key = (
            jnp.einsum(
                "bhqk,bqhd->bkhd", grad_scores, query_block, preferred_element_type=jnp.float32
            )
            * scale
        )
        pair_total = pair_total + jnp.sum(grad_scores.astype(jnp.float32), 0)
        return (
            pair_total,
            (
                grad_query.astype(jnp.bfloat16),
                grad_key.astype(jnp.bfloat16),
                grad_value.astype(jnp.bfloat16),
            ),
        )

    pair_total, (grad_queries, grad_keys, grad_values) = lax.scan(
        attend_back,
        jnp.zeros((head_count, tokens, tokens), jnp.float32),
        (
            blocked(queries),
            blocked(key_rows),
            blocked(values),
            labels,
            blocked(grad_attended),
            logsum,
        ),
    )
    table_grad = table_accumulate(pair_total, rel_index, TABLE)
    grad_queries = grad_queries.reshape(-1, head_width)
    grad_keys = grad_keys.reshape(-1, head_width)
    grad_values = grad_values.reshape(-1, head_width)
    grad_stack = jnp.stack((grad_queries, grad_keys, grad_values), axis=1)
    grad_qkv = jnp.einsum("rd,rce->cde", moved_rows, grad_stack, preferred_element_type=jnp.float32)
    grad_moved = tensor_sum(
        jnp.einsum("rce,cde->rd", grad_stack, qkv_full, preferred_element_type=jnp.float32)
    )
    grad_first = window_roll(grad_moved.astype(jnp.bfloat16), clip_count, counts, True).astype(
        jnp.float32
    )
    grad_rows = grad_middle + norm_backward(grad_first, normed_one, inv_one, gain_one)
    small_terms = (
        table_grad,
        jnp.stack(
            (
                jnp.sum(grad_queries.astype(jnp.float32), 0),
                jnp.sum(grad_values.astype(jnp.float32), 0),
            )
        ),
        jnp.sum(grad_branch.astype(jnp.float32), 0),
        jnp.sum(grad_first * normed_one, 0),
        jnp.sum(grad_first, 0),
        jnp.sum(grad_second * normed_two, 0),
        jnp.sum(grad_second, 0),
        jnp.sum(grad_hidden.astype(jnp.float32), 0),
        jnp.sum(grad_out, 0),
    )
    (
        grad_table,
        grad_b_qv,
        grad_b_proj,
        grad_gain_one,
        grad_shift_one,
        grad_gain_two,
        grad_shift_two,
        grad_b_fc1,
        grad_b_fc2,
    ) = lax.psum(
        (
            small_terms[0],
            small_terms[1],
            small_terms[2],
            small_terms[3],
            small_terms[4],
            small_terms[5],
            small_terms[6],
            small_terms[7],
            small_terms[8],
        ),
        ("shard", "ctx"),
    )
    weight_grads = (grad_qkv, grad_proj, grad_fc1, grad_fc2)
    summed_grads = (
        lax.psum_scatter(weight_grads[0], ("shard", "ctx"), scatter_dimension=1, tiled=True),
        lax.psum_scatter(weight_grads[1], ("shard", "ctx"), scatter_dimension=1, tiled=True),
        lax.psum_scatter(weight_grads[2], ("shard", "ctx"), scatter_dimension=0, tiled=True),
        lax.psum_scatter(weight_grads[3], ("shard", "ctx"), scatter_dimension=1, tiled=True),
    )
    summed_grads = (
        lax.all_gather(summed_grads[0].astype(jnp.bfloat16), "ctx", axis=1, tiled=True).astype(
            jnp.float32
        ),
        lax.all_gather(summed_grads[1].astype(jnp.bfloat16), "ctx", axis=1, tiled=True).astype(
            jnp.float32
        ),
        lax.all_gather(summed_grads[2].astype(jnp.bfloat16), "ctx", axis=0, tiled=True).astype(
            jnp.float32
        ),
        lax.all_gather(summed_grads[3].astype(jnp.bfloat16), "ctx", axis=1, tiled=True).astype(
            jnp.float32
        ),
    )
    grad_w_qkv, grad_w_proj, grad_w_fc1, grad_w_fc2 = summed_grads
    return (
        block_out.reshape(clip_input.shape),
        grad_rows.reshape(clip_input.shape),
        grad_gain_one,
        grad_shift_one,
        grad_w_qkv,
        grad_b_qv,
        grad_w_proj,
        grad_b_proj,
        grad_table,
        grad_gain_two,
        grad_shift_two,
        grad_w_fc1,
        grad_b_fc1,
        grad_w_fc2,
        grad_b_fc2,
    )


def solution(mesh):
    in_specs = (
        P("shard", "ctx", None, "tensor"),
        P("shard", "ctx", None, "tensor"),
        P("tensor"),
        P("tensor"),
        P(None, "shard", "tensor"),
        P(None, "tensor"),
        P("tensor", "shard"),
        P("tensor"),
        P("tensor", None),
        P("tensor"),
        P("tensor"),
        P("shard", "tensor"),
        P("tensor"),
        P("tensor", "shard"),
        P("tensor"),
        P(),
        P("ctx", None),
    )
    out_specs = (
        P("shard", "ctx", None, "tensor"),
        P("shard", "ctx", None, "tensor"),
        P("tensor"),
        P("tensor"),
        P(None, "shard", "tensor"),
        P(None, "tensor"),
        P("tensor", "shard"),
        P("tensor"),
        P("tensor", None),
        P("tensor"),
        P("tensor"),
        P("shard", "tensor"),
        P("tensor"),
        P("tensor", "shard"),
        P("tensor"),
    )
    return jax.shard_map(
        on_device, mesh=mesh, in_specs=in_specs, out_specs=out_specs, check_vma=False
    )
```

profile of v0, /device:TPU:0, one launch (start us, length us, event | category | flops | bytes accessed | tf_op | source)
XLA Modules:
  0.0 1216.4 jit_solution(10167951428865030951)
XLA Ops:
  8.1 9.2 fusion.111
  33.3 9.7 collective-permute-done
  49.6 6.9 fusion.95
  57.8 181.3 %while.54 = (s32[]{:T(128)}, f32[14,8,28,392]{3,1,2,0:T(8,128)}, s32[14,28,392]{2,1,0:T(8,128)S(1)}, f32[8,40,64]{2,1,0:T(8,128)S(1)}, s32[]{:T(128)}) while((s32[]{:T(128)}, f32[14,8,28,392]{3,1,2,0:T(8,128)}, s32[14,28,392]{2,1,0:T(8,128)S(1)}, f32[8,40,64]{2,1,0:T(8,128)S(1)}, s32[]{:T(128)}) %tuple.139), condition=%wide.region_6.7_spmd, body=%wide.region_4.6_spmd.sunk | while | flops 2710665984 | bytes 7960525 | solution.py:88
  58.1 11.1 multiply_reduce_fusion.12
  71.1 11.1 multiply_reduce_fusion.12
  84.0 11.1 multiply_reduce_fusion.12
  97.0 11.1 multiply_reduce_fusion.12
  109.9 11.1 multiply_reduce_fusion.12
  122.8 11.1 multiply_reduce_fusion.12
  135.8 11.1 multiply_reduce_fusion.12
  148.7 11.1 multiply_reduce_fusion.12
  161.7 11.1 multiply_reduce_fusion.12
  174.6 11.1 multiply_reduce_fusion.12
  187.6 11.1 multiply_reduce_fusion.12
  200.5 11.1 multiply_reduce_fusion.12
  213.5 11.1 multiply_reduce_fusion.12
  226.5 11.1 multiply_reduce_fusion.12
  239.3 32.9 %all_gather.37 = bf16[3,512,256]{2,1,0:T(8,128)(2,1)S(1)} all-gather(bf16[3,64,256]{2,1,0:T(8,128)(2,1)S(1)} %copy-done.37), channel_id=1, replica_groups=mesh['shard'=8,'ctx'=2,'tensor'=2] {'shard'}, dimensions={1}, use_global_device_ids=true | all-gather | bytes 884736 | tf_op jit(solution)/shard_map/all_gather | solution.py:159
  306.6 47.9 %while.55 = (s32[]{:T(128)}, bf16[2,2,392,8,32]{2,4,3,1,0:T(8,128)(2,1)}, f32[2,2,8,392]{3,2,1,0:T(8,128)S(1)}, bf16[2,2,392,8,32]{2,4,3,1,0:T(8,128)(2,1)}, bf1...) while((s32[]{:T(128)}, ...), condition=%wide.region_10.11_spmd, body=%wide.region_7.10_spmd.sunk | while | flops 352392320 | bytes 97431456 | solution.py:197
  307.2 9.6 copy.205
  330.9 9.6 copy.205
  366.1 30.7 %all_gather.38 = bf16[256,512]{0,1:T(8,128)(2,1)S(1)} all-gather(bf16[256,64]{0,1:T(8,128)(2,1)S(1)} %copy-done.39), channel_id=1, replica_groups=mesh['shard'=8,'ctx'=2,'tensor'=2] {'shard'}, dimensions={1}, use_global_device_ids=true | all-gather | bytes 294912 | tf_op jit(solution)/shard_map/all_gather | solution.py:160
  405.5 8.6 reduce-scatter.8.cloned.1.call-done
  422.9 23.1 %all-gather.11.cloned.1.call-done = bf16[512,1024]{1,0:T(8,128)(2,1)} async-done(((bf16[64,1024]{1,0:T(8,128)(2,1)}), bf16[512,1024]{1,0:T(8,128)(2,1)}) %all-gather.11.cloned.1.call-update) | async-done | bytes 1048592 | tf_op jit(solution)/shard_map/all_gather | solution.py:161
  446.0 10.2 all-gather.9.cloned.1.call-done
  456.2 18.3 %multiply_convert_fusion.1 = (bf16[1568,1024]{1,0:T(8,128)(2,1)}, f32[1568,1024]{1,0:T(8,128)}, f32[1568,1024]{1,0:T(8,128)}) fusion(f32[1024]{0:T(1024)S(1)} %copy-done.53, bf16[1568,512]{1,0:T(8,128)(2,1)} %all-gather.9.cloned.1.call-done, bf16[512,1024]{1,0:T(8,128)(2,1)} %all-gather.11.cloned.1.call-done), kind=kOutput, calls=%fused_computation.105 | convolution fusion | flops 1750138880 | bytes 18714624 | tf_op jit(solution)/shard_map/dot_general | solution.py:206
  474.6 38.0 %all-gather.13.cloned.1.call-done = bf16[1024,512]{0,1:T(8,128)(2,1)} async-done(((bf16[1024,64]{0,1:T(8,128)(2,1)}), bf16[1024,512]{0,1:T(8,128)(2,1)}) %all-gather.13.cloned.1.call-update) | async-done | bytes 1048592 | tf_op jit(solution)/shard_map/all_gather | solution.py:162
  512.6 10.1 convert_reduce_fusion.1
  545.8 6.0 reduce-scatter.10.cloned.1.call-done
  571.9 5.8 fusion.128
  577.8 10.6 collective-permute-done.2
  602.3 99.1 %while.56 = (s32[]{:T(128)}, f32[8,392,392]{1,2,0:T(8,128)}, bf16[2,2,392,8,32]{2,4,3,1,0:T(8,128)(2,1)}, bf16[2,2,392,8,32]{2,1,0,4,3:T(2,128)(2,1)}, bf16[2,2,...) while((s32[]{:T(128)}, f32[8,392,392]{1,2,0:T(8,128)}, ...), condition=%wide.region_25.26_spmd.clone, body=%wide.region_22.25_spmd.clone.sunk | while | flops 819104384 | bytes 156768384 | solution.py:270
  602.9 9.6 copy.207
  612.5 6.6 subtract_exponential_fusion.3
  621.1 6.4 multiply_reduce_fusion.13
  627.5 11.0 convert_reduce_fusion.7
  638.5 7.2 select_add_fusion.2
  651.2 9.6 copy.207
  660.8 6.6 subtract_exponential_fusion.3
  669.4 6.4 multiply_reduce_fusion.13
  675.8 11.0 convert_reduce_fusion.7
  686.8 9.1 select_add_fusion.2
  721.4 6.0 all_gather.46
  743.4 8.3 copy.147
  751.7 8.0 reshape.562
  759.7 271.3 %while.57 = (s32[]{:T(128)}, f32[8,40,64]{2,1,0:T(8,128)S(1)}, s32[14,28,392]{2,1,0:T(8,128)}, f32[14,8,10976]{2,0,1:T(8,128)}, s32[]{:T(128)}, /*index=5*/s32[]{:T(128)}) while((s32[]{:T(128)}, f32[8,40,64]{2,1,0:T(8,128)S(1)}, s32[14,28,392]{2,1,0:T(8,128)}, f32[14,8,10976]{2,0,1:T(8,128)}, s32[]{:T(128)}, ...), condition=%wide.region_43.44_spmd.clone, body=%wide.region_42.43_spmd.clone.sunk | while | flops 2705175040 | bytes 7934943 | solution.py:109
  763.1 16.1 %fusion.195 = f32[8,40,64]{2,1,0:T(8,128)S(1)} fusion(f32[10976,64]{0,1:T(8,128)S(1)} %fusion.194, f32[8,10976]{1,0:T(8,128)S(1)} %bitcast.212, s32[10976]{0:T(1024)S(1)} %get-tuple-element.738, f32[8,40,64]{2,1,0:T(8,128)S(1)} %get-tuple-element.830, pred[]{:T(512)S(6)} %compare.36), kind=kOutput, calls=%fused_computation.88.clone.1 | convolution fusion | flops 2703561472 | bytes 3368833 | tf_op jit(solution)/shard_map/while/body/eval_jaxpr/hpb,pa->hab/dot_general | solution.py:106
  782.4 16.1 %fusion.195 = f32[8,40,64]{2,1,0:T(8,128)S(1)} fusion(f32[10976,64]{0,1:T(8,128)S(1)} %fusion.194, f32[8,10976]{1,0:T(8,128)S(1)} %bitcast.212, s32[10976]{0:T(1024)S(1)} %get-tuple-element.738, f32[8,40,64]{2,1,0:T(8,128)S(1)} %get-tuple-element.830, pred[]{:T(512)S(6)} %compare.36), kind=kOutput, calls=%fused_computation.88.clone.1 | convolution fusion | flops 2703561472 | bytes 3368833 | tf_op jit(solution)/shard_map/while/body/eval_jaxpr/hpb,pa->hab/dot_general | solution.py:106
  801.8 16.1 %fusion.195 = f32[8,40,64]{2,1,0:T(8,128)S(1)} fusion(f32[10976,64]{0,1:T(8,128)S(1)} %fusion.194, f32[8,10976]{1,0:T(8,128)S(1)} %bitcast.212, s32[10976]{0:T(1024)S(1)} %get-tuple-element.738, f32[8,40,64]{2,1,0:T(8,128)S(1)} %get-tuple-element.830, pred[]{:T(512)S(6)} %compare.36), kind=kOutput, calls=%fused_computation.88.clone.1 | convolution fusion | flops 2703561472 | bytes 3368833 | tf_op jit(solution)/shard_map/while/body/eval_jaxpr/hpb,pa->hab/dot_general | solution.py:106
  821.2 16.1 %fusion.195 = f32[8,40,64]{2,1,0:T(8,128)S(1)} fusion(f32[10976,64]{0,1:T(8,128)S(1)} %fusion.194, f32[8,10976]{1,0:T(8,128)S(1)} %bitcast.212, s32[10976]{0:T(1024)S(1)} %get-tuple-element.738, f32[8,40,64]{2,1,0:T(8,128)S(1)} %get-tuple-element.830, pred[]{:T(512)S(6)} %compare.36), kind=kOutput, calls=%fused_computation.88.clone.1 | convolution fusion | flops 2703561472 | bytes 3368833 | tf_op jit(solution)/shard_map/while/body/eval_jaxpr/hpb,pa->hab/dot_general | solution.py:106
  840.6 16.1 %fusion.195 = f32[8,40,64]{2,1,0:T(8,128)S(1)} fusion(f32[10976,64]{0,1:T(8,128)S(1)} %fusion.194, f32[8,10976]{1,0:T(8,128)S(1)} %bitcast.212, s32[10976]{0:T(1024)S(1)} %get-tuple-element.738, f32[8,40,64]{2,1,0:T(8,128)S(1)} %get-tuple-element.830, pred[]{:T(512)S(6)} %compare.36), kind=kOutput, calls=%fused_computation.88.clone.1 | convolution fusion | flops 2703561472 | bytes 3368833 | tf_op jit(solution)/shard_map/while/body/eval_jaxpr/hpb,pa->hab/dot_general | solution.py:106
  859.9 16.1 %fusion.195 = f32[8,40,64]{2,1,0:T(8,128)S(1)} fusion(f32[10976,64]{0,1:T(8,128)S(1)} %fusion.194, f32[8,10976]{1,0:T(8,128)S(1)} %bitcast.212, s32[10976]{0:T(1024)S(1)} %get-tuple-element.738, f32[8,40,64]{2,1,0:T(8,128)S(1)} %get-tuple-element.830, pred[]{:T(512)S(6)} %compare.36), kind=kOutput, calls=%fused_computation.88.clone.1 | convolution fusion | flops 2703561472 | bytes 3368833 | tf_op jit(solution)/shard_map/while/body/eval_jaxpr/hpb,pa->hab/dot_general | solution.py:106
  879.3 16.1 %fusion.195 = f32[8,40,64]{2,1,0:T(8,128)S(1)} fusion(f32[10976,64]{0,1:T(8,128)S(1)} %fusion.194, f32[8,10976]{1,0:T(8,128)S(1)} %bitcast.212, s32[10976]{0:T(1024)S(1)} %get-tuple-element.738, f32[8,40,64]{2,1,0:T(8,128)S(1)} %get-tuple-element.830, pred[]{:T(512)S(6)} %compare.36), kind=kOutput, calls=%fused_computation.88.clone.1 | convolution fusion | flops 2703561472 | bytes 3368833 | tf_op jit(solution)/shard_map/while/body/eval_jaxpr/hpb,pa->hab/dot_general | solution.py:106
  898.7 16.1 %fusion.195 = f32[8,40,64]{2,1,0:T(8,128)S(1)} fusion(f32[10976,64]{0,1:T(8,128)S(1)} %fusion.194, f32[8,10976]{1,0:T(8,128)S(1)} %bitcast.212, s32[10976]{0:T(1024)S(1)} %get-tuple-element.738, f32[8,40,64]{2,1,0:T(8,128)S(1)} %get-tuple-element.830, pred[]{:T(512)S(6)} %compare.36), kind=kOutput, calls=%fused_computation.88.clone.1 | convolution fusion | flops 2703561472 | bytes 3368833 | tf_op jit(solution)/shard_map/while/body/eval_jaxpr/hpb,pa->hab/dot_general | solution.py:106
  918.0 16.1 %fusion.195 = f32[8,40,64]{2,1,0:T(8,128)S(1)} fusion(f32[10976,64]{0,1:T(8,128)S(1)} %fusion.194, f32[8,10976]{1,0:T(8,128)S(1)} %bitcast.212, s32[10976]{0:T(1024)S(1)} %get-tuple-element.738, f32[8,40,64]{2,1,0:T(8,128)S(1)} %get-tuple-element.830, pred[]{:T(512)S(6)} %compare.36), kind=kOutput, calls=%fused_computation.88.clone.1 | convolution fusion | flops 2703561472 | bytes 3368833 | tf_op jit(solution)/shard_map/while/body/eval_jaxpr/hpb,pa->hab/dot_general | solution.py:106
  937.4 16.1 %fusion.195 = f32[8,40,64]{2,1,0:T(8,128)S(1)} fusion(f32[10976,64]{0,1:T(8,128)S(1)} %fusion.194, f32[8,10976]{1,0:T(8,128)S(1)} %bitcast.212, s32[10976]{0:T(1024)S(1)} %get-tuple-element.738, f32[8,40,64]{2,1,0:T(8,128)S(1)} %get-tuple-element.830, pred[]{:T(512)S(6)} %compare.36), kind=kOutput, calls=%fused_computation.88.clone.1 | convolution fusion | flops 2703561472 | bytes 3368833 | tf_op jit(solution)/shard_map/while/body/eval_jaxpr/hpb,pa->hab/dot_general | solution.py:106
  956.8 16.1 %fusion.195 = f32[8,40,64]{2,1,0:T(8,128)S(1)} fusion(f32[10976,64]{0,1:T(8,128)S(1)} %fusion.194, f32[8,10976]{1,0:T(8,128)S(1)} %bitcast.212, s32[10976]{0:T(1024)S(1)} %get-tuple-element.738, f32[8,40,64]{2,1,0:T(8,128)S(1)} %get-tuple-element.830, pred[]{:T(512)S(6)} %compare.36), kind=kOutput, calls=%fused_computation.88.clone.1 | convolution fusion | flops 2703561472 | bytes 3368833 | tf_op jit(solution)/shard_map/while/body/eval_jaxpr/hpb,pa->hab/dot_general | solution.py:106
  976.1 16.1 %fusion.195 = f32[8,40,64]{2,1,0:T(8,128)S(1)} fusion(f32[10976,64]{0,1:T(8,128)S(1)} %fusion.194, f32[8,10976]{1,0:T(8,128)S(1)} %bitcast.212, s32[10976]{0:T(1024)S(1)} %get-tuple-element.738, f32[8,40,64]{2,1,0:T(8,128)S(1)} %get-tuple-element.830, pred[]{:T(512)S(6)} %compare.36), kind=kOutput, calls=%fused_computation.88.clone.1 | convolution fusion | flops 2703561472 | bytes 3368833 | tf_op jit(solution)/shard_map/while/body/eval_jaxpr/hpb,pa->hab/dot_general | solution.py:106
  995.5 16.1 %fusion.195 = f32[8,40,64]{2,1,0:T(8,128)S(1)} fusion(f32[10976,64]{0,1:T(8,128)S(1)} %fusion.194, f32[8,10976]{1,0:T(8,128)S(1)} %bitcast.212, s32[10976]{0:T(1024)S(1)} %get-tuple-element.738, f32[8,40,64]{2,1,0:T(8,128)S(1)} %get-tuple-element.830, pred[]{:T(512)S(6)} %compare.36), kind=kOutput, calls=%fused_computation.88.clone.1 | convolution fusion | flops 2703561472 | bytes 3368833 | tf_op jit(solution)/shard_map/while/body/eval_jaxpr/hpb,pa->hab/dot_general | solution.py:106
  1014.9 16.1 %fusion.195 = f32[8,40,64]{2,1,0:T(8,128)S(1)} fusion(f32[10976,64]{0,1:T(8,128)S(1)} %fusion.194, f32[8,10976]{1,0:T(8,128)S(1)} %bitcast.212, s32[10976]{0:T(1024)S(1)} %get-tuple-element.738, f32[8,40,64]{2,1,0:T(8,128)S(1)} %get-tuple-element.830, pred[]{:T(512)S(6)} %compare.36), kind=kOutput, calls=%fused_computation.88.clone.1 | convolution fusion | flops 2703561472 | bytes 3368833 | tf_op jit(solution)/shard_map/while/body/eval_jaxpr/hpb,pa->hab/dot_general | solution.py:106
  1050.7 13.6 %fusion.112 = (f32[256]{0:T(256)S(1)}, f32[2,2,8,7,7]{4,3,2,1,0:T(8,128)S(1)}, f32[2,2,8,7,7,256]{5,4,3,2,1,0:T(8,128)S(1)}, f32[1,1,2,2,8,7,7,256]{7,0,6,5,4,3,2,1:T(1,128)}) fusion(f32[256]{0:T(256)S(1)} %copy-done.41, bf16[1,1,2,2,8,4,7,256]{7,0,6,5,4,3,2,1:T(2,128)(2,1)S(1)} %slice.211, ...), kind=kLoop, calls=%fused_computation.217 | loop fusion | flops 4815072 | bytes 4022400 | tf_op jit(solution)/shard_map/reduce_sum | solution.py:305
  1064.5 26.2 %multiply_reduce_fusion.3 = (f32[256]{0:T(256)S(1)}, f32[4,392]{1,0:T(4,128)S(1)}) fusion(f32[1,4,392,256]{3,0,2,1:T(1,128)} %bitcast.214, f32[4,392]{1,0:T(4,128)S(1)} %mul.288, f32[4,392]{1,0:T(4,128)S(1)} %sub.119, bf16[1,4,392,256]{3,2,1,0:T(8,128)(2,1)} %param.25, f32[256]{0:T(256)S(1)} %copy-done.41), kind=kLoop, calls=%fused_computation.155 | loop fusion | flops 3209440 | bytes 2429312 | tf_op jit(solution)/shard_map/reduce_sum | solution.py:304
  1099.0 102.5 %all-reduce.11 = (f32[256]{0:T(256)}, f32[256]{0:T(256)}, bf16[3,512,256]{2,0,1:T(4,128)(2,1)S(1)}, f32[2,256]{1,0:T(2,128)}, f32[256]{0:T(256)}, /*index=5*/f32...) all-reduce(f32[256]{0:T(256)S(1)} %get-tuple-element.421, ...), channel_id=1, replica_groups=mesh['shard'=8,'ctx'=2,'tensor'=2] {'shard','ctx'}, use_global_device_ids=true, to_apply=%region_32.33 | all-reduce | flops 396288 | bytes 2383872 | tf_op jit(solution)/shard_map/psum | solution.py:321
  (501 shorter events, 328.6 us)
Async XLA Ops:
  8.0 16.4 %copy-start.40 = (f32[256]{0:T(256)S(1)}, f32[256]{0:T(256)}, u32[]{:S(2)}) copy-start(f32[256]{0:T(256)} %param.27) | copy-start | bytes 3076
  8.0 16.4 %copy-start.49 = (f32[256]{0:T(256)S(1)}, f32[256]{0:T(256)}, u32[]{:S(2)}) copy-start(f32[256]{0:T(256)} %param.28) | copy-start | bytes 3076
  8.0 264.2 %all-gather.7.cloned.1.call-start = ((), (), s32[]{:S(2)}) async-start(), calls=%async_computation.7 | async-start | bytes 2408448 | tf_op jit(solution)/shard_map/all_gather | solution.py:48
  19.6 4.7 copy-start.4
  23.6 6.5 copy-start.35
  28.4 4.7 copy-start.38
  28.4 4.8 copy-start.32
  30.3 12.7 %collective-permute-start = (bf16[1,1,2,2,4,7,7,256]{7,4,6,5,3,2,1,0:T(4,128)(2,1)S(1)}, bf16[1,1,2,2,4,7,7,256]{7,4,6,5,3,2,1,0:T(4,128)(2,1)}, u32[]{:S(2)}, u32[]{:S(2)}) collective-permute-start(bf16[1,1,2,2,4,7,7,256]{7,4,6,5,3,2,1,0:T(4,128)(2,1)S(1)} %copy.120), channel_id=1, source_target_pairs={{0,2},{2,0},{1,3},{3,1},{4,6},{6,4},{5,7},{7,5},{8,10},{10,8},{9,1... | collective-permute-start | bytes 1204232 | tf_op jit(solution)/shard_map/ppermute | solution.py:22
  57.7 356.4 %reduce-scatter.8.cloned.1.call-start = ((), (), s32[]{:S(2)}) async-start(), calls=%async_computation.8 | async-start | bytes 4816896 | tf_op jit(solution)/shard_map/reduce_scatter | solution.py:52
  57.7 181.4 %copy-start.48 = (f32[2,256]{1,0:T(2,128)S(1)}, f32[2,256]{1,0:T(2,128)}, u32[]{:S(2)}) copy-start(f32[2,256]{1,0:T(2,128)} %param.30) | copy-start | bytes 6148
  57.7 181.5 %copy-start.43 = (s32[4,392]{1,0:T(4,128)S(1)}, s32[4,392]{1,0:T(4,128)}, u32[]{:S(2)}) copy-start(s32[4,392]{1,0:T(4,128)} %param.41) | copy-start | bytes 18820
  57.8 181.5 %copy-start.37 = (bf16[3,64,256]{2,1,0:T(8,128)(2,1)S(1)}, bf16[3,64,256]{2,1,0:T(8,128)(2,1)}, u32[]{:S(2)}) copy-start(bf16[3,64,256]{2,1,0:T(8,128)(2,1)} %param.29) | copy-start | bytes 294916
  239.1 36.3 %copy-start.22 = (s32[14,28,392]{2,1,0:T(8,128)}, s32[14,28,392]{2,1,0:T(8,128)S(1)}, u32[]{:S(2)}) copy-start(s32[14,28,392]{2,1,0:T(8,128)S(1)} %get-tuple-element.892) | copy-start | bytes 1843972
  272.2 3.2 copy-start.20
  316.8 5.5 copy-start
  322.3 3.5 copy-start.6
  322.3 3.5 copy-start.16
  340.5 5.5 copy-start
  346.0 3.5 copy-start.6
  346.0 3.5 copy-start.16
  359.1 7.0 copy-start.39
  364.5 32.3 %collective-permute-start.1 = (bf16[1,1,2,2,4,7,7,256]{7,3,6,5,4,2,1,0:T(2,128)(2,1)S(1)}, bf16[1,1,2,2,4,7,7,256]{7,3,6,5,4,2,1,0:T(2,128)(2,1)S(1)}, u32[]{:S(2)}, u32[]{:S(2)}) collective-permute-start(bf16[1,1,2,2,4,7,7,256]{7,3,6,5,4,2,1,0:T(2,128)(2,1)S(1)} %get-tuple-element.536), channel_id=1, source_target_pairs={{0,2},{2,0},{1,3},{3,1},{4,6},{6,4},{5,7},{7,5},{8,10},{10,8},{9,1... | collective-permute-start | bytes 1204232 | tf_op jit(solution)/shard_map/ppermute | solution.py:22
  396.8 3.7 copy-start.23
  400.5 2.3 copy-start.18
  402.8 11.3 copy-start.51
  402.9 43.2 %all-gather.11.cloned.1.call-start = ((), (), s32[]{:S(2)}) async-start(), calls=%async_computation.10 | async-start | bytes 1179648 | tf_op jit(solution)/shard_map/all_gather | solution.py:161
  403.4 52.8 %all-gather.9.cloned.1.call-start = ((), (), s32[]{:S(2)}) async-start(), calls=%async_computation.9 | async-start | bytes 2408448 | tf_op jit(solution)/shard_map/all_gather | solution.py:48
  405.5 14.6 %copy-start.42 = (f32[256]{0:T(256)S(1)}, f32[256]{0:T(256)}, u32[]{:S(2)}) copy-start(f32[256]{0:T(256)} %param.34) | copy-start | bytes 3076
  405.5 14.6 %copy-start.50 = (f32[256]{0:T(256)S(1)}, f32[256]{0:T(256)}, u32[]{:S(2)}) copy-start(f32[256]{0:T(256)} %param.35) | copy-start | bytes 3076
  416.8 39.5 %copy-start.53 = (f32[1024]{0:T(1024)S(1)}, f32[1024]{0:T(1024)}, u32[]{:S(2)}) copy-start(f32[1024]{0:T(1024)} %param.37) | copy-start | bytes 12292
  421.5 53.0 %all-gather.15.cloned.1.call-start = ((), (), s32[]{:S(2)}) async-start(), calls=%async_computation.13 | async-start | bytes 2408448 | tf_op jit(solution)/shard_map/all_gather | solution.py:48
  422.1 90.5 %all-gather.13.cloned.1.call-start = ((), (), s32[]{:S(2)}) async-start(), calls=%async_computation.11 | async-start | bytes 1179648 | tf_op jit(solution)/shard_map/all_gather | solution.py:162
  422.8 114.6 %reduce-scatter.12.cloned.1.call-start = ((), (), s32[]{:S(2)}) async-start(), calls=%async_computation.14 | async-start | bytes 4816896 | tf_op jit(solution)/shard_map/reduce_scatter | solution.py:52
  512.6 11.7 copy-start.52
  527.9 23.8 %reduce-scatter.10.cloned.1.call-start = ((), (), s32[]{:S(2)}) async-start(), calls=%async_computation.12 | async-start | bytes 4816896 | tf_op jit(solution)/shard_map/reduce_scatter | solution.py:52
  533.9 17.8 %copy-start.14 = (bf16[1,4,392,256]{3,2,1,0:T(8,128)(2,1)S(1)}, bf16[1,4,392,256]{3,2,1,0:T(8,128)(2,1)}, u32[]{:S(2)}) copy-start(bf16[1,4,392,256]{3,2,1,0:T(8,128)(2,1)} %param.26) | copy-start | bytes 2408452
  534.0 33.8 %all-gather.17.cloned.1.call-start = ((), (), s32[]{:S(2)}) async-start(), calls=%async_computation.15 | async-start | bytes 2408448 | tf_op jit(solution)/shard_map/all_gather | solution.py:48
  556.6 11.1 copy-start.24
  556.7 163.9 %reduce-scatter.18.cloned.1.call-start = ((), (), s32[]{:S(2)}) async-start(), calls=%async_computation.19 | async-start | bytes 2228224 | tf_op jit(solution)/shard_map/reduce_scatter | solution.py:339
  562.6 171.0 %reduce-scatter.20.cloned.1.call-start = ((), (), s32[]{:S(2)}) async-start(), calls=%async_computation.20 | async-start | bytes 2228224 | tf_op jit(solution)/shard_map/reduce_scatter | solution.py:340
  570.1 18.3 %collective-permute-start.2 = (bf16[1,1,2,2,4,7,7,256]{7,6,5,4,3,2,1,0:T(8,128)(2,1)S(1)}, bf16[1,1,2,2,4,7,7,256]{7,6,5,4,3,2,1,0:T(8,128)(2,1)S(1)}, u32[]{:S(2)}, u32[]{:S(2)}) collective-permute-start(bf16[1,1,2,2,4,7,7,256]{7,6,5,4,3,2,1,0:T(8,128)(2,1)S(1)} %get-tuple-element.532), channel_id=1, source_target_pairs={{0,2},{2,0},{1,3},{3,1},{4,6},{6,4},{5,7},{7,5},{8,10},{10,8},{9,1... | collective-permute-start | bytes 1204232 | tf_op jit(solution)/shard_map/ppermute | solution.py:22
  577.8 454.4 %reduce-scatter.14.cloned.1.call-start = ((), (), s32[]{:S(2)}) async-start(), calls=%async_computation.16 | async-start | bytes 4816896 | tf_op jit(solution)/shard_map/reduce_scatter | solution.py:52
  612.5 6.7 copy-start.2
  612.5 6.7 copy-start.8
  621.1 6.5 copy-start.9
  638.5 7.2 copy-start.1
  660.8 6.6 copy-start.2
  660.8 6.6 copy-start.8
  669.3 6.5 copy-start.9
  686.8 9.1 copy-start.1
  701.3 4.6 copy-start.10
  709.2 4.4 copy-start.21
  709.2 4.4 copy-start.28
  718.2 22.0 %copy-start.19 = (bf16[1568,256]{1,0:T(8,128)(2,1)S(1)}, bf16[1568,256]{1,0:T(8,128)(2,1)}, u32[]{:S(2)}) copy-start(bf16[1568,256]{1,0:T(8,128)(2,1)} %copy-done.18) | copy-start | bytes 2408452
  718.2 323.4 %reduce-scatter.16.cloned.1.call-start = ((), (), s32[]{:S(2)}) async-start(), calls=%async_computation.17 | async-start | bytes 557056 | tf_op jit(solution)/shard_map/reduce_scatter | solution.py:338
  743.3 463.6 %all-reduce.10.cloned.1.call-start = ((), (), s32[]{:S(2)}) async-start(), calls=%async_computation.18 | async-start | bytes 163840 | tf_op jit(solution)/shard_map/psum | solution.py:321
  759.7 272.0 %copy-start.13 = (bf16[2,2,392,8,32]{2,4,3,1,0:T(8,128)(2,1)S(1)}, bf16[2,2,392,8,32]{2,4,3,1,0:T(8,128)(2,1)}, u32[]{:S(2)}) copy-start(bf16[2,2,392,8,32]{2,4,3,1,0:T(8,128)(2,1)} %get-tuple-element.238) | copy-start | bytes 2408452
  1034.3 13.4 %collective-permute-start.3 = (bf16[1,1,2,2,4,7,7,256]{7,4,6,5,3,2,1,0:T(4,128)(2,1)S(1)}, bf16[1,1,2,2,4,7,7,256]{7,4,6,5,3,2,1,0:T(4,128)(2,1)S(1)}, u32[]{:S(2)}, u32[]{:S(2)}) collective-permute-start(bf16[1,1,2,2,4,7,7,256]{7,4,6,5,3,2,1,0:T(4,128)(2,1)S(1)} %copy.142), channel_id=1, source_target_pairs={{0,2},{2,0},{1,3},{3,1},{4,6},{6,4},{5,7},{7,5},{8,10},{10,8},{9,1... | collective-permute-start | bytes 1204232 | tf_op jit(solution)/shard_map/ppermute | solution.py:22
  1048.3 2.4 copy-start.41
  1064.5 31.0 %copy-start.3 = (f32[1,4,392,256]{3,2,0,1:T(8,128)S(1)}, f32[1,4,392,256]{3,2,0,1:T(8,128)}, u32[]{:S(2)}) copy-start(f32[1,4,392,256]{3,2,0,1:T(8,128)} %copy.160) | copy-start | bytes 4816900
  1095.4 3.5 copy-start.44
  1095.4 3.5 copy-start.45
  1095.4 3.5 copy-start.46
  1095.4 3.5 copy-start.47
  (23 other events, 30.7 us)
Sparse Core Ops, SparseCore 0:
  57.8 11.1 all-gather.6
  403.0 11.1 reduce-scatter.7
  556.8 10.9 all-gather.16
  570.0 83.0 reduce-scatter.17
  655.3 78.2 reduce-scatter.19
  735.8 7.6 reduce-scatter.13
  745.8 77.7 reduce-scatter.15
  1041.7 101.3 all-reduce.9
Sparse Core Ops, SparseCore 1:
  405.5 40.5 all-gather.10
  448.1 8.1 all-gather.8
  457.7 10.8 all-gather.14
  470.9 41.6 all-gather.12
  528.0 9.3 reduce-scatter.11
  539.7 12.0 reduce-scatter.9
where the time goes:
time: 1230 us; the launch traced here: 1220 us
  matrix products  502 us (41%)
  local copies, waits for them, and re-layouts  211 us (17%)
  blocking collectives  201 us (16%)
  other arithmetic  151 us (12%)
  waiting for transfers between devices  122 us (10%)
  between operations  17.6 us (1%)
    dot_general x14, matrix products, fold_block(): jnp.einsum('hpb,pa->hab', weighted, coarse_table, precision=HIGHEST)  225 us
    dot_general x14, matrix products, lookup_block(): picked = jnp.einsum('hab,pa->hpb', padded, coarse_table, precision=HIGHEST)  155 us
    psum x1, blocking collectives, on_device(): lax.psum((small_terms[0], small_terms[1], small_terms[2], small_terms[3],...  102 us
    add x4, local copies, waits for them, and re-layouts, scored(): return raw_scores * scale + bias_full[None] + mask_add[:, None]  38.4 us
    all_gather x1, waiting for transfers between devices, on_device(): lax.all_gather(w_fc2, 'shard', axis=1, tiled=True)  38 us
    all_gather x1, blocking collectives, on_device(): lax.all_gather(w_qkv, 'shard', axis=1, tiled=True)  32.9 us
    all_gather x1, blocking collectives, on_device(): lax.all_gather(w_proj, 'shard', axis=1, tiled=True)  30.7 us
    dynamic_slice x28, local copies, waits for them, and re-layouts, table_accumulate(): folded, _ = lax.scan(fold_block, start, (index_blocks, grad_blocks))  29 us
  transfers between devices with their start and end apart: 18, of which 10 were waited for; matrix products, arithmetic and copies ran while one was open for 58% of the time, Pallas kernels for 0%

commit v1 on v0

v1 whole, which is shorter than its diff:
```python
import functools

import jax
import jax.numpy as jnp
import numpy as np
from jax import lax
from jax.experimental import pallas as pl
from jax.experimental.pallas import tpu as pltpu
from jax.sharding import PartitionSpec as P

BF = jnp.bfloat16
F32 = jnp.float32
HD = 32
WT, WH, WW = 8, 7, 7
WTOK = WT * WH * WW
TOKS = 400
HALF_ROWS = 208
TABLE = 2535
COARSE = 10
FINE = 256
ROWS = 16
GROUP = 4
EPSILON = 1e-05
LOG2E = 1.4426950408889634
VMEM_LIMIT = 56 * 1024 * 1024


def dot(a, b, ca, cb):
    return lax.dot_general(a, b, (((ca,), (cb,)), ((), ())), preferred_element_type=F32)


def one_hot(fine_row, width):
    rows = lax.broadcasted_iota(jnp.int32, (FINE, width), 0)
    return jnp.where(rows == fine_row, 1.0, 0.0).astype(BF)


def lane_tiles(width):
    return [(t, t * 128, min(128, width - t * 128)) for t in range(-(-width // 128))]


def put_rows(scratch, start, rows):
    for t, begin, size in lane_tiles(rows.shape[1]):
        scratch[t, start : start + rows.shape[0], :size] = rows[:, begin : begin + size]


def strided_rows(scratch, start, count, step, width):
    parts = [scratch[t, pl.ds(start, count, stride=step), :][:, :size] for t, _, size in lane_tiles(width)]
    return jnp.concatenate(parts, 1)


def lookup_kernel(heads, coarse, idx_ref, table_ref, out_ref, scratch):
    width = idx_ref.shape[1]
    for r in range(ROWS):
        idx = idx_ref[r : r + 1, :]
        hot = one_hot(jnp.bitwise_and(idx, FINE - 1), width)
        level = lax.shift_right_logical(idx, 8)
        picked = dot(table_ref[...], hot, 1, 0)
        acc = jnp.zeros((heads, width), F32)
        for c in range(coarse):
            acc = acc + jnp.where(level == c, picked[c * heads : (c + 1) * heads], 0.0)
        put_rows(scratch, r * heads, acc)
    for h in range(heads):
        out_ref[h] = strided_rows(scratch, h, ROWS, heads, width).astype(BF)


def lookup(idx, table, heads):
    rows, width = idx.shape
    coarse = table.shape[0] // heads
    return pl.pallas_call(
        functools.partial(lookup_kernel, heads, coarse),
        grid=(rows // ROWS,),
        in_specs=[
            pl.BlockSpec((ROWS, width), lambda i: (i, 0)),
            pl.BlockSpec(table.shape, lambda i: (0, 0)),
        ],
        out_specs=pl.BlockSpec((heads, ROWS, width), lambda i: (0, i, 0)),
        out_shape=jax.ShapeDtypeStruct((heads, rows, width), BF),
        scratch_shapes=[pltpu.VMEM((-(-width // 128), ROWS * heads, 128), F32)],
        compiler_params=pltpu.CompilerParams(vmem_limit_bytes=VMEM_LIMIT),
        cost_estimate=pl.CostEstimate(flops=2 * rows * width * FINE * table.shape[0], bytes_accessed=rows * width * heads * 2, transcendentals=0),
        name="table_lookup",
    )(idx, table)


def fold_kernel(heads, coarse, core_ref, idx_ref, own_ref, got_ref, out_ref, scratch):
    width = idx_ref.shape[1]
    step = pl.program_id(0)

    @pl.when(step == 0)
    def _():
        out_ref[...] = jnp.zeros_like(out_ref)

    @pl.when(jnp.logical_or(step > 0, core_ref[0] == 0))
    def _():
        for h in range(heads):
            put_rows(scratch, h * ROWS, own_ref[h].astype(F32) + got_ref[h].astype(F32))
        total = jnp.zeros(out_ref.shape, F32)
        for r in range(ROWS):
            idx = idx_ref[r : r + 1, :]
            hot = one_hot(jnp.bitwise_and(idx, FINE - 1), width)
            level = lax.shift_right_logical(idx, 8)
            grads = strided_rows(scratch, r, heads, ROWS, width)
            parts = [jnp.where(level == c, grads, 0.0) for c in range(coarse)]
            total = total + dot(jnp.concatenate(parts, 0).astype(BF), hot, 1, 1)
        out_ref[...] += total


def fold(core, idx, pair, got, heads, coarse):
    rows, width = idx.shape
    shift = (pair.shape[1] - rows) // ROWS
    return pl.pallas_call(
        functools.partial(fold_kernel, heads, coarse),
        grid_spec=pltpu.PrefetchScalarGridSpec(
            num_scalar_prefetch=1,
            grid=(rows // ROWS,),
            in_specs=[
                pl.BlockSpec((ROWS, width), lambda i, core: (i, 0)),
                pl.BlockSpec((heads, ROWS, width), lambda i, core: (0, core[0] * shift + i, 0)),
                pl.BlockSpec((heads, ROWS, width), lambda i, core: (0, i, 0)),
            ],
            out_specs=pl.BlockSpec((coarse * heads, FINE), lambda i, core: (0, 0)),
            scratch_shapes=[pltpu.VMEM((-(-width // 128), ROWS * heads, 128), F32)],
        ),
        out_shape=jax.ShapeDtypeStruct((coarse * heads, FINE), F32),
        compiler_params=pltpu.CompilerParams(vmem_limit_bytes=VMEM_LIMIT),
        cost_estimate=pl.CostEstimate(flops=2 * rows * width * FINE * coarse * heads, bytes_accessed=rows * width * heads * 4, transcendentals=0),
        name="table_fold",
    )(core, idx, pair, got)


def pick_bias(first, own_ref, got_ref, j, half):
    low = lax.select_n(first, got_ref[j], own_ref[j])
    skip = 2 * half - 400
    high = lax.select_n(first, own_ref[j, skip:, :], got_ref[j, skip:, :])
    return jnp.concatenate([low, high], 0).astype(F32)


def attend_kernel(group, hd, core_ref, q_ref, k_ref, v_ref, rq_ref, rk_ref, own_ref, got_ref, att_ref, exact_ref, lse_ref):
    first = core_ref[0] == 0
    ones = jnp.ones((16, q_ref.shape[2]), BF)
    for j in range(group):
        part = pl.ds(j * hd, hd)
        qa = jnp.concatenate([q_ref[0, part, :], rq_ref[0]], 0)
        ka = jnp.concatenate([k_ref[0, part, :], rk_ref[0]], 0)
        va = jnp.concatenate([v_ref[0, part, :], ones], 0)
        scores = dot(ka, qa, 0, 0) + pick_bias(first, own_ref, got_ref, j, own_ref.shape[1])
        peak = jnp.max(scores, 0, keepdims=True)
        weights = jnp.exp2(scores - peak).astype(BF)
        mixed = dot(va, weights, 1, 0)
        total = mixed[hd : hd + 1]
        out = mixed[:hd] / total
        att_ref[0, part, :] = out.astype(BF)
        exact_ref[0, part, :] = out
        lse_ref[0, 0, j : j + 1, :] = peak + jnp.log2(total)


def attend(core, q, k, v, rq, rk, own, got, hd, group):
    wins, feats, toks = q.shape
    heads = feats // hd
    half = own.shape[1]
    feat_spec = pl.BlockSpec((1, group * hd, toks), lambda h, w, core: (w, h, 0))
    reg_spec = pl.BlockSpec((1, 16, toks), lambda h, w, core: (w, 0, 0))
    bias_spec = pl.BlockSpec((group, half, toks), lambda h, w, core: (h, 0, 0))
    return pl.pallas_call(
        functools.partial(attend_kernel, group, hd),
        grid_spec=pltpu.PrefetchScalarGridSpec(
            num_scalar_prefetch=1,
            grid=(heads // group, wins),
            in_specs=[feat_spec, feat_spec, feat_spec, reg_spec, reg_spec, bias_spec, bias_spec],
            out_specs=[feat_spec, feat_spec, pl.BlockSpec((1, 1, group, toks), lambda h, w, core: (w, h, 0, 0))],
        ),
        out_shape=[
            jax.ShapeDtypeStruct(q.shape, BF),
            jax.ShapeDtypeStruct(q.shape, F32),
            jax.ShapeDtypeStruct((wins, heads // group, group, toks), F32),
        ],
        compiler_params=pltpu.CompilerParams(vmem_limit_bytes=VMEM_LIMIT),
        cost_estimate=pl.CostEstimate(flops=4 * wins * feats * toks * toks, bytes_accessed=wins * feats * toks * 12, transcendentals=wins * heads * toks * toks),
        name="attend",
    )(core, q, k, v, rq, rk, own, got)


def split3(row):
    hi = row.astype(BF)
    rest = row - hi.astype(F32)
    mid = rest.astype(BF)
    return hi.astype(F32), mid.astype(F32), rest - mid.astype(F32)


def rows16(parts, width):
    rows = lax.broadcasted_iota(jnp.int32, (16, width), 0)
    out = jnp.zeros((16, width), F32)
    for i, part in enumerate(parts):
        out = jnp.where(rows == i, part, out)
    return out.astype(BF)


def attend_back_kernel(group, hd, scale, core_ref, q_ref, k_ref, v_ref, rq_ref, rk_ref, own_ref, got_ref, exact_ref, lse_ref, g_ref, dq_ref, dk_ref, dv_ref, pair_ref, sums):
    first = core_ref[0] == 0
    toks = q_ref.shape[2]
    win = pl.program_id(1)
    minus = rows16([-1.0, -1.0, -1.0], toks)
    for j in range(group):
        part = pl.ds(j * hd, hd)
        q = q_ref[0, part, :]
        k = k_ref[0, part, :]
        g = g_ref[0, part, :]
        qa = jnp.concatenate([q, rq_ref[0], rows16(split3(lse_ref[0, 0, j : j + 1, :]), toks)], 0)
        ka = jnp.concatenate([k, rk_ref[0], minus], 0)
        va = jnp.concatenate([v_ref[0, part, :], minus], 0)
        along = jnp.sum(g.astype(F32) * exact_ref[0, part, :], 0, keepdims=True)
        ga = jnp.concatenate([g, rows16(split3(along), toks)], 0)
        probs = jnp.exp2(dot(ka, qa, 0, 0) + pick_bias(first, own_ref, got_ref, j, own_ref.shape[1]))
        grads = (probs * dot(va, ga, 0, 0)).astype(BF)
        low = probs.astype(BF)
        dv_ref[0, part, :] = dot(g, low, 1, 1).astype(BF)
        dk_ref[0, part, :] = (dot(q, grads, 1, 1) * (1.0 / LOG2E)).astype(BF)
        dq_ref[0, part, :] = (dot(k, grads, 1, 0) * scale).astype(BF)
        wide = grads.astype(F32)

        @pl.when(win == 0)
        def _():
            sums[j] = wide

        @pl.when(win > 0)
        def _():
            sums[j] = sums[j] + wide

        @pl.when(win == pl.num_programs(1) - 1)
        def _():
            pair_ref[j] = sums[j].astype(BF)


def attend_back(core, q, k, v, rq, rk, own, got, exact, lse, g, hd, group, scale):
    wins, feats, toks = q.shape
    heads = feats // hd
    half = own.shape[1]
    feat_spec = pl.BlockSpec((1, group * hd, toks), lambda h, w, core: (w, h, 0))
    reg_spec = pl.BlockSpec((1, 16, toks), lambda h, w, core: (w, 0, 0))
    bias_spec = pl.BlockSpec((group, half, toks), lambda h, w, core: (h, 0, 0))
    return pl.pallas_call(
        functools.partial(attend_back_kernel, group, hd, scale),
        grid_spec=pltpu.PrefetchScalarGridSpec(
            num_scalar_prefetch=1,
            grid=(heads // group, wins),
            in_specs=[feat_spec, feat_spec, feat_spec, reg_spec, reg_spec, bias_spec, bias_spec, feat_spec, pl.BlockSpec((1, 1, group, toks), lambda h, w, core: (w, h, 0, 0)), feat_spec],
            out_specs=[feat_spec, feat_spec, feat_spec, pl.BlockSpec((group, toks, toks), lambda h, w, core: (h, 0, 0))],
            scratch_shapes=[pltpu.VMEM((group, toks, toks), F32)],
        ),
        out_shape=[jax.ShapeDtypeStruct(q.shape, BF)] * 3 + [jax.ShapeDtypeStruct((heads, toks, toks), BF)],
        compiler_params=pltpu.CompilerParams(vmem_limit_bytes=VMEM_LIMIT),
        cost_estimate=pl.CostEstimate(flops=10 * wins * feats * toks * toks, bytes_accessed=wins * feats * toks * 16, transcendentals=wins * heads * toks * toks),
        name="attend_back",
    )(core, q, k, v, rq, rk, own, got, exact, lse, g)


def cost(flops, moved, trans=0):
    return pl.CostEstimate(flops=int(flops), bytes_accessed=int(moved), transcendentals=int(trans))


def params():
    return pltpu.CompilerParams(vmem_limit_bytes=VMEM_LIMIT)


def whole_spec(array):
    rank = len(array.shape)
    return pl.BlockSpec(array.shape, lambda w: (0,) * rank)


def window_spec(array):
    rank = len(array.shape)
    return pl.BlockSpec((1,) + array.shape[1:], lambda w: (w,) + (0,) * (rank - 1))


def normed(values):
    width = values.shape[1]
    center = jnp.sum(values, 1, keepdims=True) / width
    spread = jnp.sum(values * values, 1, keepdims=True) / width - center * center
    inv = lax.rsqrt(spread + EPSILON)
    return (values - center) * inv, inv


def norm_back(upstream, xhat, inv, gain):
    width = xhat.shape[1]
    scaled = upstream * gain
    total = jnp.sum(scaled, 1, keepdims=True) / width
    along = jnp.sum(scaled * xhat, 1, keepdims=True) / width
    return inv * (scaled - total - xhat * along)


def front_kernel(scale, x_ref, gain_ref, shift_ref, w_ref, b_ref, q_ref, k_ref, v_ref):
    xhat, _ = normed(x_ref[0].astype(F32))
    first = (xhat * gain_ref[...] + shift_ref[...]).astype(BF)
    for t in range(2):
        cols = w_ref.shape[2] // 3
        rows = pl.ds(t * cols, cols)
        made = dot(first, w_ref[t], 1, 0)
        q = (made[:, :cols] + b_ref[0:1, t * cols : (t + 1) * cols]) * scale
        v = made[:, 2 * cols :] + b_ref[1:2, t * cols : (t + 1) * cols]
        q_ref[0, rows, :] = q.T.astype(BF)
        k_ref[0, rows, :] = made[:, cols : 2 * cols].T.astype(BF)
        v_ref[0, rows, :] = v.T.astype(BF)


def front(x, gain, shift, w, b, scale):
    wins, toks, width = x.shape
    feats = 2 * (w.shape[2] // 3)
    out = jax.ShapeDtypeStruct((wins, feats, toks), BF)
    return pl.pallas_call(
        functools.partial(front_kernel, scale),
        grid=(wins,),
        in_specs=[window_spec(x), whole_spec(gain), whole_spec(shift), whole_spec(w), whole_spec(b)],
        out_specs=[window_spec(out)] * 3,
        out_shape=[out] * 3,
        compiler_params=params(),
        cost_estimate=cost(6 * wins * toks * width * feats, 4 * wins * toks * width * 2 + w.size * 2),
        name="front",
    )(x, gain, shift, w, b)


def middle_kernel(x_ref, att_ref, proj_ref, bp_ref, gain_ref, shift_ref, fc1_ref, b1_ref, fc2_ref, b2_ref, out_ref, mid_ref, second_ref, act_ref, slope_ref):
    cols = proj_ref.shape[2]
    branch = sum(dot(att_ref[0, pl.ds(t * cols, cols), :], proj_ref[t], 0, 1) for t in range(2))
    middle = x_ref[0].astype(F32) + (branch + bp_ref[...])
    mid_ref[0] = middle
    xhat, _ = normed(middle)
    second = (xhat * gain_ref[...] + shift_ref[...]).astype(BF)
    second_ref[0] = second
    wide = fc1_ref.shape[2]
    step = wide // 2
    total = jnp.zeros(middle.shape, F32)
    for t in range(2):
        for s in range(0, wide, step):
            at = t * wide + s
            hidden = dot(second, fc1_ref[t, :, s : s + step], 1, 0) + b1_ref[:, at : at + step]
            phi = 0.5 + 0.5 * lax.erf(hidden * (0.5**0.5))
            active = (hidden * phi).astype(BF)
            bell = jnp.exp2(hidden * hidden * (-0.5 * LOG2E)) * (1.0 / (2.0 * np.pi) ** 0.5)
            act_ref[0, :, at : at + step] = active
            slope_ref[0, :, at : at + step] = (phi + hidden * bell).astype(BF)
            total = total + dot(active, fc2_ref[t, :, s : s + step], 1, 1)
    out_ref[0] = middle + (total + b2_ref[...])


def middle_forward(x, att, proj, bp, gain, shift, fc1, b1, fc2, b2):
    wins, toks, width = x.shape
    hidden = 2 * fc1.shape[2]
    wide = jax.ShapeDtypeStruct((wins, toks, hidden), BF)
    plain = jax.ShapeDtypeStruct(x.shape, F32)
    outs = [plain, plain, jax.ShapeDtypeStruct(x.shape, BF), wide, wide]
    fixed = (proj, bp, gain, shift, fc1, b1, fc2, b2)
    return pl.pallas_call(
        middle_kernel,
        grid=(wins,),
        in_specs=[window_spec(x), window_spec(att)] + [whole_spec(a) for a in fixed],
        out_specs=[window_spec(o) for o in outs],
        out_shape=outs,
        compiler_params=params(),
        cost_estimate=cost(2 * wins * toks * width * (width + 2 * hidden), wins * toks * (width * 14 + hidden * 4) + fc1.size * 4),
        name="middle_forward",
    )(x, att, *fixed)


def store_halves(ref, scratch):
    cols = ref.shape[2]
    for t in range(2):
        ref[t] = scratch[:, t * cols : (t + 1) * cols].astype(BF)


def middle_back_kernel(cot_ref, mid_ref, second_ref, act_ref, slope_ref, att_ref, gain_ref, fc1_ref, fc2_ref, proj_ref, gm_ref, gr_ref, d2_ref, d1_ref, dp_ref, small_ref, b1_ref, acc2, acc1, accp):
    win = pl.program_id(0)

    @pl.when(win == 0)
    def _():
        acc2[...] = jnp.zeros_like(acc2)
        acc1[...] = jnp.zeros_like(acc1)
        accp[...] = jnp.zeros_like(accp)
        small_ref[...] = jnp.zeros_like(small_ref)
        b1_ref[...] = jnp.zeros_like(b1_ref)

    cot = cot_ref[0]
    second = second_ref[0]
    wide = fc1_ref.shape[2]
    step = wide // 2
    grad_second = jnp.zeros(cot.shape, F32)
    for t in range(2):
        for s in range(0, wide, step):
            at = t * wide + s
            span = slice(at, at + step)
            acc2[:, span] += dot(cot, act_ref[0, :, span], 0, 0)
            grad = dot(cot, fc2_ref[t, :, s : s + step], 1, 0) * slope_ref[0, :, span].astype(F32)
            grad = grad.astype(BF)
            b1_ref[:, span] += jnp.sum(grad.astype(F32), 0, keepdims=True)
            acc1[:, span] += dot(second, grad, 0, 0)
            grad_second = grad_second + dot(grad, fc1_ref[t, :, s : s + step], 1, 1)
    upstream = cot.astype(F32)
    xhat, inv = normed(mid_ref[0])
    grad_mid = upstream + norm_back(grad_second, xhat, inv, gain_ref[...])
    gm_ref[0] = grad_mid
    branch = grad_mid.astype(BF)
    cols = proj_ref.shape[2]
    for t in range(2):
        gr_ref[0, pl.ds(t * cols, cols), :] = dot(proj_ref[t], branch, 0, 1).astype(BF)
    accp[...] += dot(branch, att_ref[0], 0, 1)
    small_ref[0:1, :] += jnp.sum(upstream, 0, keepdims=True)
    small_ref[1:2, :] += jnp.sum(grad_second * xhat, 0, keepdims=True)
    small_ref[2:3, :] += jnp.sum(grad_second, 0, keepdims=True)
    small_ref[3:4, :] += jnp.sum(branch.astype(F32), 0, keepdims=True)

    @pl.when(win == pl.num_programs(0) - 1)
    def _():
        store_halves(d2_ref, acc2)
        store_halves(d1_ref, acc1)
        store_halves(dp_ref, accp)


def middle_back(cot, mid, second, act, slope, att, gain, fc1, fc2, proj):
    wins, toks, width = cot.shape
    hidden = act.shape[2]
    windows = (cot, mid, second, act, slope, att)
    fixed = (gain, fc1, fc2, proj)
    outs = [jax.ShapeDtypeStruct(mid.shape, F32), jax.ShapeDtypeStruct(att.shape, BF)]
    sums = [jax.ShapeDtypeStruct(fc2.shape, BF), jax.ShapeDtypeStruct(fc1.shape, BF), jax.ShapeDtypeStruct(proj.shape, BF), jax.ShapeDtypeStruct((4, width), F32), jax.ShapeDtypeStruct((1, hidden), F32)]
    return pl.pallas_call(
        middle_back_kernel,
        grid=(wins,),
        in_specs=[window_spec(a) for a in windows] + [whole_spec(a) for a in fixed],
        out_specs=[window_spec(o) for o in outs] + [whole_spec(o) for o in sums],
        out_shape=outs + sums,
        scratch_shapes=[pltpu.VMEM((width, hidden), F32), pltpu.VMEM((width, hidden), F32), pltpu.VMEM((width, att.shape[1]), F32)],
        compiler_params=params(),
        cost_estimate=cost(4 * wins * toks * width * (width + 2 * hidden), wins * toks * (width * 16 + hidden * 4) + fc1.size * 8),
        name="middle_back",
    )(*windows, *fixed)


def back_kernel(x_ref, dq_ref, dk_ref, dv_ref, gm_ref, gain_ref, shift_ref, w_ref, gx_ref, dw_ref, small_ref, acc):
    win = pl.program_id(0)

    @pl.when(win == 0)
    def _():
        acc[...] = jnp.zeros_like(acc)
        small_ref[...] = jnp.zeros_like(small_ref)

    xhat, inv = normed(x_ref[0].astype(F32))
    first = (xhat * gain_ref[...] + shift_ref[...]).astype(BF)
    cols = w_ref.shape[2] // 3
    moved = jnp.zeros(xhat.shape, F32)
    for t in range(2):
        rows = pl.ds(t * cols, cols)
        grads = jnp.concatenate([dq_ref[0, rows, :], dk_ref[0, rows, :], dv_ref[0, rows, :]], 0)
        moved = moved + dot(grads, w_ref[t], 0, 1)
        acc[t] += dot(first, grads, 0, 1)
    grad_first = moved.astype(BF).astype(F32)
    gx_ref[0] = (gm_ref[0] + norm_back(grad_first, xhat, inv, gain_ref[...])).astype(gx_ref.dtype)
    ones = jnp.ones((8, dq_ref.shape[2]), BF)
    small_ref[0:1, :] += dot(ones, dq_ref[0], 1, 1)[0:1]
    small_ref[1:2, :] += dot(ones, dv_ref[0], 1, 1)[0:1]
    small_ref[2:3, :] += jnp.sum(grad_first * xhat, 0, keepdims=True)
    small_ref[3:4, :] += jnp.sum(grad_first, 0, keepdims=True)

    @pl.when(win == pl.num_programs(0) - 1)
    def _():
        dw_ref[...] = acc[...].astype(BF)


def back(x, dq, dk, dv, gm, gain, shift, w):
    wins, toks, width = x.shape
    windows = (x, dq, dk, dv, gm)
    fixed = (gain, shift, w)
    outs = [jax.ShapeDtypeStruct(x.shape, F32), jax.ShapeDtypeStruct(w.shape, BF), jax.ShapeDtypeStruct((4, width), F32)]
    return pl.pallas_call(
        back_kernel,
        grid=(wins,),
        in_specs=[window_spec(a) for a in windows] + [whole_spec(a) for a in fixed],
        out_specs=[window_spec(outs[0]), whole_spec(outs[1]), whole_spec(outs[2])],
        out_shape=outs,
        scratch_shapes=[pltpu.VMEM(w.shape, F32)],
        compiler_params=params(),
        cost_estimate=cost(12 * wins * toks * width * width, wins * toks * width * 16 + w.size * 4),
        name="back",
    )(*windows, *fixed)


def bits_of(axis):
    return lax.axis_size(axis).bit_length() - 1


def bit_on(axis, bit):
    return lax.shift_right_logical(lax.axis_index(axis), bit) % 2 == 1


def swap(value, axis, bit=0):
    pairs = [(source, source ^ (1 << bit)) for source in range(lax.axis_size(axis))]
    return lax.ppermute(value, axis, pairs)


def ordered(on, mine, other, axis):
    return jnp.concatenate((jnp.where(on, other, mine), jnp.where(on, mine, other)), axis)


def bit_order(axis):
    count = bits_of(axis)
    return [b for b in range(1, count)] + ([0] if count else [])


def gather_rows(part):
    count = bits_of("shard")
    rows, cols = part.shape
    held = part.reshape((1,) * count + (rows, cols))
    for bit in bit_order("shard"):
        held = ordered(bit_on("shard", bit), held, swap(held, "shard", bit), count - 1 - bit)
    return held.reshape(-1, cols)


def both_halves(mine):
    on = lax.axis_index("tensor") == 1
    return ordered(on, mine[None], swap(mine, "tensor")[None], 0)


def add_rounded(a, b):
    return (a.astype(F32) + b.astype(F32)).astype(BF)


def choose(array, index, axis):
    return lax.dynamic_slice_in_dim(array, index, 1, axis)


def scatter_halves(halves):
    core = lax.axis_index("tensor")
    got = swap(choose(halves, 1 - core, 0), "tensor")
    return add_rounded(choose(halves, core, 0), got)[0]


def scatter_rows(part):
    count = bits_of("shard")
    rows, cols = part.shape
    held = part.reshape((2,) * count + (rows >> count, cols))
    for bit in reversed(bit_order("shard")):
        axis = count - 1 - bit
        own = bit_on("shard", bit).astype(jnp.int32)
        got = swap(choose(held, 1 - own, axis), "shard", bit)
        held = add_rounded(choose(held, own, axis), got)
    held = held.reshape(rows >> count, cols)
    for bit in range(bits_of("ctx")):
        held = held.astype(F32) + swap(held.astype(BF), "ctx", bit).astype(F32)
        if bit + 1 < bits_of("ctx"):
            held = held.astype(BF)
    return held.astype(F32)


def sum_all(value):
    for axis in ("shard", "ctx"):
        for bit in range(bits_of(axis)):
            value = value + swap(value, axis, bit)
    return value


def roll_axis(shaped, axis_pos, levels, backward):
    token_axis = 4 + axis_pos
    length = shaped.shape[token_axis]
    border = length - length // 2 if backward else length // 2
    before = lax.slice_in_dim(shaped, 0, border, axis=token_axis)
    after = lax.slice_in_dim(shaped, border, length, axis=token_axis)
    moving = after if backward else before
    if axis_pos < levels:
        moving = swap(moving, "ctx", levels - 1 - axis_pos)
    else:
        moving = jnp.roll(moving, 1 if backward else -1, axis=1 + axis_pos)
    return jnp.concatenate((moving, before) if backward else (after, moving), axis=token_axis)


def window_roll(windows, clips, counts, backward):
    shaped = windows.reshape((clips,) + counts + (WT, WH, WW, windows.shape[-1]))
    for axis_pos in range(3):
        shaped = roll_axis(shaped, axis_pos, bits_of("ctx"), backward)
    return shaped.reshape(windows.shape)


HELD = WTOK // 2
SENT_IN = 200
SENT_OUT = 208


def frame_sources():
    source = np.zeros((4, HELD), np.int64)
    for h in range(2 * WH):
        for w in range(2 * WW):
            here = (h // WH) * 2 + w // WW
            there_h, there_w = (h + WH // 2) % (2 * WH), (w + WW // 2) % (2 * WW)
            there = (there_h // WH) * 2 + there_w // WW
            for a in range(WT // 2):
                row = (a * WH + h % WH) * WW + w % WW
                source[here, row] = there * HELD + (a * WH + there_h % WH) * WW + there_w % WW
    return source


def selector(picks, width):
    cells = lax.broadcasted_iota(jnp.int32, (picks.size, width), 1)
    return (jnp.asarray(picks.reshape(-1, 1), jnp.int32) == cells).astype(BF)


def shift_in(windows):
    source = frame_sources()
    there, row = source // HELD, source % HELD
    near = np.full((4, TOKS), -1)
    near[:, :HELD] = there * WTOK + HELD + row
    far = np.full((4, TOKS), -1)
    far[:, HELD:WTOK] = there * SENT_IN + row
    width = windows.shape[-1]
    got = swap(windows[:, :SENT_IN].reshape(-1, width), "ctx")
    kept = dot(selector(near, 4 * WTOK), windows.reshape(-1, width), 1, 0)
    return (kept + dot(selector(far, 4 * SENT_IN), got, 1, 0)).astype(BF).reshape(4, TOKS, width)


def shift_out(windows):
    source = frame_sources().reshape(-1)
    place = np.argsort(source).reshape(4, HELD)
    there, row = place // HELD, place % HELD
    near = np.full((4, WTOK), -1)
    near[:, HELD:] = there * TOKS + row
    far = np.full((4, WTOK), -1)
    far[:, :HELD] = there * SENT_OUT + row + HELD - (TOKS - SENT_OUT)
    width = windows.shape[-1]
    got = swap(windows[:, TOKS - SENT_OUT :].reshape(-1, width), "ctx")
    kept = dot(selector(near, 4 * TOKS), windows.reshape(-1, width), 1, 0)
    return (kept + dot(selector(far, 4 * SENT_OUT), got, 1, 0)).reshape(4, WTOK, width)


def to_shifted(windows, clips, counts):
    if bits_of("ctx") == 1 and clips == 1:
        moved = shift_in(windows)
    else:
        moved = jnp.pad(window_roll(windows, clips, counts, False), ((0, 0), (0, TOKS - WTOK), (0, 0)))
    half = moved.shape[0] // 2
    core = lax.axis_index("tensor")
    mine = lax.dynamic_slice_in_dim(moved, core * half, half, 0)
    other = swap(lax.dynamic_slice_in_dim(moved, (1 - core) * half, half, 0), "tensor")
    return ordered(core == 1, mine, other, 2)


def from_shifted(values, clips, counts):
    values = values.astype(BF)
    width = values.shape[2] // 2
    core = lax.axis_index("tensor")
    mine = lax.dynamic_slice_in_dim(values, core * width, width, 2)
    other = swap(lax.dynamic_slice_in_dim(values, (1 - core) * width, width, 2), "tensor")
    windows = ordered(core == 1, mine, other, 0)
    if bits_of("ctx") == 1 and clips == 1:
        return shift_out(windows)
    return window_roll(windows[:, :WTOK], clips, counts, True).astype(F32)


def region_rows(regions):
    padded = jnp.pad(regions, ((0, 0), (0, TOKS - WTOK)))
    query_rows, key_rows = [], []
    pieces = []
    rest = np.float32(-100.0 * LOG2E)
    for _ in range(3):
        piece = np.float32(rest.astype(jnp.bfloat16))
        pieces.append(float(piece))
        rest = np.float32(rest - piece)
    for region in range(4):
        same = padded == region
        for piece in pieces:
            query_rows.append(same.astype(F32))
            key_rows.append(jnp.where(same, 0.0, piece))
    blank = jnp.zeros(padded.shape, F32)
    past = jnp.broadcast_to(jnp.arange(TOKS) >= WTOK, padded.shape)
    query_rows += [blank] * 3 + [blank + 1.0]
    key_rows += [blank] * 3 + [jnp.where(past, -1e30, 0.0)]
    return jnp.stack(query_rows, 1).astype(BF), jnp.stack(key_rows, 1).astype(BF)


def on_device(
    clip_input,
    cotangent,
    gain_one,
    shift_one,
    w_qkv,
    b_qv,
    w_proj,
    b_proj,
    bias_table,
    gain_two,
    shift_two,
    w_fc1,
    b_fc1,
    w_fc2,
    b_fc2,
    rel_index,
    regions,
):
    clips, window_count, tokens, half_width = clip_input.shape
    width = 2 * half_width
    heads = 2 * bias_table.shape[0]
    levels = bits_of("ctx")
    counts = tuple(1 if axis_pos < levels else 2 for axis_pos in range(3))
    core = lax.axis_index("tensor")
    core_row = core.astype(jnp.int32).reshape(1)
    total_windows = clips * window_count
    held_windows = total_windows // 2
    scale = HD ** (-0.5)

    vectors = jnp.concatenate((gain_one, shift_one, b_qv.reshape(-1), b_proj, gain_two, shift_two, b_fc2, b_fc1, bias_table.reshape(-1)))
    pairs = both_halves(vectors)
    names = pairs[:, : 8 * half_width].reshape(2, 8, half_width).transpose(1, 0, 2).reshape(8, 1, width)
    gain1, shift1, bq, bv, bp, gain2, shift2, b2 = [names[i] for i in range(8)]
    start = 8 * half_width
    b1 = pairs[:, start : start + b_fc1.shape[0]].reshape(1, -1)
    table = pairs[:, start + b_fc1.shape[0] :].reshape(heads, TABLE)

    x = to_shifted(clip_input.reshape(total_windows, tokens, half_width), clips, counts)
    qkv_part = w_qkv.transpose(1, 0, 2).reshape(w_qkv.shape[1], -1)
    rest_part = jnp.concatenate((w_proj.T, w_fc1, w_fc2.T), 1)
    qkv_mine = gather_rows(qkv_part)
    rest_mine = gather_rows(rest_part)
    cot = to_shifted(cotangent.reshape(total_windows, tokens, half_width), clips, counts)

    table = jnp.pad(table * LOG2E, ((0, 0), (0, COARSE * FINE - TABLE)))
    table = table.reshape(heads, COARSE, FINE).transpose(1, 0, 2).reshape(COARSE * heads, FINE).astype(BF)
    index = jnp.pad(rel_index.T, ((0, TOKS - tokens), (0, TOKS - tokens)))
    index = lax.dynamic_slice_in_dim(index, core * (TOKS - HALF_ROWS), HALF_ROWS, 0)
    bias_own = lookup(index, table, heads)
    bias_got = swap(bias_own, "tensor")
    labels = jnp.tile(regions, (clips, 1))
    labels = lax.dynamic_slice_in_dim(labels, core * held_windows, held_windows, 0)
    query_rows, key_rows = region_rows(labels)

    qkv = both_halves(qkv_mine)
    queries, keys, values = front(x, gain1, shift1, qkv, jnp.concatenate((bq, bv), 0), scale * LOG2E)
    att, exact, lse = attend(core_row, queries, keys, values, query_rows, key_rows, bias_own, bias_got, HD, GROUP)
    edge = half_width
    proj = both_halves(rest_mine[:, :edge])
    fc1 = both_halves(rest_mine[:, edge : edge + w_fc1.shape[1]])
    fc2 = both_halves(rest_mine[:, edge + w_fc1.shape[1] :])
    out, mid, second, act, slope = middle_forward(x, att, proj, bp, gain2, shift2, fc1, b1, fc2, b2)
    block_out = from_shifted(out, clips, counts)
    grad_mid, grad_att, d_fc2, d_fc1, d_proj, small_mid, d_b1 = middle_back(cot, mid, second, act, slope, att, gain2, fc1, fc2, proj)
    dq, dk, dv, pair = attend_back(core_row, queries, keys, values, query_rows, key_rows, bias_own, bias_got, exact, lse, grad_att, HD, GROUP, scale)
    sent = lax.dynamic_slice_in_dim(pair, (1 - core) * (TOKS - HALF_ROWS), HALF_ROWS, 1)
    pair_got = swap(sent, "tensor")
    grad_x, d_qkv, small_end = back(x, dq, dk, dv, grad_mid, gain1, shift1, qkv)
    folded = fold(core_row, index, pair, pair_got, heads, COARSE)
    grad_input = from_shifted(grad_x, clips, counts)

    rest_grads = jnp.concatenate((scatter_halves(d_proj), scatter_halves(d_fc1), scatter_halves(d_fc2)), 1)
    rest_grads = scatter_rows(rest_grads)
    qkv_grads = scatter_rows(scatter_halves(d_qkv))

    small = jnp.concatenate((small_mid, small_end), 0).reshape(8, 2, half_width).transpose(1, 0, 2).reshape(2, -1)
    folded = folded.reshape(COARSE, heads, FINE).transpose(1, 0, 2).reshape(2, -1)
    small = jnp.concatenate((small, d_b1.reshape(2, -1), folded), 1).reshape(2, -1, 256)
    small = choose(small, core, 0) + swap(choose(small, 1 - core, 0), "tensor")
    small = sum_all(small[0]).reshape(-1)
    names = small[: 8 * half_width].reshape(8, half_width)
    d_b1 = small[start : start + b_fc1.shape[0]]
    grad_table = small[start + b_fc1.shape[0] :].reshape(heads // 2, COARSE * FINE)[:, :TABLE]

    rows = w_fc1.shape[0]
    return (
        block_out.reshape(clip_input.shape),
        grad_input.reshape(clip_input.shape),
        names[6],
        names[7],
        qkv_grads.reshape(rows, 3, half_width).transpose(1, 0, 2),
        jnp.stack((names[4], names[5])),
        rest_grads[:, :edge].T,
        names[3],
        grad_table,
        names[1],
        names[2],
        rest_grads[:, edge : edge + w_fc1.shape[1]],
        d_b1,
        rest_grads[:, edge + w_fc1.shape[1] :].T,
        names[0],
    )


def solution(mesh):
    in_specs = (
        P("shard", "ctx", None, "tensor"),
        P("shard", "ctx", None, "tensor"),
        P("tensor"),
        P("tensor"),
        P(None, "shard", "tensor"),
        P(None, "tensor"),
        P("tensor", "shard"),
        P("tensor"),
        P("tensor", None),
        P("tensor"),
        P("tensor"),
        P("shard", "tensor"),
        P("tensor"),
        P("tensor", "shard"),
        P("tensor"),
        P(),
        P("ctx", None),
    )
    out_specs = (
        P("shard", "ctx", None, "tensor"),
        P("shard", "ctx", None, "tensor"),
        P("tensor"),
        P("tensor"),
        P(None, "shard", "tensor"),
        P(None, "tensor"),
        P("tensor", "shard"),
        P("tensor"),
        P("tensor", None),
        P("tensor"),
        P("tensor"),
        P("shard", "tensor"),
        P("tensor"),
        P("tensor", "shard"),
        P("tensor"),
    )
    return jax.shard_map(
        on_device, mesh=mesh, in_specs=in_specs, out_specs=out_specs, check_vma=False
    )
```

time: 1230 us -> 375 us (0.30)
  matrix products: 502 us -> 22.5 us
  blocking collectives: 201 us -> 0 us
  local copies, waits for them, and re-layouts: 211 us -> 57.7 us
  Pallas kernels: 0 us -> 135 us
  other arithmetic: 151 us -> 27 us
  waiting for transfers between devices: 122 us -> 90.8 us
  starting transfers between devices: 7.48 us -> 32.7 us
  between operations: 17.6 us -> 1.99 us
    dot_general x54 -> x8, matrix products: 502 us -> 22.5 us  [dot(): lax.dot_general(a, b, (((ca,), (cb,)), ((), ())), preferred_element_type=...]
    pallas_call x0 -> x8, Pallas kernels: none -> 135 us  [the longest x1 27.5 us: attend_back(): pl.pallas_call(functools.partial(attend_back_kernel, group, hd, scale), g...]
    psum x5 -> x0, blocking collectives: 117 us -> none  [the longest x1 102 us: on_device(): lax.psum((small_terms[0], small_terms[1], small_terms[2], small_terms[3],...]
    reduce_sum x12 -> x0, other arithmetic: 86.9 us -> none  [the longest x1 26.2 us: on_device(): jnp.sum(grad_first * normed_one, 0)]
    all_gather x6 -> x0, blocking collectives: 84 us -> none  [the longest x1 32.9 us: on_device(): lax.all_gather(w_qkv, 'shard', axis=1, tiled=True)]
    all_gather x6 -> x0, waiting for transfers between devices: 76.4 us -> none  [the longest x1 38 us: on_device(): lax.all_gather(w_fc2, 'shard', axis=1, tiled=True)]
    ppermute x4 -> x38, waiting for transfers between devices: 20.3 us -> 90.8 us  [swap(): return lax.ppermute(value, axis, pairs)]
    add x6 -> x0, local copies, waits for them, and re-layouts: 38.5 us -> none  [the longest x4 38.4 us: scored(): return raw_scores * scale + bias_full[None] + mask_add[:, None]]
  transfers between devices with their start and end apart: 18 -> 38, of which waited for: 10 -> 12; matrix products, arithmetic and copies ran while one was open for 58% -> 25% of each run, Pallas kernels for 0% -> 34%
where the time goes in v1:
time: 375 us; the launch traced here: 368 us
  Pallas kernels  135 us (36%)
  waiting for transfers between devices  90.8 us (24%)
  local copies, waits for them, and re-layouts  57.7 us (15%)
  starting transfers between devices  32.7 us (9%)
  other arithmetic  27 us (7%)
  matrix products  22.5 us (6%)
    ppermute x38, waiting for transfers between devices, swap(): return lax.ppermute(value, axis, pairs)  90.8 us
    ppermute x38, starting transfers between devices, swap(): return lax.ppermute(value, axis, pairs)  32.7 us
    pallas_call x1, Pallas kernels, attend_back(): pl.pallas_call(functools.partial(attend_back_kernel, group, hd, scale), g...  27.5 us
    pallas_call x1, Pallas kernels, lookup(): pl.pallas_call(functools.partial(lookup_kernel, heads, coarse), grid=(row...  23.6 us
    pallas_call x1, Pallas kernels, fold(): pl.pallas_call(functools.partial(fold_kernel, heads, coarse), grid_spec=p...  23.3 us
    dot_general x8, matrix products, dot(): lax.dot_general(a, b, (((ca,), (cb,)), ((), ())), preferred_element_type=...  22.5 us
    pallas_call x1, Pallas kernels, middle_back(): pl.pallas_call(middle_back_kernel, grid=(wins,), in_specs=[window_spec(a)...  19.6 us
    pallas_call x1, Pallas kernels, attend(): pl.pallas_call(functools.partial(attend_kernel, group, hd), grid_spec=plt...  16.1 us
  transfers between devices with their start and end apart: 38, of which 12 were waited for; matrix products, arithmetic and copies ran while one was open for 25% of the time, Pallas kernels for 34%

profile of v1, /device:TPU:0, one launch (start us, length us, event | category | flops | bytes accessed | tf_op | source)
XLA Modules:
  0.0 368.0 jit_solution(534390604844496319)
XLA Ops:
  8.9 2.7 collective-permute-start.3
  12.6 1.0 slice.147
  13.6 2.0 collective-permute-start
  15.6 1.0 slice.163
  17.5 4.4 %fusion = f32[1600,256]{1,0:T(8,128)} fusion(bf16[1568,256]{1,0:T(8,128)(2,1)} %bitcast.182, s32[1600]{0:T(1024)S(1)} %copy-done.24), kind=kOutput, calls=%fused_computation.1 | convolution fusion | flops 1287014400 | bytes 2447616 | tf_op jit(solution)/shard_map/dot_general | solution.py:29
  21.9 3.2 fusion.1
  25.2 1.3 stack.106.rq_ref
  26.5 1.3 stack.120.rk_ref
  30.0 23.6 %table_lookup.1.own_ref = bf16[16,208,400]{2,1,0:T(8,128)(2,1)} custom-call(s32[208,400]{1,0:T(8,128)} %pad_dynamic-slice_fusion.idx_ref, bf16[160,256]{1,0:T(8,128)(2,1)} %bitcast.190), custom_call_target="tpu_custom_call" | custom-call | flops 6815744000 | bytes 2662400 | tf_op jit(solution)/shard_map/table_lookup/pallas_call | solution.py:69
  54.4 3.1 collective-permute-start.9
  61.0 5.9 %copy.532 = bf16[16,208,400]{1,2,0:T(8,128)(2,1)} copy(bf16[16,208,400]{2,1,0:T(8,128)(2,1)} %table_lookup.1.own_ref) | data formatting | bytes 5324800 | tf_op jit(solution)/shard_map/table_lookup/pallas_call | solution.py:69
  67.7 20.7 %collective-permute-done.9 = bf16[1,2,1,64,2304]{4,3,2,1,0:T(8,128)(2,1)S(1)} collective-permute-done((bf16[1,2,1,64,2304]{4,3,2,1,0:T(8,128)(2,1)S(1)}, bf16[1,2,1,64,2304]{4,3,2,1,0:T(8,128)(2,1)S(1)}, u32[]{:S(2)}, u32[]{:S(2)}) %collective-permute-start.9) | collective-permute-done | bytes 589856 | tf_op jit(solution)/shard_map/ppermute | solution.py:495
  88.6 1.6 collective-permute-start.10
  90.2 1.2 collective-permute-done.4
  91.5 1.6 collective-permute-start.5
  93.1 2.3 fusion.20
  95.6 2.3 fusion.21
  98.4 19.2 %collective-permute-done.10 = bf16[2,2,1,64,2304]{4,3,2,1,0:T(8,128)(2,1)S(1)} collective-permute-done((bf16[2,2,1,64,2304]{4,3,2,1,0:T(8,128)(2,1)S(1)}, bf16[2,2,1,64,2304]{4,3,2,1,0:T(8,128)(2,1)S(1)}, u32[]{:S(2)}, u32[]{:S(2)}) %collective-permute-start.10) | collective-permute-done | bytes 1179680 | tf_op jit(solution)/shard_map/ppermute | solution.py:495
  118.2 4.5 %collective-permute-done.5 = bf16[2,2,1,64,768]{4,3,2,1,0:T(8,128)(2,1)S(1)} collective-permute-done((bf16[2,2,1,64,768]{4,3,2,1,0:T(8,128)(2,1)S(1)}, bf16[2,2,1,64,768]{4,3,2,1,0:T(8,128)(2,1)S(1)}, u32[]{:S(2)}, u32[]{:S(2)}) %collective-permute-start.5) | collective-permute-done | bytes 393248 | tf_op jit(solution)/shard_map/ppermute | solution.py:495
  125.0 1.5 select_bitcast_fusion.1
  127.3 1.3 pad_maximum_fusion.4.w_ref
  128.6 4.7 %front.1 = (bf16[2,512,400]{2,1,0:T(8,128)(2,1)}, bf16[2,512,400]{2,1,0:T(8,128)(2,1)}, bf16[2,512,400]{2,1,0:T(8,128)(2,1)}) custom-call(bf16[2,400,512]{2,1,0:T(8,128)(2,1)} %pad_maximum_fusion.8.x_ref, f32[1,512]{1,0:T(1,128)} %bitcast.202, f32[1,512]{1,0:T(1,128)} %bitcast.200, bf16[2,512,768]{2,1,0:T(8,128)(2,1)} %pad_maximum_fusion.4.w_ref, ...), custom_call_target="tpu_custom_call" | custom-call | flops 1258291200 | bytes 4849664 | tf_op jit(solution)/shard_map/front/pallas_call | solution.py:309
  134.2 5.9 %copy.533.got_ref = bf16[16,208,400]{2,1,0:T(8,128)(2,1)} copy(bf16[16,208,400]{1,2,0:T(8,128)(2,1)} %collective-permute-done.7) | data formatting | bytes 5324800 | tf_op jit(solution)/shard_map/ppermute | solution.py:495
  140.2 16.1 %attend.1 = (bf16[2,512,400]{2,1,0:T(8,128)(2,1)}, f32[2,512,400]{2,1,0:T(8,128)}, f32[2,4,4,400]{3,2,1,0:T(4,128)}) custom-call(s32[1]{0:T(128)} %bitcast.4.core_ref, bf16[2,512,400]{2,1,0:T(8,128)(2,1)} %get-tuple-element.40.q_ref, bf16[2,512,400]{2,1,0:T(8,128)(2,1)} %get-tuple-element.41.k_ref, bf16[2,512,400]{2,1,0:T(8,128)(2,1)} %get-tuple-element.42.v_ref, ...), custom_call_target="tpu_custom_call" | custom-call | flops 655360000 | bytes 4915200 | tf_op jit(solution)/shard_map/attend/pallas_call | solution.py:164
  156.2 1.5 pad_maximum_fusion.3.fc2_ref
  157.8 1.4 select_bitcast_fusion.3
  159.2 1.5 pad_maximum_fusion.2.fc1_ref
  160.7 11.3 %middle_forward.1 = (f32[2,400,512]{2,1,0:T(8,128)}, f32[2,400,512]{2,1,0:T(8,128)}, bf16[2,400,512]{2,1,0:T(8,128)(2,1)}, bf16[2,400,2048]{2,1,0:T(8,128)(2,1)}, bf16[2,400,2048]{2,1,0:T(8,128)(2,1)}) custom-call(bf16[2,400,512]{2,1,0:T(8,128)(2,1)} %pad_maximum_fusion.8.x_ref, bf16[2,512,400]{2,1,0:T(8,128)(2,1)} %get-tuple-element.43.att_ref, ...), custom_call_target="tpu_custom_call" | custom-call | flops 3774873600 | bytes 16482304 | tf_op jit(solution)/shard_map/middle_forward/pallas_call | solution.py:352
  172.0 1.5 convert_element_type.161
  175.7 19.6 %middle_back.1 = (f32[2,400,512]{2,1,0:T(8,128)}, bf16[2,512,400]{2,1,0:T(8,128)(2,1)}, bf16[2,512,1024]{2,1,0:T(8,128)(2,1)}, bf16[2,512,1024]{2,1,0:T(8,128)(2...) custom-call(bf16[2,400,512]{2,1,0:T(8,128)(2,1)} %pad_maximum_fusion.9.cot_ref, ...), custom_call_target="tpu_custom_call" | custom-call | flops 7549747200 | bytes 21495808 | tf_op jit(solution)/shard_map/middle_back/pallas_call | solution.py:424
  195.3 27.5 %attend_back.1 = (bf16[2,512,400]{2,1,0:T(8,128)(2,1)}, bf16[2,512,400]{2,1,0:T(8,128)(2,1)}, bf16[2,512,400]{2,1,0:T(8,128)(2,1)}, bf16[16,400,400]{2,1,0:T(8,128)(2,1)}) custom-call(s32[1]{0:T(128)} %bitcast.4.core_ref, bf16[2,512,400]{2,1,0:T(8,128)(2,1)} %get-tuple-element.40.q_ref, bf16[2,512,400]{2,1,0:T(8,128)(2,1)} %get-tuple-element.41.k_ref, ...), custom_call_target="tpu_custom_call" | custom-call | flops 1638400000 | bytes 6553600 | tf_op jit(solution)/shard_map/attend_back/pallas_call | solution.py:241
  222.8 9.1 %back.1 = (f32[2,400,512]{2,1,0:T(8,128)}, bf16[2,512,768]{2,1,0:T(8,128)(2,1)}, f32[4,512]{1,0:T(4,128)}) custom-call(bf16[2,400,512]{2,1,0:T(8,128)(2,1)} %pad_maximum_fusion.8.x_ref, bf16[2,512,400]{2,1,0:T(8,128)(2,1)} %get-tuple-element.52.dq_ref, bf16[2,512,400]{2,1,0:T(8,128)(2,1)} %get-tuple-element.53.dk_ref, ...), custom_call_target="tpu_custom_call" | custom-call | flops 2516582400 | bytes 9699328 | tf_op jit(solution)/shard_map/back/pallas_call | solution.py:472
  232.0 1.6 convert_element_type.163
  234.1 1.1 reduce.3
  237.3 2.1 constant_dynamic-slice_fusion.8
  239.4 1.0 constant_dynamic-slice_fusion.2
  240.9 2.2 constant_dynamic-slice_fusion.10
  243.1 4.0 %copy.535 = bf16[16,208,400]{1,2,0:T(8,128)(2,1)} copy(bf16[16,208,400]{2,1,0:T(8,128)(2,1)S(1)} %constant_dynamic-slice_fusion.10) | data formatting | bytes 5324800 | tf_op jit(solution)/shard_map/dynamic_slice | solution.py:741
  247.1 1.4 constant_dynamic-slice_fusion.3
  248.6 1.1 add_convert_fusion.7
  250.3 1.5 broadcast_select_fusion.4
  251.8 1.7 collective-permute-start.19
  254.2 1.4 add_convert_fusion.3
  255.6 8.9 %collective-permute-done.19 = bf16[832,256]{1,0:T(8,128)(2,1)S(1)} collective-permute-done((bf16[832,256]{1,0:T(8,128)(2,1)S(1)}, bf16[832,256]{1,0:T(8,128)(2,1)S(1)}, u32[]{:S(2)}, u32[]{:S(2)}) %collective-permute-start.19) | collective-permute-done | bytes 426016 | tf_op jit(solution)/shard_map/ppermute | solution.py:495
  264.6 1.6 collective-permute-start.27
  266.2 1.5 fusion.6
  267.7 1.8 add_convert_fusion.1
  270.9 3.2 fusion.19
  274.1 2.5 collective-permute-done.27
  276.9 2.3 fusion.7
  279.2 6.3 %collective-permute-done.28 = bf16[1,2,1,64,768]{4,3,2,1,0:T(8,128)(2,1)S(1)} collective-permute-done((bf16[1,2,1,64,768]{4,3,2,1,0:T(8,128)(2,1)S(1)}, bf16[1,2,1,64,768]{4,3,2,1,0:T(8,128)(2,1)S(1)}, u32[]{:S(2)}, u32[]{:S(2)}) %collective-permute-start.28) | collective-permute-done | bytes 196640 | tf_op jit(solution)/shard_map/ppermute | solution.py:495
  286.0 13.1 %collective-permute-done.34 = bf16[2,2,1,64,2304]{4,3,2,1,0:T(8,128)(2,1)S(1)} collective-permute-done((bf16[2,2,1,64,2304]{4,3,2,1,0:T(8,128)(2,1)S(1)}, bf16[2,2,1,64,2304]{4,3,2,1,0:T(8,128)(2,1)S(1)}, u32[]{:S(2)}, u32[]{:S(2)}) %collective-permute-start.34) | collective-permute-done | bytes 1179680 | tf_op jit(solution)/shard_map/ppermute | solution.py:495
  299.5 5.9 %copy.536.got_ref = bf16[16,208,400]{2,1,0:T(8,128)(2,1)} copy(bf16[16,208,400]{1,2,0:T(8,128)(2,1)} %collective-permute-done.20) | data formatting | bytes 5324800 | tf_op jit(solution)/shard_map/ppermute | solution.py:495
  305.4 23.3 %table_fold.1 = f32[160,256]{1,0:T(8,128)} custom-call(s32[1]{0:T(128)} %bitcast.4.core_ref, s32[208,400]{1,0:T(8,128)} %pad_dynamic-slice_fusion.idx_ref, bf16[16,400,400]{2,1,0:T(8,128)(2,1)} %get-tuple-element.60.own_ref, bf16[16,208,400]{2,1,0:T(8,128)(2,1)} %copy.536.got_ref), custom_call_target="tpu_custom_call" | custom-call | flops 6815744000 | bytes 5324800 | tf_op jit(solution)/shard_map/table_fold/pallas_call | solution.py:111
  331.2 1.7 collective-permute-start.30
  333.0 1.6 collective-permute-start.22
  334.5 1.2 add_convert_fusion.4
  335.8 5.2 %collective-permute-start.36 = (bf16[1,1,1,64,2304]{4,3,2,1,0:T(8,128)(2,1)S(1)}, bf16[1,1,1,64,2304]{4,3,2,1,0:T(8,128)(2,1)S(1)}, u32[]{:S(2)}, u32[]{:S(2)}) collective-permute-start(bf16[1,1,1,64,2304]{4,3,2,1,0:T(8,128)(2,1)S(1)} %constant_dynamic-slice_fusion.14), channel_id=1, source_target_pairs={{0,8},{4,12},{8,0},{12,4},{16,24},{20,28},{24,16},{28,20},{1,9},{5... | collective-permute-start | bytes 884744 | tf_op jit(solution)/shard_map/ppermute | solution.py:495
  341.0 2.0 collective-permute-start.23
  343.0 3.2 fusion.18
  346.3 3.8 %collective-permute-done.23 = f32[92,256]{1,0:T(8,128)S(1)} collective-permute-done((f32[92,256]{1,0:T(8,128)S(1)}, f32[92,256]{1,0:T(8,128)S(1)}, u32[]{:S(2)}, u32[]{:S(2)}) %collective-permute-start.23) | collective-permute-done | bytes 94240 | tf_op jit(solution)/shard_map/ppermute | solution.py:495
  351.0 6.1 %collective-permute-done.24 = f32[92,256]{1,0:T(8,128)S(1)} collective-permute-done((f32[92,256]{1,0:T(8,128)S(1)}, f32[92,256]{1,0:T(8,128)S(1)}, u32[]{:S(2)}, u32[]{:S(2)}) %collective-permute-start.24) | collective-permute-done | bytes 94240 | tf_op jit(solution)/shard_map/ppermute | solution.py:495
  357.8 1.6 collective-permute-start.37
  359.3 3.6 collective-permute-done.25
  (247 shorter events, 40.6 us)
Async XLA Ops:
  0.6 16.2 %copy-start = (s32[4,392]{1,0:T(4,128)S(1)}, s32[4,392]{1,0:T(4,128)}, u32[]{:S(2)}) copy-start(s32[4,392]{1,0:T(4,128)} %param.41) | copy-start | bytes 18820
  0.7 16.5 %copy-start.11 = (s32[392,392]{1,0:T(8,128)S(1)}, s32[392,392]{1,0:T(8,128)}, u32[]{:S(2)}) copy-start(s32[392,392]{1,0:T(8,128)} %param.40) | copy-start | bytes 1843972
  7.2 21.4 %collective-permute-start.2 = (f32[23352]{0:T(1024)S(1)}, f32[23352]{0:T(1024)S(1)}, u32[]{:S(2)}, u32[]{:S(2)}) collective-permute-start(f32[23352]{0:T(1024)S(1)} %constant_dynamic-update-slice_fusion), channel_id=1, source_target_pairs={{0,1},{1,0},{2,3},{3,2},{4,5},{5,4},{6,7},{7,6},{8,9},{9,8},{10,11... | collective-permute-start | bytes 280232 | tf_op jit(solution)/shard_map/ppermute | solution.py:495
  8.9 58.7 %collective-permute-start.3 = (bf16[1,1,1,64,768]{4,3,2,1,0:T(8,128)(2,1)S(1)}, bf16[1,1,1,64,768]{4,3,2,1,0:T(8,128)(2,1)S(1)}, u32[]{:S(2)}, u32[]{:S(2)}) collective-permute-start(bf16[1,1,1,64,768]{4,3,2,1,0:T(8,128)(2,1)S(1)} %reshape_reshape.16), channel_id=1, source_target_pairs={{0,8},{4,12},{8,0},{12,4},{16,24},{20,28},{24,16},{28,20},{1,9},{5... | collective-permute-start | bytes 294920 | tf_op jit(solution)/shard_map/ppermute | solution.py:495
  11.5 6.0 %copy-start.24 = (s32[1600]{0:T(1024)S(1)}, s32[1600]{0:T(1024)}, u32[]{:S(2)}) copy-start(s32[1600]{0:T(1024)} %constant.113) | copy-start | bytes 19204
  12.5 41.7 %collective-permute-start.8 = (bf16[1,1,1,64,2304]{4,3,2,1,0:T(8,128)(2,1)S(1)}, bf16[1,1,1,64,2304]{4,3,2,1,0:T(8,128)(2,1)S(1)}, u32[]{:S(2)}, u32[]{:S(2)}) collective-permute-start(bf16[1,1,1,64,2304]{4,3,2,1,0:T(8,128)(2,1)S(1)} %maximum_bitcast_fusion), channel_id=1, source_target_pairs={{0,8},{4,12},{8,0},{12,4},{16,24},{20,28},{24,16},{28,20},{1,9},{5... | collective-permute-start | bytes 884744 | tf_op jit(solution)/shard_map/ppermute | solution.py:495
  13.6 81.9 %collective-permute-start = (bf16[800,256]{1,0:T(8,128)(2,1)S(1)}, bf16[800,256]{1,0:T(8,128)(2,1)}, u32[]{:S(2)}, u32[]{:S(2)}) collective-permute-start(bf16[800,256]{1,0:T(8,128)(2,1)S(1)} %bitcast.179), channel_id=1, source_target_pairs={{0,2},{2,0},{1,3},{3,1},{4,6},{6,4},{5,7},{7,5},{8,10},{10,8},{9,1... | collective-permute-start | bytes 1228808 | tf_op jit(solution)/shard_map/ppermute | solution.py:495
  16.7 76.4 %collective-permute-start.16 = (bf16[800,256]{1,0:T(8,128)(2,1)S(1)}, bf16[800,256]{1,0:T(8,128)(2,1)}, u32[]{:S(2)}, u32[]{:S(2)}) collective-permute-start(bf16[800,256]{1,0:T(8,128)(2,1)S(1)} %bitcast.180), channel_id=1, source_target_pairs={{0,2},{2,0},{1,3},{3,1},{4,6},{6,4},{5,7},{7,5},{8,10},{10,8},{9,1... | collective-permute-start | bytes 1228808 | tf_op jit(solution)/shard_map/ppermute | solution.py:495
  17.5 4.4 %copy-start.15 = (bf16[1,4,392,256]{3,2,1,0:T(8,128)(2,1)S(1)}, bf16[1,4,392,256]{3,2,1,0:T(8,128)(2,1)}, u32[]{:S(2)}) copy-start(bf16[1,4,392,256]{3,2,1,0:T(8,128)(2,1)} %param.25) | copy-start | bytes 2408452
  30.0 24.2 %copy-start.13 = (bf16[1024,64]{0,1:T(8,128)(2,1)S(1)}, bf16[1024,64]{0,1:T(8,128)(2,1)}, u32[]{:S(2)}) copy-start(bf16[1024,64]{0,1:T(8,128)(2,1)} %param.38) | copy-start | bytes 393220
  30.0 24.2 %copy-start.14 = (bf16[64,1024]{1,0:T(8,128)(2,1)S(1)}, bf16[64,1024]{1,0:T(8,128)(2,1)}, u32[]{:S(2)}) copy-start(bf16[64,1024]{1,0:T(8,128)(2,1)} %param.36) | copy-start | bytes 393220
  30.0 24.2 %copy-start.16 = (bf16[256,64]{0,1:T(8,128)(2,1)S(1)}, bf16[256,64]{0,1:T(8,128)(2,1)}, u32[]{:S(2)}) copy-start(bf16[256,64]{0,1:T(8,128)(2,1)} %param.31) | copy-start | bytes 98308
  54.4 34.0 %collective-permute-start.9 = (bf16[1,2,1,64,2304]{4,3,2,1,0:T(8,128)(2,1)S(1)}, bf16[1,2,1,64,2304]{4,3,2,1,0:T(8,128)(2,1)S(1)}, u32[]{:S(2)}, u32[]{:S(2)}) collective-permute-start(bf16[1,2,1,64,2304]{4,3,2,1,0:T(8,128)(2,1)S(1)} %pad_maximum_fusion.11), channel_id=1, source_target_pairs={{0,16},{4,20},{8,24},{12,28},{16,0},{20,4},{24,8},{28,12},{1,17},{... | collective-permute-start | bytes 1769480 | tf_op jit(solution)/shard_map/ppermute | solution.py:495
  66.9 67.3 %collective-permute-start.7 = (bf16[16,208,400]{1,2,0:T(8,128)(2,1)}, bf16[16,208,400]{1,2,0:T(8,128)(2,1)}, u32[]{:S(2)}, u32[]{:S(2)}) collective-permute-start(bf16[16,208,400]{1,2,0:T(8,128)(2,1)} %copy.532), channel_id=1, source_target_pairs={{0,1},{1,0},{2,3},{3,2},{4,5},{5,4},{6,7},{7,6},{8,9},{9,8},{10,11... | collective-permute-start | bytes 7987208 | tf_op jit(solution)/shard_map/ppermute | solution.py:495
  67.6 23.8 %collective-permute-start.4 = (bf16[1,2,1,64,768]{4,3,2,1,0:T(8,128)(2,1)S(1)}, bf16[1,2,1,64,768]{4,3,2,1,0:T(8,128)(2,1)S(1)}, u32[]{:S(2)}, u32[]{:S(2)}) collective-permute-start(bf16[1,2,1,64,768]{4,3,2,1,0:T(8,128)(2,1)S(1)} %pad_maximum_fusion.14), channel_id=1, source_target_pairs={{0,16},{4,20},{8,24},{12,28},{16,0},{20,4},{24,8},{28,12},{1,17},{... | collective-permute-start | bytes 589832 | tf_op jit(solution)/shard_map/ppermute | solution.py:495
  88.5 4.6 %copy-start.23 = (s32[1600]{0:T(1024)S(1)}, s32[1600]{0:T(1024)}, u32[]{:S(2)}) copy-start(s32[1600]{0:T(1024)} %constant.114) | copy-start | bytes 19204
  88.5 4.6 %copy-start.26 = (f32[1600,256]{1,0:T(8,128)S(1)}, f32[1600,256]{1,0:T(8,128)}, u32[]{:S(2)}) copy-start(f32[1600,256]{1,0:T(8,128)} %fusion) | copy-start | bytes 4915204
  88.6 29.0 %collective-permute-start.10 = (bf16[2,2,1,64,2304]{4,3,2,1,0:T(8,128)(2,1)S(1)}, bf16[2,2,1,64,2304]{4,3,2,1,0:T(8,128)(2,1)S(1)}, u32[]{:S(2)}, u32[]{:S(2)}) collective-permute-start(bf16[2,2,1,64,2304]{4,3,2,1,0:T(8,128)(2,1)S(1)} %pad_maximum_fusion.5), channel_id=1, source_target_pairs={{0,4},{4,0},{8,12},{12,8},{16,20},{20,16},{24,28},{28,24},{1,5},{5... | collective-permute-start | bytes 3538952 | tf_op jit(solution)/shard_map/ppermute | solution.py:495
  91.5 4.1 %copy-start.25 = (f32[1600,256]{1,0:T(8,128)S(1)}, f32[1600,256]{1,0:T(8,128)}, u32[]{:S(2)}) copy-start(f32[1600,256]{1,0:T(8,128)} %fusion.1) | copy-start | bytes 4915204
  91.5 31.2 %collective-permute-start.5 = (bf16[2,2,1,64,768]{4,3,2,1,0:T(8,128)(2,1)S(1)}, bf16[2,2,1,64,768]{4,3,2,1,0:T(8,128)(2,1)S(1)}, u32[]{:S(2)}, u32[]{:S(2)}) collective-permute-start(bf16[2,2,1,64,768]{4,3,2,1,0:T(8,128)(2,1)S(1)} %pad_maximum_fusion.13), channel_id=1, source_target_pairs={{0,4},{4,0},{8,12},{12,8},{16,20},{20,16},{24,28},{28,24},{1,5},{5... | collective-permute-start | bytes 1179656 | tf_op jit(solution)/shard_map/ppermute | solution.py:495
  95.5 27.5 %collective-permute-start.17 = (bf16[2,400,256]{2,1,0:T(8,128)(2,1)S(1)}, bf16[2,400,256]{2,1,0:T(8,128)(2,1)S(1)}, u32[]{:S(2)}, u32[]{:S(2)}) collective-permute-start(bf16[2,400,256]{2,1,0:T(8,128)(2,1)S(1)} %constant_dynamic-slice_fusion.12), channel_id=1, source_target_pairs={{0,1},{1,0},{2,3},{3,2},{4,5},{5,4},{6,7},{7,6},{8,9},{9,8},{10,11... | collective-permute-start | bytes 1228808 | tf_op jit(solution)/shard_map/ppermute | solution.py:495
  97.9 26.1 %collective-permute-start.1 = (bf16[2,400,256]{2,1,0:T(8,128)(2,1)S(1)}, bf16[2,400,256]{2,1,0:T(8,128)(2,1)S(1)}, u32[]{:S(2)}, u32[]{:S(2)}) collective-permute-start(bf16[2,400,256]{2,1,0:T(8,128)(2,1)S(1)} %constant_dynamic-slice_fusion.16), channel_id=1, source_target_pairs={{0,1},{1,0},{2,3},{3,2},{4,5},{5,4},{6,7},{7,6},{8,9},{9,8},{10,11... | collective-permute-start | bytes 1228808 | tf_op jit(solution)/shard_map/ppermute | solution.py:495
  118.1 6.9 %collective-permute-start.13 = (bf16[512,1024]{1,0:T(8,128)(2,1)S(1)}, bf16[512,1024]{1,0:T(8,128)(2,1)S(1)}, u32[]{:S(2)}, u32[]{:S(2)}) collective-permute-start(bf16[512,1024]{1,0:T(8,128)(2,1)S(1)} %slice.159), channel_id=1, source_target_pairs={{0,1},{1,0},{2,3},{3,2},{4,5},{5,4},{6,7},{7,6},{8,9},{9,8},{10,11... | collective-permute-start | bytes 3145736 | tf_op jit(solution)/shard_map/ppermute | solution.py:495
  122.8 4.2 %collective-permute-start.6 = (bf16[512,768]{1,0:T(8,128)(2,1)S(1)}, bf16[512,768]{1,0:T(8,128)(2,1)S(1)}, u32[]{:S(2)}, u32[]{:S(2)}) collective-permute-start(bf16[512,768]{1,0:T(8,128)(2,1)S(1)} %bitcast.164), channel_id=1, source_target_pairs={{0,1},{1,0},{2,3},{3,2},{4,5},{5,4},{6,7},{7,6},{8,9},{9,8},{10,11... | collective-permute-start | bytes 2359304 | tf_op jit(solution)/shard_map/ppermute | solution.py:495
  126.6 31.2 %collective-permute-start.12 = (bf16[512,1024]{1,0:T(8,128)(2,1)}, bf16[512,1024]{1,0:T(8,128)(2,1)}, u32[]{:S(2)}, u32[]{:S(2)}) collective-permute-start(bf16[512,1024]{1,0:T(8,128)(2,1)} %get-tuple-element.334), channel_id=1, source_target_pairs={{0,1},{1,0},{2,3},{3,2},{4,5},{5,4},{6,7},{7,6},{8,9},{9,8},{10,11... | collective-permute-start | bytes 3145736 | tf_op jit(solution)/shard_map/ppermute | solution.py:495
  127.2 6.1 %collective-permute-start.11 = (bf16[512,256]{1,0:T(8,128)(2,1)S(1)}, bf16[512,256]{1,0:T(8,128)(2,1)S(1)}, u32[]{:S(2)}, u32[]{:S(2)}) collective-permute-start(bf16[512,256]{1,0:T(8,128)(2,1)S(1)} %slice.154), channel_id=1, source_target_pairs={{0,1},{1,0},{2,3},{3,2},{4,5},{5,4},{6,7},{7,6},{8,9},{9,8},{10,11... | collective-permute-start | bytes 786440 | tf_op jit(solution)/shard_map/ppermute | solution.py:495
  140.2 16.1 %copy-start.2 = (bf16[1,512,1024]{2,1,0:T(8,128)(2,1)S(1)}, bf16[1,512,1024]{2,1,0:T(8,128)(2,1)}, u32[]{:S(2)}) copy-start(bf16[1,512,1024]{2,1,0:T(8,128)(2,1)} %get-tuple-element.329) | copy-start | bytes 3145732
  175.2 74.5 %collective-permute-start.14 = (bf16[2,400,256]{2,1,0:T(8,128)(2,1)}, bf16[2,400,256]{2,1,0:T(8,128)(2,1)}, u32[]{:S(2)}, u32[]{:S(2)}) collective-permute-start(bf16[2,400,256]{2,1,0:T(8,128)(2,1)} %constant_dynamic-slice_fusion.13), channel_id=1, source_target_pairs={{0,1},{1,0},{2,3},{3,2},{4,5},{5,4},{6,7},{7,6},{8,9},{9,8},{10,11... | collective-permute-start | bytes 1228808 | tf_op jit(solution)/shard_map/ppermute | solution.py:495
  232.0 2.2 copy-start.17
  232.0 3.3 copy-start.18
  232.0 3.3 copy-start.19
  232.0 3.3 copy-start.12
  233.6 6.8 %copy-start.5 = (bf16[2,400,512]{2,1,0:T(8,128)(2,1)}, bf16[2,400,512]{2,1,0:T(8,128)(2,1)S(1)}, u32[]{:S(2)}) copy-start(bf16[2,400,512]{2,1,0:T(8,128)(2,1)S(1)} %convert_element_type.163) | copy-start | bytes 2457604
  233.6 5.8 %copy-start.8 = (bf16[2,512,1024]{2,1,0:T(8,128)(2,1)S(1)}, bf16[2,512,1024]{2,1,0:T(8,128)(2,1)}, u32[]{:S(2)}) copy-start(bf16[2,512,1024]{2,1,0:T(8,128)(2,1)} %get-tuple-element.64) | copy-start | bytes 6291460
  236.0 12.5 %collective-permute-start.31 = (bf16[1,512,256]{2,1,0:T(8,128)(2,1)}, bf16[1,512,256]{2,1,0:T(8,128)(2,1)}, u32[]{:S(2)}, u32[]{:S(2)}) collective-permute-start(bf16[1,512,256]{2,1,0:T(8,128)(2,1)} %constant_dynamic-slice_fusion.4), channel_id=1, source_target_pairs={{0,1},{1,0},{2,3},{3,2},{4,5},{5,4},{6,7},{7,6},{8,9},{9,8},{10,11... | collective-permute-start | bytes 786440 | tf_op jit(solution)/shard_map/ppermute | solution.py:495
  236.8 13.5 %collective-permute-start.18 = (bf16[2,400,256]{2,1,0:T(8,128)(2,1)}, bf16[2,400,256]{2,1,0:T(8,128)(2,1)}, u32[]{:S(2)}, u32[]{:S(2)}) collective-permute-start(bf16[2,400,256]{2,1,0:T(8,128)(2,1)} %constant_dynamic-slice_fusion.11), channel_id=1, source_target_pairs={{0,1},{1,0},{2,3},{3,2},{4,5},{5,4},{6,7},{7,6},{8,9},{9,8},{10,11... | collective-permute-start | bytes 1228808 | tf_op jit(solution)/shard_map/ppermute | solution.py:495
  239.4 14.4 %collective-permute-start.26 = (bf16[1,512,768]{2,1,0:T(8,128)(2,1)}, bf16[1,512,768]{2,1,0:T(8,128)(2,1)}, u32[]{:S(2)}, u32[]{:S(2)}) collective-permute-start(bf16[1,512,768]{2,1,0:T(8,128)(2,1)} %constant_dynamic-slice_fusion.8), channel_id=1, source_target_pairs={{0,1},{1,0},{2,3},{3,2},{4,5},{5,4},{6,7},{7,6},{8,9},{9,8},{10,11... | collective-permute-start | bytes 2359304 | tf_op jit(solution)/shard_map/ppermute | solution.py:495
  240.4 27.3 %collective-permute-start.33 = (bf16[1,512,1024]{2,1,0:T(8,128)(2,1)}, bf16[1,512,1024]{2,1,0:T(8,128)(2,1)}, u32[]{:S(2)}, u32[]{:S(2)}) collective-permute-start(bf16[1,512,1024]{2,1,0:T(8,128)(2,1)} %constant_dynamic-slice_fusion.2), channel_id=1, source_target_pairs={{0,1},{1,0},{2,3},{3,2},{4,5},{5,4},{6,7},{7,6},{8,9},{9,8},{10,11... | collective-permute-start | bytes 3145736 | tf_op jit(solution)/shard_map/ppermute | solution.py:495
  247.1 3.2 copy-start.4
  247.1 3.2 copy-start.6
  248.6 20.9 %collective-permute-start.32 = (bf16[1,512,1024]{2,1,0:T(8,128)(2,1)S(1)}, bf16[1,512,1024]{2,1,0:T(8,128)(2,1)S(1)}, u32[]{:S(2)}, u32[]{:S(2)}) collective-permute-start(bf16[1,512,1024]{2,1,0:T(8,128)(2,1)S(1)} %constant_dynamic-slice_fusion.3), channel_id=1, source_target_pairs={{0,1},{1,0},{2,3},{3,2},{4,5},{5,4},{6,7},{7,6},{8,9},{9,8},{10,11... | collective-permute-start | bytes 3145736 | tf_op jit(solution)/shard_map/ppermute | solution.py:495
  249.7 49.7 %collective-permute-start.20 = (bf16[16,208,400]{1,2,0:T(8,128)(2,1)}, bf16[16,208,400]{1,2,0:T(8,128)(2,1)}, u32[]{:S(2)}, u32[]{:S(2)}) collective-permute-start(bf16[16,208,400]{1,2,0:T(8,128)(2,1)} %copy.535), channel_id=1, source_target_pairs={{0,1},{1,0},{2,3},{3,2},{4,5},{5,4},{6,7},{7,6},{8,9},{9,8},{10,11... | collective-permute-start | bytes 7987208 | tf_op jit(solution)/shard_map/ppermute | solution.py:495
  251.8 2.4 copy-start.10
  251.8 12.7 %collective-permute-start.19 = (bf16[832,256]{1,0:T(8,128)(2,1)S(1)}, bf16[832,256]{1,0:T(8,128)(2,1)S(1)}, u32[]{:S(2)}, u32[]{:S(2)}) collective-permute-start(bf16[832,256]{1,0:T(8,128)(2,1)S(1)} %bitcast.178), channel_id=1, source_target_pairs={{0,2},{2,0},{1,3},{3,1},{4,6},{6,4},{5,7},{7,5},{8,10},{10,8},{9,1... | collective-permute-start | bytes 1277960 | tf_op jit(solution)/shard_map/ppermute | solution.py:495
  253.7 12.5 %copy-start.22 = (s32[1568]{0:T(1024)S(1)}, s32[1568]{0:T(1024)}, u32[]{:S(2)}) copy-start(s32[1568]{0:T(1024)} %constant.115) | copy-start | bytes 18820
  253.7 23.1 %collective-permute-start.15 = (bf16[832,256]{1,0:T(8,128)(2,1)S(1)}, bf16[832,256]{1,0:T(8,128)(2,1)S(1)}, u32[]{:S(2)}, u32[]{:S(2)}) collective-permute-start(bf16[832,256]{1,0:T(8,128)(2,1)S(1)} %bitcast.177), channel_id=1, source_target_pairs={{0,2},{2,0},{1,3},{3,1},{4,6},{6,4},{5,7},{7,5},{8,10},{10,8},{9,1... | collective-permute-start | bytes 1277960 | tf_op jit(solution)/shard_map/ppermute | solution.py:495
  255.6 12.0 %copy-start.9 = (bf16[2,512,1024]{2,1,0:T(8,128)(2,1)S(1)}, bf16[2,512,1024]{2,1,0:T(8,128)(2,1)}, u32[]{:S(2)}) copy-start(bf16[2,512,1024]{2,1,0:T(8,128)(2,1)} %get-tuple-element.64) | copy-start | bytes 6291460
  264.6 12.1 %collective-permute-start.27 = (bf16[2,2,1,64,768]{4,3,2,1,0:T(8,128)(2,1)S(1)}, bf16[2,2,1,64,768]{4,3,2,1,0:T(8,128)(2,1)S(1)}, u32[]{:S(2)}, u32[]{:S(2)}) collective-permute-start(bf16[2,2,1,64,768]{4,3,2,1,0:T(8,128)(2,1)S(1)} %constant_dynamic-slice_fusion.7), channel_id=1, source_target_pairs={{0,4},{4,0},{8,12},{12,8},{16,20},{20,16},{24,28},{28,24},{1,5},{5... | collective-permute-start | bytes 1179656 | tf_op jit(solution)/shard_map/ppermute | solution.py:495
  267.7 1.9 copy-start.7
  270.3 28.8 %collective-permute-start.34 = (bf16[2,2,1,64,2304]{4,3,2,1,0:T(8,128)(2,1)S(1)}, bf16[2,2,1,64,2304]{4,3,2,1,0:T(8,128)(2,1)S(1)}, u32[]{:S(2)}, u32[]{:S(2)}) collective-permute-start(bf16[2,2,1,64,2304]{4,3,2,1,0:T(8,128)(2,1)S(1)} %constant_dynamic-slice_fusion.1), channel_id=1, source_target_pairs={{0,4},{4,0},{8,12},{12,8},{16,20},{20,16},{24,28},{28,24},{1,5},{5... | collective-permute-start | bytes 3538952 | tf_op jit(solution)/shard_map/ppermute | solution.py:495
  276.8 8.7 %collective-permute-start.28 = (bf16[1,2,1,64,768]{4,3,2,1,0:T(8,128)(2,1)S(1)}, bf16[1,2,1,64,768]{4,3,2,1,0:T(8,128)(2,1)S(1)}, u32[]{:S(2)}, u32[]{:S(2)}) collective-permute-start(bf16[1,2,1,64,768]{4,3,2,1,0:T(8,128)(2,1)S(1)} %constant_dynamic-slice_fusion.6), channel_id=1, source_target_pairs={{0,16},{4,20},{8,24},{12,28},{16,0},{20,4},{24,8},{28,12},{1,17},{... | collective-permute-start | bytes 589832 | tf_op jit(solution)/shard_map/ppermute | solution.py:495
  285.6 44.6 %collective-permute-start.29 = (bf16[1,1,1,64,768]{4,3,2,1,0:T(8,128)(2,1)S(1)}, bf16[1,1,1,64,768]{4,3,2,1,0:T(8,128)(2,1)}, u32[]{:S(2)}, u32[]{:S(2)}) collective-permute-start(bf16[1,1,1,64,768]{4,3,2,1,0:T(8,128)(2,1)S(1)} %constant_dynamic-slice_fusion.5), channel_id=1, source_target_pairs={{0,8},{4,12},{8,0},{12,4},{16,24},{20,28},{24,16},{28,20},{1,9},{5... | collective-permute-start | bytes 294920 | tf_op jit(solution)/shard_map/ppermute | solution.py:495
  299.4 35.1 %collective-permute-start.35 = (bf16[1,2,1,64,2304]{4,3,2,1,0:T(8,128)(2,1)S(1)}, bf16[1,2,1,64,2304]{4,3,2,1,0:T(8,128)(2,1)}, u32[]{:S(2)}, u32[]{:S(2)}) collective-permute-start(bf16[1,2,1,64,2304]{4,3,2,1,0:T(8,128)(2,1)S(1)} %constant_dynamic-slice_fusion), channel_id=1, source_target_pairs={{0,16},{4,20},{8,24},{12,28},{16,0},{20,4},{24,8},{28,12},{1,17},{... | collective-permute-start | bytes 1769480 | tf_op jit(solution)/shard_map/ppermute | solution.py:495
  329.9 13.1 %copy-start.21 = (s32[1568]{0:T(1024)S(1)}, s32[1568]{0:T(1024)}, u32[]{:S(2)}) copy-start(s32[1568]{0:T(1024)} %constant.112) | copy-start | bytes 18820
  330.1 12.9 %copy-start.27 = (f32[1568,256]{1,0:T(8,128)S(1)}, f32[1568,256]{1,0:T(8,128)}, u32[]{:S(2)}) copy-start(f32[1568,256]{1,0:T(8,128)} %fusion.7) | copy-start | bytes 4816900
  330.1 2.8 collective-permute-start.21
  331.2 18.9 %collective-permute-start.30 = (bf16[64,768]{1,0:T(8,128)(2,1)S(1)}, bf16[64,768]{1,0:T(8,128)(2,1)S(1)}, u32[]{:S(2)}, u32[]{:S(2)}) collective-permute-start(bf16[64,768]{1,0:T(8,128)(2,1)S(1)} %fusion.28), channel_id=1, source_target_pairs={{0,2},{2,0},{1,3},{3,1},{4,6},{6,4},{5,7},{7,5},{8,10},{10,8},{9,1... | collective-permute-start | bytes 294920 | tf_op jit(solution)/shard_map/ppermute | solution.py:495
  333.0 8.0 %collective-permute-start.22 = (f32[92,256]{1,0:T(8,128)S(1)}, f32[92,256]{1,0:T(8,128)S(1)}, u32[]{:S(2)}, u32[]{:S(2)}) collective-permute-start(f32[92,256]{1,0:T(8,128)S(1)} %add_bitcast_fusion), channel_id=1, source_target_pairs={{0,4},{4,0},{8,12},{12,8},{16,20},{20,16},{24,28},{28,24},{1,5},{5... | collective-permute-start | bytes 282632 | tf_op jit(solution)/shard_map/ppermute | solution.py:495
  335.8 21.9 %collective-permute-start.36 = (bf16[1,1,1,64,2304]{4,3,2,1,0:T(8,128)(2,1)S(1)}, bf16[1,1,1,64,2304]{4,3,2,1,0:T(8,128)(2,1)S(1)}, u32[]{:S(2)}, u32[]{:S(2)}) collective-permute-start(bf16[1,1,1,64,2304]{4,3,2,1,0:T(8,128)(2,1)S(1)} %constant_dynamic-slice_fusion.14), channel_id=1, source_target_pairs={{0,8},{4,12},{8,0},{12,4},{16,24},{20,28},{24,16},{28,20},{1,9},{5... | collective-permute-start | bytes 884744 | tf_op jit(solution)/shard_map/ppermute | solution.py:495
  341.0 9.1 %collective-permute-start.23 = (f32[92,256]{1,0:T(8,128)S(1)}, f32[92,256]{1,0:T(8,128)S(1)}, u32[]{:S(2)}, u32[]{:S(2)}) collective-permute-start(f32[92,256]{1,0:T(8,128)S(1)} %add.169), channel_id=1, source_target_pairs={{0,8},{4,12},{8,0},{12,4},{16,24},{20,28},{24,16},{28,20},{1,9},{5... | collective-permute-start | bytes 282632 | tf_op jit(solution)/shard_map/ppermute | solution.py:495
  350.1 7.0 %collective-permute-start.24 = (f32[92,256]{1,0:T(8,128)S(1)}, f32[92,256]{1,0:T(8,128)S(1)}, u32[]{:S(2)}, u32[]{:S(2)}) collective-permute-start(f32[92,256]{1,0:T(8,128)S(1)} %add.170), channel_id=1, source_target_pairs={{0,16},{4,20},{8,24},{12,28},{16,0},{20,4},{24,8},{28,12},{1,17},{... | collective-permute-start | bytes 282632 | tf_op jit(solution)/shard_map/ppermute | solution.py:495
  350.3 17.5 %copy-start.1 = (s32[4,392]{1,0:T(4,128)S(1)}, s32[4,392]{1,0:T(4,128)}, u32[]{:S(2)}) copy-start(s32[4,392]{1,0:T(4,128)} %param.41) | copy-start | bytes 18820
  357.1 5.8 %collective-permute-start.25 = (f32[92,256]{1,0:T(8,128)S(1)}, f32[92,256]{1,0:T(8,128)S(1)}, u32[]{:S(2)}, u32[]{:S(2)}) collective-permute-start(f32[92,256]{1,0:T(8,128)S(1)} %add.171), channel_id=1, source_target_pairs={{0,2},{2,0},{1,3},{3,1},{4,6},{6,4},{5,7},{7,5},{8,10},{10,8},{9,1... | collective-permute-start | bytes 282632 | tf_op jit(solution)/shard_map/ppermute | solution.py:495
  357.8 8.5 %collective-permute-start.37 = (bf16[64,2304]{1,0:T(8,128)(2,1)S(1)}, bf16[64,2304]{1,0:T(8,128)(2,1)S(1)}, u32[]{:S(2)}, u32[]{:S(2)}) collective-permute-start(bf16[64,2304]{1,0:T(8,128)(2,1)S(1)} %fusion.24), channel_id=1, source_target_pairs={{0,2},{2,0},{1,3},{3,1},{4,6},{6,4},{5,7},{7,5},{8,10},{10,8},{9,1... | collective-permute-start | bytes 884744 | tf_op jit(solution)/shard_map/ppermute | solution.py:495
  (2 other events, 1.6 us)

commit v2 on v0

v2 whole, which is shorter than its diff:
```python
import functools

import jax
import jax.numpy as jnp
import numpy as np
from jax import lax
from jax.experimental import pallas as pl
from jax.experimental.pallas import tpu as pltpu
from jax.sharding import PartitionSpec as P

BF = jnp.bfloat16
F32 = jnp.float32
HD = 32
WT, WH, WW = 8, 7, 7
WTOK = WT * WH * WW
TOKS = 400
LANES = 512
HALF_ROWS = 208
TABLE = 2535
COARSE = 10
FINE = 256
ROWS = 16
GROUP = 4
EPSILON = 1e-05
LOG2E = 1.4426950408889634
VMEM_LIMIT = 56 * 1024 * 1024
VECTOR_ROWS = 96
GAIN1, SHIFT1, BIAS_Q, BIAS_V, BIAS_P, GAIN2, SHIFT2, BIAS2, BIAS1 = range(80, 89)
ANY = pl.BlockSpec(memory_space=pl.ANY)


def dot(a, b, ca, cb):
    return lax.dot_general(a, b, (((ca,), (cb,)), ((), ())), preferred_element_type=F32)


def cost(flops, moved, trans=0):
    return pl.CostEstimate(flops=1, bytes_accessed=1, transcendentals=0)


def params():
    return pltpu.CompilerParams(vmem_limit_bytes=VMEM_LIMIT)


def whole_spec(array):
    rank = len(array.shape)
    return pl.BlockSpec(array.shape, lambda *_: (0,) * rank)


def window_spec(array):
    rank = len(array.shape)
    return pl.BlockSpec((1,) + array.shape[1:], lambda w, *_: (w,) + (0,) * (rank - 1))


def flip(values, axis=1):
    half = values.shape[axis] // 2
    low = lax.slice_in_dim(values, 0, half, axis=axis)
    high = lax.slice_in_dim(values, half, 2 * half, axis=axis)
    return jnp.concatenate([high, low], axis)


def row_pair(own_ref, got_ref, row, count=1):
    return jnp.concatenate([ref[r : r + 1, :] for ref in (own_ref, got_ref) for r in range(row, row + count)], 1)


def normed(values):
    width = values.shape[1]
    center = jnp.sum(values, 1, keepdims=True) / width
    spread = jnp.sum(values * values, 1, keepdims=True) / width - center * center
    inv = lax.rsqrt(spread + EPSILON)
    return (values - center) * inv, inv


def norm_back(upstream, xhat, inv, gain):
    width = xhat.shape[1]
    scaled = upstream * gain
    total = jnp.sum(scaled, 1, keepdims=True) / width
    along = jnp.sum(scaled * xhat, 1, keepdims=True) / width
    return inv * (scaled - total - xhat * along)


def pack_kernel(gain1, shift1, bqv, bp, gain2, shift2, b2, b1, table, out_ref):
    out_ref[...] = jnp.zeros_like(out_ref)
    heads = table.shape[0]
    for c in range(COARSE):
        size = min(FINE, TABLE - c * FINE)
        out_ref[c * heads : (c + 1) * heads, :size] = table[:, c * FINE : c * FINE + size]
    rows = ((GAIN1, gain1), (SHIFT1, shift1), (BIAS_P, bp), (GAIN2, gain2), (SHIFT2, shift2), (BIAS2, b2))
    for row, ref in rows:
        out_ref[row : row + 1, :] = ref[...].reshape(1, -1)
    out_ref[BIAS_Q : BIAS_Q + 2, :] = bqv[...]
    wide = b1[...].reshape(1, -1)
    for i in range(4):
        out_ref[BIAS1 + i : BIAS1 + i + 1, :] = wide[:, i * 256 : (i + 1) * 256]


def pack(*arrays):
    return pl.pallas_call(
        pack_kernel,
        out_shape=jax.ShapeDtypeStruct((VECTOR_ROWS, FINE), F32),
        cost_estimate=cost(1000, 200000),
        name="pack",
    )(*arrays)


def unpack_kernel(a_ref, b_ref, c_ref, d_ref, gain1, shift1, bqv, bp, table, gain2, shift2, b1, b2):
    total = (a_ref[...] + b_ref[...]) + (c_ref[...] + d_ref[...])
    heads = table.shape[0]
    for c in range(COARSE):
        size = min(FINE, TABLE - c * FINE)
        table[:, c * FINE : c * FINE + size] = total[c * heads : (c + 1) * heads, :size]
    rows = ((GAIN1, gain1), (SHIFT1, shift1), (BIAS_P, bp), (GAIN2, gain2), (SHIFT2, shift2), (BIAS2, b2))
    for row, ref in rows:
        ref[...] = total[row : row + 1].reshape(-1)
    bqv[...] = total[BIAS_Q : BIAS_Q + 2]
    b1[...] = jnp.concatenate([total[BIAS1 + i : BIAS1 + i + 1] for i in range(4)], 1).reshape(-1)


def unpack(parts, heads):
    vector = jax.ShapeDtypeStruct((FINE,), F32)
    return pl.pallas_call(
        unpack_kernel,
        out_shape=[vector, vector, jax.ShapeDtypeStruct((2, FINE), F32), vector, jax.ShapeDtypeStruct((heads, TABLE), F32), vector, vector, jax.ShapeDtypeStruct((4 * FINE,), F32), vector],
        cost_estimate=cost(1000, 200000),
        name="unpack",
    )(*parts)


def lane_tiles(width):
    return [(t, t * 128, min(128, width - t * 128)) for t in range(-(-width // 128))]


def put_rows(scratch, start, rows):
    for t, begin, size in lane_tiles(rows.shape[1]):
        scratch[t, start : start + rows.shape[0], :size] = rows[:, begin : begin + size]


def strided_rows(scratch, start, count, step, width):
    parts = [scratch[t, pl.ds(start, count, stride=step), :][:, :size] for t, _, size in lane_tiles(width)]
    return jnp.concatenate(parts, 1)


def one_hot(fine_row, width):
    rows = lax.broadcasted_iota(jnp.int32, (FINE, width), 0).astype(jnp.int16)
    return jnp.where(rows == fine_row.astype(jnp.int16), jnp.ones((), BF), jnp.zeros((), BF))


def lookup_kernel(heads, idx_ref, own_ref, got_ref, out_ref, scratch, table):
    width = idx_ref.shape[1]
    size = COARSE * heads

    @pl.when(pl.program_id(0) == 0)
    def _():
        table[:size, :] = (own_ref[:size, :] * LOG2E).astype(BF)
        table[size:, :] = (got_ref[:size, :] * LOG2E).astype(BF)

    for r in range(ROWS):
        idx = idx_ref[r : r + 1, :]
        hot = one_hot(jnp.bitwise_and(idx, FINE - 1), width)
        level = lax.shift_right_logical(idx, 8)
        picked = dot(table[...], hot, 1, 0)
        for half in range(2):
            acc = jnp.zeros((heads, width), F32)
            for c in range(COARSE):
                at = half * size + c * heads
                acc = jnp.where(level == c, picked[at : at + heads], acc)
            put_rows(scratch, (2 * r + half) * heads, acc)
    for h in range(2 * heads):
        out_ref[h, :, :width] = strided_rows(scratch, h, ROWS, 2 * heads, width).astype(BF)


def lookup(idx, own, got, heads, start, count):
    width = idx.shape[1]
    rows = count * ROWS
    return pl.pallas_call(
        functools.partial(lookup_kernel, heads),
        grid=(rows // ROWS,),
        in_specs=[pl.BlockSpec((ROWS, width), lambda i: (start + i, 0)), whole_spec(own), whole_spec(got)],
        out_specs=pl.BlockSpec((2 * heads, ROWS, LANES), lambda i: (0, i, 0)),
        out_shape=jax.ShapeDtypeStruct((2 * heads, rows, LANES), BF),
        scratch_shapes=[pltpu.VMEM((-(-width // 128), 2 * ROWS * heads, 128), F32), pltpu.VMEM((2 * COARSE * heads, FINE), BF)],
        compiler_params=params(),
        cost_estimate=cost(4 * rows * LANES * FINE * COARSE * heads, rows * width * heads * 4),
        name="table_lookup",
    )(idx, own, got)


def fold_rows(heads, idx_ref, pair_m, pair_o, sent_m, sent_o, scratch, total):
    width = idx_ref.shape[1]
    for h in range(heads):
        put_rows(scratch, h * ROWS, pair_m[h, :, :width].astype(F32) + sent_o[h, :, :width].astype(F32))
        put_rows(scratch, (heads + h) * ROWS, pair_o[h, :, :width].astype(F32) + sent_m[h, :, :width].astype(F32))
    part = jnp.zeros(total.shape, F32)
    for r in range(ROWS):
        idx = idx_ref[r : r + 1, :]
        hot = one_hot(jnp.bitwise_and(idx, FINE - 1), width)
        level = lax.shift_right_logical(idx, 8)
        grads = strided_rows(scratch, r, 2 * heads, ROWS, width)
        parts = [jnp.where(level == c, grads[half * heads : (half + 1) * heads], 0.0) for half in range(2) for c in range(COARSE)]
        part = part + dot(hot, jnp.concatenate(parts, 0).astype(BF), 1, 1)
    total[...] += part


def fold_start_kernel(heads, core_ref, idx_ref, pair_m, pair_o, sent_m, sent_o, total, scratch):
    step = pl.program_id(0)

    @pl.when(step == 0)
    def _():
        total[...] = jnp.zeros_like(total)

    @pl.when(jnp.logical_or(step > 0, core_ref[0] == 0))
    def _():
        fold_rows(heads, idx_ref, pair_m, pair_o, sent_m, sent_o, scratch, total)


def fold_end_kernel(heads, core_ref, idx_ref, pair_m, pair_o, sent_m, sent_o, init_ref, mid_ref, wide_ref, end_ref, mine_ref, other_ref, scratch, total):
    step = pl.program_id(0)
    size = COARSE * heads

    @pl.when(step == 0)
    def _():
        total[...] = init_ref[...]

    fold_rows(heads, idx_ref, pair_m, pair_o, sent_m, sent_o, scratch, total)

    @pl.when(step == pl.num_programs(0) - 1)
    def _():
        binned = total[...].T
        for half, ref in enumerate((mine_ref, other_ref)):
            ref[:size, :] = binned[half * size : (half + 1) * size]
            span = slice(half * 256, (half + 1) * 256)
            rows = ((GAIN1, end_ref, 2), (SHIFT1, end_ref, 3), (BIAS_Q, end_ref, 0), (BIAS_V, end_ref, 1), (BIAS_P, mid_ref, 3), (GAIN2, mid_ref, 1), (SHIFT2, mid_ref, 2), (BIAS2, mid_ref, 0))
            for row, source, at in rows:
                ref[row : row + 1, :] = source[at : at + 1, span]
            for i in range(4):
                at = half * 1024 + i * 256
                ref[BIAS1 + i : BIAS1 + i + 1, :] = wide_ref[:, at : at + 256]
            ref[BIAS1 + 4 :, :] = jnp.zeros((VECTOR_ROWS - BIAS1 - 4, 256), F32)


def fold(core, idx, pairs, heads, start, count, extra=()):
    width = idx.shape[1]
    scratch = [pltpu.VMEM((-(-width // 128), 2 * ROWS * heads, 128), F32)]
    total = jax.ShapeDtypeStruct((FINE, 2 * COARSE * heads), F32)
    ends = jax.ShapeDtypeStruct((VECTOR_ROWS, FINE), F32)
    outs = [ends, ends] if extra else [total]
    pair = pl.BlockSpec((heads, ROWS, LANES), lambda i, core: (0, start + i, 0))
    return pl.pallas_call(
        functools.partial(fold_end_kernel if extra else fold_start_kernel, heads),
        grid_spec=pltpu.PrefetchScalarGridSpec(
            num_scalar_prefetch=1,
            grid=(count,),
            in_specs=[pl.BlockSpec((ROWS, width), lambda i, core: (start + i, 0))] + [pair] * 4 + [whole_spec(e) for e in extra],
            out_specs=[whole_spec(o) for o in outs],
            scratch_shapes=scratch + ([pltpu.VMEM(total.shape, F32)] if extra else []),
        ),
        out_shape=outs,
        compiler_params=params(),
        cost_estimate=cost(0, 0),
        name="table_fold",
    )(core, idx, *pairs, *extra)


def mask_pieces():
    pieces = []
    rest = np.float32(-100.0 * LOG2E)
    for _ in range(3):
        piece = np.float32(rest.astype(jnp.bfloat16))
        pieces.append(float(piece))
        rest = np.float32(rest - piece)
    return pieces


def region_rows(label):
    width = label.shape[1]
    rows = lax.broadcasted_iota(jnp.int32, (16, width), 0)
    lanes = lax.broadcasted_iota(jnp.int32, (16, width), 1)
    same = jnp.bitwise_and(rows, 3) == label
    level = lax.shift_right_logical(rows, 2)
    high, mid, low = mask_pieces()
    piece = jnp.where(level == 0, high, jnp.where(level == 1, mid, low))
    queries = jnp.where(rows < 12, jnp.where(same, 1.0, 0.0), jnp.where(rows == 15, 1.0, 0.0))
    past = jnp.where(jnp.logical_and(rows == 15, lanes >= WTOK), -1e30, 0.0)
    keys = jnp.where(rows < 12, jnp.where(same, 0.0, piece), past)
    return queries.astype(BF), keys.astype(BF)


def pick_bias(first, own_ref, got_ref, j):
    heads = own_ref.shape[0]
    del heads
    skip = 2 * HALF_ROWS - TOKS
    low = lax.select_n(first, got_ref[j, :, :TOKS], own_ref[j, :, :TOKS])
    high = lax.select_n(first, own_ref[j, skip:, :TOKS], got_ref[j, skip:, :TOKS])
    return jnp.concatenate([low, high], 0).astype(F32)


def attend_kernel(core_ref, q_ref, k_ref, v_ref, label_ref, own_ref, got_ref, *rest):
    att_ref, exact_ref, lse_ref = rest[-3:]
    first = core_ref[0] == 0
    ones = jnp.ones((16, TOKS), BF)
    query_rows, key_rows = region_rows(label_ref[0])
    for j in range(GROUP):
        part = pl.ds(j * HD, HD)
        qa = jnp.concatenate([q_ref[0, part, :], query_rows], 0)
        ka = jnp.concatenate([k_ref[0, part, :], key_rows], 0)
        va = jnp.concatenate([v_ref[0, part, :], ones], 0)
        scores = dot(ka, qa, 0, 0) + pick_bias(first, own_ref, got_ref, j)
        peak = jnp.max(scores, 0, keepdims=True)
        weights = jnp.exp2(scores - peak).astype(BF)
        mixed = dot(va, weights, 1, 0)
        total = mixed[HD : HD + 1]
        out = mixed[:HD] / total
        att_ref[0, part, :] = out.astype(BF)
        exact_ref[0, part, :] = out
        lse_ref[0, 0, j : j + 1, :] = peak + jnp.log2(total)


def attention_specs(heads, skip=0):
    half = heads // (2 * GROUP)
    feat = pl.BlockSpec((1, GROUP * HD, TOKS), lambda h, w, core: (w, h + skip, 0))
    label = pl.BlockSpec((1, 1, TOKS), lambda h, w, core: (w, 0, 0))
    own = pl.BlockSpec((GROUP, HALF_ROWS, LANES), lambda h, w, core: (h + skip, 0, 0))
    got = pl.BlockSpec((GROUP, HALF_ROWS, LANES), lambda h, w, core: ((h + skip + half) % (2 * half), 0, 0))
    stat = pl.BlockSpec((1, 1, GROUP, TOKS), lambda h, w, core: (w, h + skip, 0, 0))
    return feat, label, own, got, stat


def attend(core, q, k, v, labels, own, got, deps):
    wins, feats, toks = q.shape
    heads = feats // HD
    feat, label, own_spec, got_spec, stat = attention_specs(heads)
    return pl.pallas_call(
        attend_kernel,
        grid_spec=pltpu.PrefetchScalarGridSpec(
            num_scalar_prefetch=1,
            grid=(heads // GROUP, wins),
            in_specs=[feat, feat, feat, label, own_spec, got_spec] + [ANY] * len(deps),
            out_specs=[feat, feat, stat],
        ),
        out_shape=[
            jax.ShapeDtypeStruct(q.shape, BF),
            jax.ShapeDtypeStruct(q.shape, F32),
            jax.ShapeDtypeStruct((wins, heads // GROUP, GROUP, toks), F32),
        ],
        compiler_params=params(),
        cost_estimate=cost(40 * wins * feats * toks * toks, wins * feats * toks * 12, wins * heads * toks * toks),
        name="attend",
    )(core, q, k, v, labels, own, got, *deps)


def split3(row):
    hi = row.astype(BF)
    rest = row - hi.astype(F32)
    mid = rest.astype(BF)
    return hi.astype(F32), mid.astype(F32), rest - mid.astype(F32)


def rows16(parts, width):
    rows = lax.broadcasted_iota(jnp.int32, (16, width), 0)
    out = jnp.zeros((16, width), F32)
    for i, part in enumerate(parts):
        out = jnp.where(rows == i, part, out)
    return out.astype(BF)


def attend_back_kernel(scale, core_ref, q_ref, k_ref, v_ref, label_ref, own_ref, got_ref, exact_ref, lse_ref, g_ref, *rest):
    dq_ref, dk_ref, dv_ref, pair_ref, sent_ref, sums = rest[-6:]
    core = core_ref[0]
    first = core_ref[0] == 0
    win = pl.program_id(1)
    minus = rows16([-1.0, -1.0, -1.0], TOKS)
    query_rows, key_rows = region_rows(label_ref[0])
    for j in range(GROUP):
        part = pl.ds(j * HD, HD)
        q = q_ref[0, part, :]
        k = k_ref[0, part, :]
        g = g_ref[0, part, :]
        qa = jnp.concatenate([q, query_rows, rows16(split3(lse_ref[0, 0, j : j + 1, :]), TOKS)], 0)
        ka = jnp.concatenate([k, key_rows, minus], 0)
        va = jnp.concatenate([v_ref[0, part, :], minus], 0)
        along = jnp.sum(g.astype(F32) * exact_ref[0, part, :], 0, keepdims=True)
        ga = jnp.concatenate([g, rows16(split3(along), TOKS)], 0)
        probs = jnp.exp2(dot(ka, qa, 0, 0) + pick_bias(first, own_ref, got_ref, j))
        grads = (probs * dot(va, ga, 0, 0)).astype(BF)
        low = probs.astype(BF)
        dv_ref[0, part, :] = dot(g, low, 1, 1).astype(BF)
        dk_ref[0, part, :] = (dot(q, grads, 1, 1) * (1.0 / LOG2E)).astype(BF)
        dq_ref[0, part, :] = (dot(k, grads, 1, 0) * scale).astype(BF)
        wide = grads.astype(F32)

        @pl.when(win == 0)
        def _():
            sums[j] = wide

        @pl.when(win > 0)
        def _():
            sums[j] = sums[j] + wide

        @pl.when(win == pl.num_programs(1) - 1)
        def _():
            step = TOKS - HALF_ROWS
            mine, other = pl.multiple_of(core * step, 8), pl.multiple_of((1 - core) * step, 8)
            pair_ref[j, :, :TOKS] = sums[j, pl.ds(mine, HALF_ROWS), :].astype(BF)
            sent_ref[j, :, :TOKS] = sums[j, pl.ds(other, HALF_ROWS), :].astype(BF)


def attend_back(core, q, k, v, labels, own, got, exact, lse, g, scale, side):
    wins, feats, toks = q.shape
    heads = feats // HD
    blocks = heads // (2 * GROUP)
    feat, label, own_spec, got_spec, stat = attention_specs(heads, side * blocks)
    out = pl.BlockSpec((1, GROUP * HD, toks), lambda h, w, core: (w, h, 0))
    pair = pl.BlockSpec((GROUP, HALF_ROWS, LANES), lambda h, w, core: (h, 0, 0))
    return pl.pallas_call(
        functools.partial(attend_back_kernel, scale),
        grid_spec=pltpu.PrefetchScalarGridSpec(
            num_scalar_prefetch=1,
            grid=(blocks, wins),
            in_specs=[feat, feat, feat, label, own_spec, got_spec, feat, stat, feat],
            out_specs=[out, out, out, pair, pair],
            scratch_shapes=[pltpu.VMEM((GROUP, toks, toks), F32)],
        ),
        out_shape=[jax.ShapeDtypeStruct((wins, feats // 2, toks), BF)] * 3 + [jax.ShapeDtypeStruct((heads // 2, HALF_ROWS, LANES), BF)] * 2,
        compiler_params=params(),
        cost_estimate=cost(0, 0),
        name="attend_back",
    )(core, q, k, v, labels, own, got, exact, lse, g)


def front_kernel(scale, xm_ref, xo_ref, own_ref, got_ref, wm_ref, wo_ref, *rest):
    q_ref, k_ref, v_ref = rest[-3:]
    x = jnp.concatenate([xm_ref[0], xo_ref[0]], 1).astype(F32)
    xhat, _ = normed(x)
    first = (xhat * row_pair(own_ref, got_ref, GAIN1) + row_pair(own_ref, got_ref, SHIFT1)).astype(BF)
    for t, (w_ref, vec_ref) in enumerate(((wm_ref, own_ref), (wo_ref, got_ref))):
        cols = w_ref.shape[1] // 3
        rows = pl.ds(t * cols, cols)
        made = dot(first if t == 0 else flip(first), w_ref[...], 1, 0)
        q = (made[:, :cols] + vec_ref[BIAS_Q : BIAS_Q + 1, :]) * scale
        v = made[:, 2 * cols :] + vec_ref[BIAS_V : BIAS_V + 1, :]
        q_ref[0, rows, :] = q.astype(BF).T
        k_ref[0, rows, :] = made[:, cols : 2 * cols].astype(BF).T
        v_ref[0, rows, :] = v.astype(BF).T


def front(xm, xo, own, got, wm, wo, scale, deps):
    wins, toks, half = xm.shape
    out = jax.ShapeDtypeStruct((wins, 2 * (wm.shape[1] // 3), toks), BF)
    return pl.pallas_call(
        functools.partial(front_kernel, scale),
        grid=(wins,),
        in_specs=[window_spec(xm), window_spec(xo), whole_spec(own), whole_spec(got), whole_spec(wm), whole_spec(wo)] + [ANY] * len(deps),
        out_specs=[window_spec(out)] * 3,
        out_shape=[out] * 3,
        compiler_params=params(),
        cost_estimate=cost(8 * wins * toks * half * wm.shape[1], wins * toks * half * 16 + wm.size * 4),
        name="front",
    )(xm, xo, own, got, wm, wo, *deps)


def middle_kernel(xm_ref, xo_ref, att_ref, own_ref, got_ref, wm_ref, wo_ref, *rest):
    mid_ref, second_ref, act_ref, slope_ref = rest[-4:]
    half = xm_ref.shape[2]
    wide = wm_ref.shape[1] - half
    restored = att_ref[0].T
    branch = dot(restored[:, :half], wm_ref[:, :half], 1, 1) + flip(dot(restored[:, half:], wo_ref[:, :half], 1, 1))
    x = jnp.concatenate([xm_ref[0], xo_ref[0]], 1).astype(F32)
    middle = x + (branch + row_pair(own_ref, got_ref, BIAS_P))
    mid_ref[0] = middle
    xhat, _ = normed(middle)
    second = (xhat * row_pair(own_ref, got_ref, GAIN2) + row_pair(own_ref, got_ref, SHIFT2)).astype(BF)
    second_ref[0] = second
    turned = flip(second)
    for t, (w_ref, vec_ref) in enumerate(((wm_ref, own_ref), (wo_ref, got_ref))):
        for s in range(0, wide, 256):
            at = t * wide + s
            bias = vec_ref[BIAS1 + s // 256 : BIAS1 + s // 256 + 1, :]
            hidden = dot(second if t == 0 else turned, w_ref[:, half + s : half + s + 256], 1, 0) + bias
            phi = 0.5 + 0.5 * lax.erf(hidden * (0.5**0.5))
            bell = jnp.exp2(hidden * hidden * (-0.5 * LOG2E)) * (1.0 / (2.0 * np.pi) ** 0.5)
            act_ref[0, :, at : at + 256] = (hidden * phi).astype(BF)
            slope_ref[0, :, at : at + 256] = (phi + hidden * bell).astype(BF)


def middle_forward(xm, xo, att, own, got, wm, wo, deps):
    wins, toks, half = xm.shape
    width = 2 * half
    hidden = 2 * (wm.shape[1] - half)
    wide = jax.ShapeDtypeStruct((wins, toks, hidden), BF)
    outs = [jax.ShapeDtypeStruct((wins, toks, width), F32), jax.ShapeDtypeStruct((wins, toks, width), BF), wide, wide]
    fixed = (own, got, wm, wo)
    return pl.pallas_call(
        middle_kernel,
        grid=(wins,),
        in_specs=[window_spec(xm), window_spec(xo), window_spec(att)] + [whole_spec(a) for a in fixed] + [ANY] * len(deps),
        out_specs=[window_spec(o) for o in outs],
        out_shape=outs,
        compiler_params=params(),
        cost_estimate=cost(8 * wins * toks * width * wm.shape[1], wins * toks * (width * 10 + hidden * 4) + wm.size * 4, wins * toks * hidden),
        name="middle_forward",
    )(xm, xo, att, *fixed, *deps)


def middle_back_kernel(cm_ref, co_ref, mid_ref, second_ref, act_ref, slope_ref, att_ref, own_ref, got_ref, wm_ref, wo_ref, fm_ref, fo_ref, *rest):
    outm_ref, outo_ref, gm_ref, gr_ref, dm_ref, do_ref, small_ref, wide_ref, accm, acco = rest[-10:]
    win = pl.program_id(0)
    half = cm_ref.shape[2]
    wide = fm_ref.shape[1]

    @pl.when(win == 0)
    def _():
        accm[...] = jnp.zeros_like(accm)
        acco[...] = jnp.zeros_like(acco)
        small_ref[...] = jnp.zeros_like(small_ref)
        wide_ref[...] = jnp.zeros_like(wide_ref)

    cot = jnp.concatenate([cm_ref[0], co_ref[0]], 1)
    cot_turned = flip(cot)
    cot_t = cot.T
    second_t = second_ref[0].T
    sides = (
        (wm_ref, fm_ref, accm, cot, cot_t, second_t),
        (wo_ref, fo_ref, acco, cot_turned, flip(cot_t, 0), flip(second_t, 0)),
    )
    made, pulled = [], []
    for t, (w_ref, f_ref, acc, c, c_t, s_t) in enumerate(sides):
        forward = jnp.zeros(cot.shape, F32)
        grad_second = jnp.zeros(cot.shape, F32)
        for s in range(0, wide, 512):
            span = slice(t * wide + s, t * wide + s + 512)
            fc2 = f_ref[:, s : s + 512]
            active = act_ref[0, :, span]
            forward = forward + dot(active, fc2, 1, 1)
            grad = (dot(c, fc2, 1, 0) * slope_ref[0, :, span].astype(F32)).astype(BF)
            wide_ref[:, span] += jnp.sum(grad.astype(F32), 0, keepdims=True)
            acc[:, half + wide + s : half + wide + s + 512] += dot(c_t, active, 1, 0)
            acc[:, half + s : half + s + 512] += dot(s_t, grad, 1, 0)
            grad_second = grad_second + dot(grad, w_ref[:, half + s : half + s + 512], 1, 1)
        made.append(forward)
        pulled.append(grad_second)
    out = mid_ref[0] + (made[0] + flip(made[1]) + row_pair(own_ref, got_ref, BIAS2))
    outm_ref[0] = out[:, :half].astype(BF)
    outo_ref[0] = out[:, half:].astype(BF)
    grad_second = pulled[0] + flip(pulled[1])
    upstream = cot.astype(F32)
    xhat, inv = normed(mid_ref[0])
    grad_mid = upstream + norm_back(grad_second, xhat, inv, row_pair(own_ref, got_ref, GAIN2))
    gm_ref[0] = grad_mid
    branch = grad_mid.astype(BF)
    branch_t = branch.T
    gr_ref[0, :half, :] = dot(branch, wm_ref[:, :half], 1, 0).astype(BF).T
    gr_ref[0, half:, :] = dot(flip(branch), wo_ref[:, :half], 1, 0).astype(BF).T
    accm[:, :half] += dot(branch_t, att_ref[0, :half, :], 1, 1)
    acco[:, :half] += dot(flip(branch_t, 0), att_ref[0, half:, :], 1, 1)
    small_ref[0:1, :] += jnp.sum(upstream, 0, keepdims=True)
    small_ref[1:2, :] += jnp.sum(grad_second * xhat, 0, keepdims=True)
    small_ref[2:3, :] += jnp.sum(grad_second, 0, keepdims=True)
    small_ref[3:4, :] += jnp.sum(branch.astype(F32), 0, keepdims=True)

    @pl.when(win == pl.num_programs(0) - 1)
    def _():
        dm_ref[...] = accm[...].astype(BF)
        do_ref[...] = acco[...].astype(BF)


def middle_back(cm, co, mid, second, act, slope, att, own, got, wm, wo, fm, fo, deps):
    wins, toks, half = cm.shape
    width = 2 * half
    hidden = act.shape[2]
    windows = (cm, co, mid, second, act, slope, att)
    fixed = (own, got, wm, wo, fm, fo)
    plain = jax.ShapeDtypeStruct(cm.shape, BF)
    outs = [plain, plain, jax.ShapeDtypeStruct(mid.shape, F32), jax.ShapeDtypeStruct(att.shape, BF)]
    grads = jax.ShapeDtypeStruct((width, wm.shape[1] + fm.shape[1]), BF)
    sums = [grads, grads, jax.ShapeDtypeStruct((4, width), F32), jax.ShapeDtypeStruct((1, hidden), F32)]
    return pl.pallas_call(
        middle_back_kernel,
        grid=(wins,),
        in_specs=[window_spec(a) for a in windows] + [whole_spec(a) for a in fixed] + [ANY] * len(deps),
        out_specs=[window_spec(o) for o in outs] + [whole_spec(o) for o in sums],
        out_shape=outs + sums,
        scratch_shapes=[pltpu.VMEM(grads.shape, F32), pltpu.VMEM(grads.shape, F32)],
        compiler_params=params(),
        cost_estimate=cost(12 * wins * toks * width * (width + 2 * hidden), wins * toks * (width * 16 + hidden * 4) + fm.size * 12),
        name="middle_back",
    )(*windows, *fixed, *deps)


def first_rows(xm_ref, xo_ref, own_ref, got_ref):
    xhat, inv = normed(jnp.concatenate([xm_ref[0], xo_ref[0]], 1).astype(F32))
    gain = row_pair(own_ref, got_ref, GAIN1)
    return xhat, inv, gain, (xhat * gain + row_pair(own_ref, got_ref, SHIFT1)).astype(BF)


def side_kernel(xm_ref, xo_ref, dq_ref, dk_ref, dv_ref, own_ref, got_ref, do_ref, acc):
    win = pl.program_id(0)
    _, _, _, first = first_rows(xm_ref, xo_ref, own_ref, got_ref)
    grads = jnp.concatenate([dq_ref[0], dk_ref[0], dv_ref[0]], 0)
    part = dot(flip(first.T, 0), grads, 1, 1)

    @pl.when(win == 0)
    def _():
        acc[...] = part

    @pl.when(win > 0)
    def _():
        acc[...] += part

    @pl.when(win == pl.num_programs(0) - 1)
    def _():
        do_ref[...] = acc[...].astype(BF)


def side_grads(xm, xo, grads, own, got):
    wins, toks, half = xm.shape
    windows = (xm, xo) + grads
    out = jax.ShapeDtypeStruct((2 * half, 3 * half), BF)
    return pl.pallas_call(
        side_kernel,
        grid=(wins,),
        in_specs=[window_spec(a) for a in windows] + [whole_spec(own), whole_spec(got)],
        out_specs=whole_spec(out),
        out_shape=out,
        scratch_shapes=[pltpu.VMEM(out.shape, F32)],
        compiler_params=params(),
        cost_estimate=cost(0, 0),
        name="side_grads",
    )(*windows, own, got)


def back_kernel(xm_ref, xo_ref, qm_ref, km_ref, vm_ref, qo_ref, ko_ref, vo_ref, gm_ref, own_ref, got_ref, wm_ref, wo_ref, side_ref, gxm_ref, gxo_ref, dm_ref, small_ref, acc):
    win = pl.program_id(0)

    @pl.when(win == 0)
    def _():
        acc[...] = side_ref[...].astype(F32)
        small_ref[...] = jnp.zeros_like(small_ref)

    xhat, inv, gain, first = first_rows(xm_ref, xo_ref, own_ref, got_ref)
    half = xm_ref.shape[2]
    mine = jnp.concatenate([qm_ref[0], km_ref[0], vm_ref[0]], 0)
    other = jnp.concatenate([qo_ref[0], ko_ref[0], vo_ref[0]], 0)
    acc[...] += dot(first.T, mine, 1, 1)
    grad_first = dot(mine, wm_ref[...], 0, 1) + flip(dot(other, wo_ref[...], 0, 1))
    grad_first = grad_first.astype(BF).astype(F32)
    grad_x = gm_ref[0] + norm_back(grad_first, xhat, inv, gain)
    gxm_ref[0] = grad_x[:, :half].astype(BF)
    gxo_ref[0] = grad_x[:, half:].astype(BF)
    ones = jnp.ones((8, mine.shape[1]), BF)
    for t, side in enumerate((mine, other)):
        sums = dot(ones, side, 1, 1)[0:1]
        span = slice(t * half, (t + 1) * half)
        small_ref[0:1, span] += sums[:, :half]
        small_ref[1:2, span] += sums[:, 2 * half :]
    small_ref[2:3, :] += jnp.sum(grad_first * xhat, 0, keepdims=True)
    small_ref[3:4, :] += jnp.sum(grad_first, 0, keepdims=True)

    @pl.when(win == pl.num_programs(0) - 1)
    def _():
        dm_ref[...] = acc[...].astype(BF)


def back(xm, xo, mine, other, gm, own, got, wm, wo, side):
    wins, toks, half = xm.shape
    windows = (xm, xo) + mine + other + (gm,)
    fixed = (own, got, wm, wo, side)
    plain = jax.ShapeDtypeStruct(xm.shape, BF)
    grads = jax.ShapeDtypeStruct(wm.shape, BF)
    small = jax.ShapeDtypeStruct((4, 2 * half), F32)
    return pl.pallas_call(
        back_kernel,
        grid=(wins,),
        in_specs=[window_spec(a) for a in windows] + [whole_spec(a) for a in fixed],
        out_specs=[window_spec(plain), window_spec(plain), whole_spec(grads), whole_spec(small)],
        out_shape=[plain, plain, grads, small],
        scratch_shapes=[pltpu.VMEM(wm.shape, F32)],
        compiler_params=params(),
        cost_estimate=cost(0, 0),
        name="back",
    )(*windows, *fixed)


def one_hot_rows(picks, size):
    cells = lax.broadcasted_iota(jnp.int32, (picks.shape[0], size), 1)
    return jnp.where(cells == picks, 1.0, 0.0).astype(BF)


def select_in_kernel(core_ref, picks_ref, near_ref, far_ref, out_ref):
    skip = WTOK - SENT_IN
    near = jnp.concatenate([near_ref[w, skip:, :] for w in range(4)], 0)
    low = dot(one_hot_rows(picks_ref[0, 0, :SENT_IN, :], near.shape[0]), near, 1, 0)
    high = dot(one_hot_rows(picks_ref[0, 0, skip:, :], far_ref.shape[0]), far_ref[...], 1, 0)
    over = SENT_IN - skip
    rows = lax.broadcasted_iota(jnp.int32, (over, 1), 0) + skip
    whole = jnp.concatenate([low[:skip], jnp.where(rows < HELD, low[skip:], high[:over]), high[over:]], 0)
    out_ref[0] = whole.astype(BF)


def select_in(core, picks, near, far):
    width = near.shape[2]
    out = jax.ShapeDtypeStruct((4, TOKS, width), BF)
    return pl.pallas_call(
        select_in_kernel,
        grid_spec=pltpu.PrefetchScalarGridSpec(
            num_scalar_prefetch=1,
            grid=(4,),
            in_specs=[pl.BlockSpec((1, 1, TOKS, 1), lambda i, core: (core[0], i, 0, 0)), whole_spec(near), whole_spec(far)],
            out_specs=window_spec(out),
        ),
        out_shape=out,
        compiler_params=params(),
        cost_estimate=cost(0, 0),
        name="select_in",
    )(core, picks, near, far)


def select_out_kernel(core_ref, picks_ref, kept_ref, beside_ref, across_ref, corner_ref, out_ref):
    skip = WTOK - SENT_IN
    near = jnp.concatenate([kept_ref[...], beside_ref[...]], 0)
    far = jnp.concatenate([across_ref[...], corner_ref[...]], 0)
    low = dot(one_hot_rows(picks_ref[0, 0, :SENT_IN, :], far.shape[0]), far, 1, 0)
    high = dot(one_hot_rows(picks_ref[0, 0, skip:, :], near.shape[0]), near, 1, 0)
    rows = lax.broadcasted_iota(jnp.int32, (SENT_IN - skip, 1), 0) + skip
    out_ref[0, :skip, :] = low[:skip]
    out_ref[0, skip:SENT_IN, :] = jnp.where(rows < HELD, low[skip:], high[: SENT_IN - skip])
    out_ref[0, SENT_IN:, :] = high[SENT_IN - skip :]


def select_out(core, picks, arrays):
    width = arrays[0].shape[1]
    out = jax.ShapeDtypeStruct((4, WTOK, width), F32)
    return pl.pallas_call(
        select_out_kernel,
        grid_spec=pltpu.PrefetchScalarGridSpec(
            num_scalar_prefetch=1,
            grid=(4,),
            in_specs=[pl.BlockSpec((1, 1, WTOK, 1), lambda i, core: (core[0], i, 0, 0))] + [whole_spec(a) for a in arrays],
            out_specs=window_spec(out),
        ),
        out_shape=out,
        compiler_params=params(),
        cost_estimate=cost(0, 0),
        name="select_out",
    )(core, picks, *arrays)


def bits_of(axis):
    return lax.axis_size(axis).bit_length() - 1


def bit_on(axis, bit):
    return lax.shift_right_logical(lax.axis_index(axis), bit) % 2


def swap(value, axis, bit=0):
    pairs = [(source, source ^ (1 << bit)) for source in range(lax.axis_size(axis))]
    return lax.ppermute(value, axis, pairs)


def bit_order():
    count = bits_of("shard")
    return list(range(1, count)) + [0]


def row_place(bit):
    place = bit_on("shard", bit)
    if bit == bits_of("shard") - 1:
        place = jnp.bitwise_xor(place, lax.axis_index("tensor"))
    return place


def ordered(on, mine, other, axis):
    return jnp.concatenate((jnp.where(on, other, mine), jnp.where(on, mine, other)), axis)


def after(value, *deps):
    return lax.optimization_barrier((value,) + deps)[0]


def gather_start(part):
    rows, cols = part.shape
    return part.reshape((1,) * bits_of("shard") + (rows, cols))


def gather_step(held, bit, *deps):
    got = after(swap(held, "shard", bit), *deps)
    return ordered(row_place(bit) == 1, held, got, bits_of("shard") - 1 - bit)


def choose(array, index, axis):
    return lax.dynamic_slice_in_dim(array, index, 1, axis)


def add_rounded(a, b):
    return (a.astype(F32) + b.astype(F32)).astype(BF)


def split_rows(part):
    count = bits_of("shard")
    return part.reshape((2,) * count + (part.shape[0] >> count, part.shape[1]))


def scatter_step(held, bit, *deps):
    axis = bits_of("shard") - 1 - bit
    own = row_place(bit)
    got = after(swap(choose(held, 1 - own, axis), "shard", bit), *deps)
    return add_rounded(choose(held, own, axis), got)


def ctx_split(held, bit, *deps):
    axis = held.ndim - 2
    half = held.shape[axis] // 2
    own = bit_on("ctx", bit)
    sent = lax.dynamic_slice_in_dim(held, (1 - own) * half, half, axis)
    got = after(swap(sent, "ctx", bit), *deps)
    return add_rounded(lax.dynamic_slice_in_dim(held, own * half, half, axis), got)


def ctx_join(held, bit, *deps):
    got = after(swap(held, "ctx", bit), *deps)
    return ordered(bit_on("ctx", bit) == 1, held, got, held.ndim - 2)


def flat(held):
    return held.reshape(held.shape[-2:])


def ctx_sum(held, *deps):
    held = flat(held)
    for bit in range(bits_of("ctx")):
        got = after(swap(held.astype(BF), "ctx", bit), *deps)
        held = held.astype(BF).astype(F32) + got.astype(F32)
    return held.astype(F32)


def joint_swap(value, mask):
    size = lax.axis_size("shard") * lax.axis_size("ctx")
    return lax.ppermute(value, ("shard", "ctx"), [(i, i ^ mask) for i in range(size)])


def joint_parts(value, bits):
    low = 1 << bits[0]
    if len(bits) == 1:
        return [value, joint_swap(value, low), jnp.zeros_like(value), jnp.zeros_like(value)]
    high = 1 << bits[1]
    return [value, joint_swap(value, low), joint_swap(value, high), joint_swap(value, low | high)]


def add_parts(parts):
    return (parts[0] + parts[1]) + (parts[2] + parts[3])


def joint_groups():
    bits = list(range(bits_of("shard") + bits_of("ctx")))
    return [bits[i : i + 2] for i in range(0, len(bits), 2)]


def roll_axis(shaped, axis_pos, levels, backward):
    token_axis = 4 + axis_pos
    length = shaped.shape[token_axis]
    border = length - length // 2 if backward else length // 2
    before = lax.slice_in_dim(shaped, 0, border, axis=token_axis)
    after = lax.slice_in_dim(shaped, border, length, axis=token_axis)
    moving = after if backward else before
    if axis_pos < levels:
        moving = swap(moving, "ctx", levels - 1 - axis_pos)
    else:
        moving = jnp.roll(moving, 1 if backward else -1, axis=1 + axis_pos)
    return jnp.concatenate((moving, before) if backward else (after, moving), axis=token_axis)


def window_roll(windows, clips, counts, backward):
    shaped = windows.reshape((clips,) + counts + (WT, WH, WW, windows.shape[-1]))
    for axis_pos in range(3):
        shaped = roll_axis(shaped, axis_pos, bits_of("ctx"), backward)
    return shaped.reshape(windows.shape)


HELD = WTOK // 2
SENT_IN = 200
SENT_OUT = 208


def frame_sources():
    source = np.zeros((4, HELD), np.int64)
    for h in range(2 * WH):
        for w in range(2 * WW):
            here = (h // WH) * 2 + w // WW
            there_h, there_w = (h + WH // 2) % (2 * WH), (w + WW // 2) % (2 * WW)
            there = (there_h // WH) * 2 + there_w // WW
            for a in range(WT // 2):
                row = (a * WH + h % WH) * WW + w % WW
                source[here, row] = there * HELD + (a * WH + there_h % WH) * WW + there_w % WW
    return source


def picks_in():
    source = frame_sources()
    there, row = source // HELD, source % HELD
    picks = np.full((4, TOKS), -1)
    picks[:, :HELD] = there * SENT_IN + row + SENT_IN - HELD
    picks[:, HELD:WTOK] = there * SENT_IN + row
    both = np.stack((picks, np.concatenate((picks[2:], picks[:2]))))
    return jnp.asarray(both[..., None], jnp.int32)


def picks_out():
    place = np.argsort(frame_sources().reshape(-1)).reshape(4, HELD)
    there, row = place // HELD, place % HELD
    both = []
    for core in range(2):
        block = ((there // 2 + core) % 2) * 2 * SENT_OUT + (there % 2) * SENT_OUT
        picks = np.zeros((4, WTOK), np.int64)
        picks[:, HELD:] = block + row
        picks[:, :HELD] = block + row + HELD - (TOKS - SENT_OUT)
        both.append(picks[..., None])
    return jnp.asarray(np.stack(both), jnp.int32)


def plain_ring(clips):
    return bits_of("ctx") == 1 and clips == 1


def shift_start(windows, clips):
    if plain_ring(clips):
        return swap(windows[:, :SENT_IN].reshape(-1, windows.shape[-1]), "ctx")
    return windows[:1, :8]


def shift_in(windows, got, clips, counts, core_row):
    half = windows.shape[0] // 2
    if plain_ring(clips):
        moved = select_in(core_row, picks_in(), windows, got)
        return moved[:half], swap(moved[half:], "tensor")
    moved = jnp.pad(window_roll(windows, clips, counts, False), ((0, 0), (0, TOKS - WTOK), (0, 0)))
    core = lax.axis_index("tensor")
    mine = lax.dynamic_slice_in_dim(moved, core * half, half, 0)
    return mine, swap(lax.dynamic_slice_in_dim(moved, (1 - core) * half, half, 0), "tensor")


def shift_out(mine, other, clips, counts, core_row, *deps):
    width = mine.shape[-1]
    if plain_ring(clips):
        cut = TOKS - SENT_OUT
        kept = after(mine[:, :SENT_OUT].reshape(-1, width), *deps)
        beside = swap(other[:, :SENT_OUT].reshape(-1, width), "tensor")
        across = swap(mine[:, cut:].reshape(-1, width), "ctx")
        corner = lax.ppermute(other[:, cut:].reshape(-1, width), ("ctx", "tensor"), [(i, i ^ 3) for i in range(4)])
        return select_out(core_row, picks_out(), (kept, beside, across, corner))
    other = swap(other, "tensor")
    windows = ordered(lax.axis_index("tensor") == 1, mine, other, 0)
    return window_roll(windows[:, :WTOK], clips, counts, True).astype(F32)


def on_device(
    clip_input,
    cotangent,
    gain_one,
    shift_one,
    w_qkv,
    b_qv,
    w_proj,
    b_proj,
    bias_table,
    gain_two,
    shift_two,
    w_fc1,
    b_fc1,
    w_fc2,
    b_fc2,
    rel_index,
    regions,
):
    clips, window_count, tokens, half_width = clip_input.shape
    heads = bias_table.shape[0]
    levels = bits_of("ctx")
    counts = tuple(1 if axis_pos < levels else 2 for axis_pos in range(3))
    core = lax.axis_index("tensor")
    core_row = core.astype(jnp.int32).reshape(1)
    total_windows = clips * window_count
    held_windows = total_windows // 2
    scale = HD ** (-0.5)
    hidden = w_fc1.shape[1]

    own = pack(gain_one, shift_one, b_qv, b_proj, gain_two, shift_two, b_fc2, b_fc1, bias_table)
    got = swap(own, "tensor")
    qkv = gather_start(w_qkv.transpose(1, 0, 2).reshape(w_qkv.shape[1], -1))
    early = gather_start(jnp.concatenate((w_proj.T, w_fc1), 1))
    late = gather_start(w_fc2.T)
    index = jnp.pad(rel_index.T, ((0, TOKS - tokens), (0, TOKS - tokens)))
    index = lax.dynamic_slice_in_dim(index, core * (TOKS - HALF_ROWS), HALF_ROWS, 0)
    labels = jnp.tile(regions, (clips, 1))
    labels = lax.dynamic_slice_in_dim(labels, core * held_windows, held_windows, 0)
    labels = jnp.pad(labels, ((0, 0), (0, TOKS - tokens)))[:, None, :]

    order = bit_order()
    first, middle, last = order[0], order[1:-1], order[-1]
    clip_rows = clip_input.reshape(total_windows, tokens, half_width)
    cot_rows = cotangent.reshape(total_windows, tokens, half_width)

    clip_got = shift_start(clip_rows, clips)
    qkv = gather_step(qkv, first)
    bias_own = lookup(after(index, qkv), own, got, heads, 0, HALF_ROWS // ROWS)
    early = after(early, qkv)
    for bit in middle:
        qkv = gather_step(qkv, bit, bias_own)
    clip_got = after(clip_got, bias_own)
    early = gather_step(early, first, qkv, clip_got)
    bias_got = after(swap(bias_own, "tensor"), qkv)
    xm, xo = shift_in(clip_rows, after(clip_got, early), clips, counts, core_row)
    cot_got = shift_start(after(cot_rows, clip_got), clips)
    qkv = gather_step(qkv, last, xm)
    late = gather_step(after(late, early), first, xm, qkv)
    for bit in middle:
        early = gather_step(early, bit, late)
    qkv = qkv.reshape(-1, qkv.shape[-1])
    qkv_other = swap(qkv, "tensor")
    queries, keys, values = front(after(xm, early), xo, own, got, qkv, qkv_other, scale * LOG2E, ())
    late = after(late, early)
    att, exact, lse = attend(core_row, queries, keys, values, labels, bias_own, bias_got, ())
    for bit in middle:
        late = gather_step(late, bit, att)
    early = gather_step(early, last, att, late)
    early = early.reshape(-1, early.shape[-1])
    early_other = swap(early, "tensor")
    mid, second, act, slope = middle_forward(xm, xo, att, own, got, early, early_other, ())
    cm, co = shift_in(cot_rows, after(cot_got, act), clips, counts, core_row)
    late = gather_step(late, last, cm)
    late = late.reshape(-1, late.shape[-1])
    late_other = swap(late, "tensor")
    outm, outo, grad_mid, grad_att, rest_mine, rest_other, small_mid, small_wide = middle_back(cm, co, mid, second, act, slope, att, own, got, early, early_other, late, late_other, ())

    order = order[::-1]
    twice = bits_of("ctx") == 1
    args = (core_row, queries, keys, values, labels, bias_own, bias_got, exact, lse)
    qo, ko, vo, pair_o, sent_o = attend_back(*args, grad_att, scale, 1)
    edge = half_width + hidden
    one_mine, one_other = rest_mine[:, half_width:edge], rest_other[:, half_width:edge]
    two_mine, two_other = [jnp.concatenate((r[:, :half_width], r[:, edge:]), 1) for r in (rest_mine, rest_other)]
    one = split_rows(add_rounded(one_mine, after(swap(one_other, "tensor"), qo)))
    two = split_rows(add_rounded(two_mine, after(swap(two_other, "tensor"), qo)))
    side = side_grads(xm, xo, (after(qo, one, two), ko, vo), own, got)
    qm, km, vm, pair_m, sent_m = attend_back(*args, after(grad_att, side), scale, 0)
    side = after(swap(side, "tensor"), qm)
    one = scatter_step(one, order[0], qm)
    two = ctx_split(two, 0, qm) if twice else scatter_step(two, order[0], qm)
    mine = (after(qm, one, two), km, vm)
    gxm, gxo, qkv_grads, small_end = back(xm, xo, mine, (qo, ko, vo), grad_mid, own, got, qkv, qkv_other, side)
    block_out = shift_out(outm, outo, clips, counts, core_row, small_end)
    one = scatter_step(one, order[1], block_out)
    two = scatter_step(two, order[0] if twice else order[1], block_out)
    qkv_grads = split_rows(qkv_grads)
    pairs = (pair_m, pair_o, after(swap(sent_m, "tensor"), small_end), swap(sent_o, "tensor"))
    block = HALF_ROWS // ROWS
    cut = block // 2
    (folded,) = fold(core_row, after(index, one, two), pairs, heads, 0, cut)
    qkv_grads = scatter_step(qkv_grads, order[0], folded)
    one = scatter_step(one, order[2], folded, qkv_grads)
    two = scatter_step(two, order[1] if twice else order[2], folded, qkv_grads)
    fold_mine, fold_other = fold(core_row, after(index, one, two, qkv_grads), pairs, heads, cut, block - cut, (folded, small_mid, small_wide, small_end))
    qkv_grads = scatter_step(qkv_grads, order[1], fold_mine)
    for bit in order[3:]:
        one = scatter_step(one, bit, fold_mine)
        two = two if twice else scatter_step(two, bit, fold_mine)
    if twice:
        for bit in order[2:]:
            two = scatter_step(two, bit, fold_mine)
    one = ctx_sum(one, fold_mine)
    small = fold_mine + swap(after(fold_other, qkv_grads), "tensor")
    groups = joint_groups()
    for group in groups[:-1]:
        small = add_parts(joint_parts(small, group))
    for bit in order[2:]:
        qkv_grads = scatter_step(qkv_grads, bit)
    two = flat(ctx_join(two, 0, small)).astype(F32) if twice else ctx_sum(two, small)
    grad_input = shift_out(gxm, gxo, clips, counts, core_row, small, qkv_grads)
    qkv_grads = ctx_sum(qkv_grads, grad_input)
    parts = joint_parts(small, groups[-1])
    parts = [parts[0], after(parts[1], grad_input)] + parts[2:]
    d_gain1, d_shift1, d_bqv, d_bp, d_table, d_gain2, d_shift2, d_b1, d_b2 = unpack(parts, heads)
    rows = w_fc1.shape[0]
    return (
        block_out.reshape(clip_input.shape),
        grad_input.reshape(clip_input.shape),
        d_gain1,
        d_shift1,
        qkv_grads.reshape(rows, 3, half_width).transpose(1, 0, 2),
        d_bqv,
        two[:, :half_width].T,
        d_bp,
        d_table,
        d_gain2,
        d_shift2,
        one,
        d_b1,
        two[:, half_width:].T,
        d_b2,
    )


def solution(mesh):
    in_specs = (
        P("shard", "ctx", None, "tensor"),
        P("shard", "ctx", None, "tensor"),
        P("tensor"),
        P("tensor"),
        P(None, "shard", "tensor"),
        P(None, "tensor"),
        P("tensor", "shard"),
        P("tensor"),
        P("tensor", None),
        P("tensor"),
        P("tensor"),
        P("shard", "tensor"),
        P("tensor"),
        P("tensor", "shard"),
        P("tensor"),
        P(),
        P("ctx", None),
    )
    out_specs = (
        P("shard", "ctx", None, "tensor"),
        P("shard", "ctx", None, "tensor"),
        P("tensor"),
        P("tensor"),
        P(None, "shard", "tensor"),
        P(None, "tensor"),
        P("tensor", "shard"),
        P("tensor"),
        P("tensor", None),
        P("tensor"),
        P("tensor"),
        P("shard", "tensor"),
        P("tensor"),
        P("tensor", "shard"),
        P("tensor"),
    )
    return jax.shard_map(
        on_device, mesh=mesh, in_specs=in_specs, out_specs=out_specs, check_vma=False
    )
```

time: 1230 us -> 271 us (0.22); the launches traced: 1220 us -> 270 us
  matrix products: 502 us -> 0 us
  blocking collectives: 201 us -> 0 us
  local copies, waits for them, and re-layouts: 211 us -> 28.7 us
  Pallas kernels: 0 us -> 155 us
  other arithmetic: 151 us -> 15.6 us
  waiting for transfers between devices: 122 us -> 25.8 us
  starting transfers between devices: 7.48 us -> 43.5 us
  between operations: 17.6 us -> 1.55 us
    dot_general x54 -> x0, matrix products: 502 us -> none  [the longest x14 225 us: fold_block(): jnp.einsum('hpb,pa->hab', weighted, coarse_table, precision=HIGHEST)]
    pallas_call x0 -> x17, Pallas kernels: none -> 155 us  [the longest x2 31 us: attend_back(): pl.pallas_call(functools.partial(attend_back_kernel, scale), grid_spec=pl...]
    psum x5 -> x0, blocking collectives: 117 us -> none  [the longest x1 102 us: on_device(): lax.psum((small_terms[0], small_terms[1], small_terms[2], small_terms[3],...]
    reduce_sum x12 -> x0, other arithmetic: 86.9 us -> none  [the longest x1 26.2 us: on_device(): jnp.sum(grad_first * normed_one, 0)]
    all_gather x6 -> x0, blocking collectives: 84 us -> none  [the longest x1 32.9 us: on_device(): lax.all_gather(w_qkv, 'shard', axis=1, tiled=True)]
    all_gather x6 -> x0, waiting for transfers between devices: 76.4 us -> none  [the longest x1 38 us: on_device(): lax.all_gather(w_fc2, 'shard', axis=1, tiled=True)]
    add x6 -> x0, local copies, waits for them, and re-layouts: 38.5 us -> none  [the longest x4 38.4 us: scored(): return raw_scores * scale + bias_full[None] + mask_add[:, None]]
    dynamic_slice x56 -> x12, local copies, waits for them, and re-layouts: 41.1 us -> 2.72 us  [the longest x9 1.03 us: choose(): return lax.dynamic_slice_in_dim(array, index, 1, axis)]
  transfers between devices with their start and end apart: 18 -> 49, of which waited for: 10 -> 9; matrix products, arithmetic and copies ran while one was open for 58% -> 10% of each run, Pallas kernels for 0% -> 43%
where the time goes in v2:
time: 271 us; the launch traced here: 270 us
  Pallas kernels  155 us (57%)
  starting transfers between devices  43.5 us (16%)
  local copies, waits for them, and re-layouts  28.7 us (11%)
  waiting for transfers between devices  25.8 us (10%)
  other arithmetic  15.6 us (6%)
    ppermute x41, starting transfers between devices, swap(): return lax.ppermute(value, axis, pairs)  35.5 us
    pallas_call x2, Pallas kernels, attend_back(): pl.pallas_call(functools.partial(attend_back_kernel, scale), grid_spec=pl...  31 us
    ppermute x41, waiting for transfers between devices, swap(): return lax.ppermute(value, axis, pairs)  22.2 us
    pallas_call x2, Pallas kernels, fold(): pl.pallas_call(functools.partial(fold_end_kernel if extra else fold_start...  22.2 us
    pallas_call x1, Pallas kernels, middle_back(): pl.pallas_call(middle_back_kernel, grid=(wins,), in_specs=[window_spec(a)...  20.5 us
    pallas_call x1, Pallas kernels, lookup(): pl.pallas_call(functools.partial(lookup_kernel, heads), grid=(rows // ROW...  17.3 us
    pallas_call x1, Pallas kernels, attend(): pl.pallas_call(attend_kernel, grid_spec=pltpu.PrefetchScalarGridSpec(num_...  16.1 us
    unnamed x78, local copies, waits for them, and re-layouts  13.5 us
  transfers between devices with their start and end apart: 49, of which 9 were waited for; matrix products, arithmetic and copies ran while one was open for 10% of the time, Pallas kernels for 43%

profile of v2, /device:TPU:0, one launch (start us, length us, event | category | flops | bytes accessed | tf_op | source)
XLA Modules:
  0.0 270.0 jit_solution(10814839924234118315)
XLA Ops:
  0.7 1.0 copy.38
  1.8 3.1 %collective-permute-start.1 = (bf16[1,1,1,64,768]{4,3,2,1,0:T(8,128)(2,1)S(1)}, bf16[1,1,1,64,768]{4,3,2,1,0:T(8,128)(2,1)S(1)}, u32[]{:S(2)}, u32[]{:S(2)}) collective-permute-start(bf16[1,1,1,64,768]{4,3,2,1,0:T(8,128)(2,1)S(1)} %reshape_reshape.3), channel_id=1, source_target_pairs={{0,8},{4,12},{8,0},{12,4},{16,24},{20,28},{24,16},{28,20},{1,9},{5... | collective-permute-start | bytes 294920 | tf_op jit(solution)/shard_map/ppermute | solution.py:756
  4.9 1.7 pack.1.own_ref
  6.5 1.4 copy.37
  10.2 17.3 %table_lookup.1.own_ref = bf16[16,208,512]{2,1,0:T(8,128)(2,1)} custom-call(s32[208,400]{1,0:T(8,128)} %pad_dynamic-slice_fusion.idx_ref, f32[96,256]{1,0:T(8,128)} %pack.1.own_ref, f32[96,256]{1,0:T(8,128)} %copy-done.8), custom_call_target="tpu_custom_call" | custom-call | flops 1 | bytes 1 | tf_op jit(solution)/shard_map/table_lookup/pallas_call | solution.py:174
  28.7 1.5 collective-permute-start
  30.2 2.6 collective-permute-start.5
  33.9 8.3 %collective-permute-done.5 = bf16[1,2,1,64,768]{4,3,2,1,0:T(8,128)(2,1)} collective-permute-done((bf16[1,2,1,64,768]{4,3,2,1,0:T(8,128)(2,1)}, bf16[1,2,1,64,768]{4,3,2,1,0:T(8,128)(2,1)}, u32[]{:S(2)}, u32[]{:S(2)}) %collective-permute-start.5) | collective-permute-done | bytes 196640 | tf_op jit(solution)/shard_map/ppermute | solution.py:756
  42.3 1.0 broadcast_select_fusion.11
  43.3 1.6 collective-permute-start.9
  45.0 0.9 broadcast_select_fusion.13
  46.0 3.2 %collective-permute-start.8 = (bf16[1,1,1,64,1024]{4,3,2,1,0:T(8,128)(2,1)S(1)}, bf16[1,1,1,64,1024]{4,3,2,1,0:T(8,128)(2,1)S(1)}, u32[]{:S(2)}, u32[]{:S(2)}) collective-permute-start(bf16[1,1,1,64,1024]{4,3,2,1,0:T(8,128)(2,1)S(1)} %bitcast.70), channel_id=1, source_target_pairs={{0,8},{4,12},{8,0},{12,4},{16,24},{20,28},{24,16},{28,20},{1,9},{5... | collective-permute-start | bytes 393224 | tf_op jit(solution)/shard_map/ppermute | solution.py:756
  49.2 4.7 %select_in.2 = bf16[4,400,256]{2,1,0:T(8,128)(2,1)} custom-call(s32[1]{0:T(128)} %bitcast.core_ref, s32[2,4,400,1]{3,2,1,0:T(8,128)} %constant.89.clone.picks_ref, bf16[4,392,256]{2,1,0:T(8,128)(2,1)} %bitcast.53, bf16[800,256]{1,0:T(8,128)(2,1)} %collective-permute-done.far_ref), custom_call_target="tpu_custom_call" | custom-call | flops 1 | bytes 1 | tf_op jit(solution)/shard_map/select_in/pallas_call | solution.py:701
  53.9 2.1 fusion.3
  56.0 1.0 pad_maximum_fusion.3
  58.2 4.3 %collective-permute-done.7 = bf16[1,2,1,64,1280]{4,3,2,1,0:T(8,128)(2,1)S(1)} collective-permute-done((bf16[1,2,1,64,1280]{4,3,2,1,0:T(8,128)(2,1)S(1)}, bf16[1,2,1,64,1280]{4,3,2,1,0:T(8,128)(2,1)S(1)}, u32[]{:S(2)}, u32[]{:S(2)}) %collective-permute-start.7) | collective-permute-done | bytes 327712 | tf_op jit(solution)/shard_map/ppermute | solution.py:756
  65.4 4.8 %front.1 = (bf16[2,512,400]{2,1,0:T(8,128)(2,1)}, bf16[2,512,400]{2,1,0:T(8,128)(2,1)}, bf16[2,512,400]{2,1,0:T(8,128)(2,1)}) custom-call(bf16[2,400,256]{2,1,0:T(8,128)(2,1)} %get-tuple-element.112.xm_ref, bf16[2,400,256]{2,1,0:T(8,128)(2,1)} %collective-permute-done.6.xo_ref, f32[96,256]{1,0:T(8,128)} %pack.1.own_ref, f32[96,256]{1,0:T(8,128)} %copy-done.8, ...), custom_call_target="tpu_custom_call" | custom-call | flops 1 | bytes 1 | tf_op jit(solution)/shard_map/front/pallas_call | solution.py:448
  70.2 1.7 copy-done.2
  71.9 16.1 %attend.1 = (bf16[2,512,400]{2,1,0:T(8,128)(2,1)}, f32[2,512,400]{2,1,0:T(8,128)}, f32[2,4,4,400]{3,2,1,0:T(4,128)}) custom-call(s32[1]{0:T(128)} %bitcast.core_ref, bf16[2,512,400]{2,1,0:T(8,128)(2,1)} %get-tuple-element.113.q_ref, bf16[2,512,400]{2,1,0:T(8,128)(2,1)} %get-tuple-element.114.k_ref, bf16[2,512,400]{2,1,0:T(8,128)(2,1)} %get-tuple-element.115.v_ref, ...), custom_call_target="tpu_custom_call" | custom-call | flops 1 | bytes 1 | tf_op jit(solution)/shard_map/attend/pallas_call | solution.py:331
  88.1 1.1 broadcast_select_fusion.9
  89.3 1.2 broadcast_select_fusion.1
  90.7 1.1 copy-done.15
  92.5 1.3 collective-permute-start.16
  93.8 1.1 copy-done.6
  94.9 8.4 %middle_forward.1 = (f32[2,400,512]{2,1,0:T(8,128)}, bf16[2,400,512]{2,1,0:T(8,128)(2,1)}, bf16[2,400,2048]{2,1,0:T(8,128)(2,1)}, bf16[2,400,2048]{2,1,0:T(8,128)(2,1)}) custom-call(bf16[2,400,256]{2,1,0:T(8,128)(2,1)} %get-tuple-element.112.xm_ref, bf16[2,400,256]{2,1,0:T(8,128)(2,1)} %collective-permute-done.6.xo_ref, ...), custom_call_target="tpu_custom_call" | custom-call | flops 1 | bytes 1 | tf_op jit(solution)/shard_map/middle_forward/pallas_call | solution.py:491
  104.0 4.6 %select_in.3 = bf16[4,400,256]{2,1,0:T(8,128)(2,1)} custom-call(s32[1]{0:T(128)} %bitcast.core_ref, s32[2,4,400,1]{3,2,1,0:T(8,128)} %constant.89.clone.picks_ref, bf16[4,392,256]{2,1,0:T(8,128)(2,1)} %bitcast.55, bf16[800,256]{1,0:T(8,128)(2,1)} %copy-done.24), custom_call_target="tpu_custom_call" | custom-call | flops 1 | bytes 1 | tf_op jit(solution)/shard_map/select_in/pallas_call | solution.py:701
  108.7 1.9 fusion.2
  111.4 2.7 %collective-permute-done.15.co_ref = bf16[2,400,256]{2,1,0:T(8,128)(2,1)S(1)} collective-permute-done((bf16[2,400,256]{2,1,0:T(8,128)(2,1)S(1)}, bf16[2,400,256]{2,1,0:T(8,128)(2,1)S(1)}, u32[]{:S(2)}, u32[]{:S(2)}) %collective-permute-start.15) | collective-permute-done | bytes 409632 | tf_op jit(solution)/shard_map/ppermute | solution.py:756
  115.3 20.5 %middle_back.1 = (bf16[2,400,256]{2,1,0:T(8,128)(2,1)}, bf16[2,400,256]{2,1,0:T(8,128)(2,1)}, f32[2,400,512]{2,1,0:T(8,128)}, bf16[2,512,400]{2,1,0:T(8,128)(2,1...) custom-call(bf16[2,400,256]{2,1,0:T(8,128)(2,1)} %get-tuple-element.209.cm_ref,, ...), custom_call_target="tpu_custom_call" | custom-call | flops 1 | bytes 1 | tf_op jit(solution)/shard_map/middle_back/pallas_call | solution.py:575
  135.8 1.7 fusion.1
  137.5 1.0 slice.77
  139.2 15.4 %attend_back.2 = (bf16[2,256,400]{2,1,0:T(8,128)(2,1)}, bf16[2,256,400]{2,1,0:T(8,128)(2,1)}, bf16[2,256,400]{2,1,0:T(8,128)(2,1)}, bf16[8,208,512]{2,1,0:T(8,128)(2,1)}, bf16[8,208,512]{2,1,0:T(8,128)(2,1)}) custom-call(s32[1]{0:T(128)} %bitcast.core_ref, bf16[2,512,400]{2,1,0:T(8,128)(2,1)} %get-tuple-element.113.q_ref, ...), custom_call_target="tpu_custom_call" | custom-call | flops 1 | bytes 1 | tf_op jit(solution)/shard_map/attend_back/pallas_call | solution.py:413
  156.0 1.5 collective-permute-start.20
  157.5 1.6 add_convert_fusion
  160.8 0.9 fusion.6
  162.2 4.4 %side_grads.1 = bf16[512,768]{1,0:T(8,128)(2,1)} custom-call(bf16[2,400,256]{2,1,0:T(8,128)(2,1)} %get-tuple-element.112.xm_ref, bf16[2,400,256]{2,1,0:T(8,128)(2,1)} %collective-permute-done.6.xo_ref, bf16[2,256,400]{2,1,0:T(8,128)(2,1)} %get-tuple-element.136.dq_ref.qo_ref, bf16[2,256,400]{2,1,0:T(8,128)(2,1)} %get-tuple-element.137.dk_ref.ko_ref, ...), custom_call_target="tpu_custom_call" | custom-call | flops 1 | bytes 1 | tf_op jit(solution)/shard_map/side_grads/pallas_call | solution.py:617
  166.7 15.6 %attend_back.3 = (bf16[2,256,400]{2,1,0:T(8,128)(2,1)}, bf16[2,256,400]{2,1,0:T(8,128)(2,1)}, bf16[2,256,400]{2,1,0:T(8,128)(2,1)}, bf16[8,208,512]{2,1,0:T(8,128)(2,1)}, bf16[8,208,512]{2,1,0:T(8,128)(2,1)}) custom-call(s32[1]{0:T(128)} %bitcast.core_ref, bf16[2,512,400]{2,1,0:T(8,128)(2,1)} %get-tuple-element.113.q_ref, ...), custom_call_target="tpu_custom_call" | custom-call | flops 1 | bytes 1 | tf_op jit(solution)/shard_map/attend_back/pallas_call | solution.py:413
  182.8 1.2 add_convert_fusion.3
  184.1 3.0 %collective-permute-start.26 = (bf16[1,2,1,64,1024]{4,3,2,1,0:T(8,128)(2,1)S(1)}, bf16[1,2,1,64,1024]{4,3,2,1,0:T(8,128)(2,1)S(1)}, u32[]{:S(2)}, u32[]{:S(2)}) collective-permute-start(bf16[1,2,1,64,1024]{4,3,2,1,0:T(8,128)(2,1)S(1)} %constant_dynamic-slice_fusion.6), channel_id=1, source_target_pairs={{0,16},{4,20},{8,24},{12,28},{16,0},{20,4},{24,8},{28,12},{1,17},{... | collective-permute-start | bytes 786440 | tf_op jit(solution)/shard_map/ppermute | solution.py:756
  187.1 1.3 add_convert_fusion.2
  188.4 1.4 collective-permute-start.24
  190.6 7.9 %back.1 = (bf16[2,400,256]{2,1,0:T(8,128)(2,1)}, bf16[2,400,256]{2,1,0:T(8,128)(2,1)}, bf16[512,768]{1,0:T(8,128)(2,1)}, f32[4,512]{1,0:T(4,128)}) custom-call(bf16[2,400,256]{2,1,0:T(8,128)(2,1)} %get-tuple-element.112.xm_ref, bf16[2,400,256]{2,1,0:T(8,128)(2,1)} %collective-permute-done.6.xo_ref, bf16[2,256,400]{2,1,0:T(8,128)(2,1)} %get-tuple-element.143.qm_ref, ...), custom_call_target="tpu_custom_call" | custom-call | flops 1 | bytes 1 | tf_op jit(solution)/shard_map/back/pallas_call | solution.py:669
  199.9 4.7 %select_out.2 = f32[4,392,256]{2,1,0:T(8,128)} custom-call(s32[1]{0:T(128)} %bitcast.core_ref, s32[2,4,392,1]{3,2,1,0:T(8,128)} %constant.90.clone.picks_ref, bf16[416,256]{1,0:T(8,128)(2,1)} %bitcast.61, bf16[416,256]{1,0:T(8,128)(2,1)} %collective-permute-done.23.beside_ref, bf16[416,256]{1,0:T(8,128)(2,1)} %copy-done.30, bf16[416,256]{1,0:T(8,128)(2,1)} %copy-done.31), custom_call_target="tpu_custom_call" | custom-call | flops 1 | bytes 1 | tf_op jit(solution)/shard_map/select_out/pallas_call | solution.py:731
  204.7 1.5 collective-permute-start.31
  207.1 1.3 collective-permute-done.28
  208.5 1.4 collective-permute-start.40
  211.1 10.2 %table_fold.2.init_ref = f32[256,160]{1,0:T(8,128)} custom-call(s32[1]{0:T(128)} %bitcast.core_ref, s32[208,400]{1,0:T(8,128)} %pad_dynamic-slice_fusion.idx_ref, bf16[8,208,512]{2,1,0:T(8,128)(2,1)} %get-tuple-element.155.pair_m, bf16[8,208,512]{2,1,0:T(8,128)(2,1)} %get-tuple-element.156.pair_o, bf16[8,208,512]{2,1,0:T(8,128)(2,1)} %copy-done.5, ...), custom_call_target="tpu_custom_call" | custom-call | flops 1 | bytes 1 | tf_op jit(solution)/shard_map/table_fold/pallas_call | solution.py:247
  222.4 1.0 collective-permute-start.46
  223.4 1.8 collective-permute-start.33
  225.2 12.0 %table_fold.3 = (f32[96,256]{1,0:T(8,128)}, f32[96,256]{1,0:T(8,128)}) custom-call(s32[1]{0:T(128)} %bitcast.core_ref, s32[208,400]{1,0:T(8,128)} %pad_dynamic-slice_fusion.idx_ref, bf16[8,208,512]{2,1,0:T(8,128)(2,1)} %get-tuple-element.155.pair_m, bf16[8,208,512]{2,1,0:T(8,128)(2,1)} %get-tuple-element.156.pair_o, bf16[8,208,512]{2,1,0:T(8,128)(2,1)} %copy-done.5, ...), custom_call_target="tpu_custom_call" | custom-call | flops 1 | bytes 1 | tf_op jit(solution)/shard_map/table_fold/pallas_call | solution.py:247
  237.4 1.1 collective-permute-start.38
  239.2 0.9 add.156
  240.1 1.4 collective-permute-start.35
  242.6 1.4 collective-permute-start.37
  244.1 1.0 collective-permute-done.35
  245.3 1.6 collective-permute-done.36
  247.4 1.0 collective-permute-done.37
  248.4 1.3 collective-permute-start.45
  249.8 4.9 %collective-permute-done.47 = bf16[1,1,1,32,1280]{4,3,2,1,0:T(8,128)(2,1)S(1)} collective-permute-done((bf16[1,1,1,32,1280]{4,3,2,1,0:T(8,128)(2,1)S(1)}, bf16[1,1,1,32,1280]{4,3,2,1,0:T(8,128)(2,1)S(1)}, u32[]{:S(2)}, u32[]{:S(2)}) %collective-permute-start.47) | collective-permute-done | bytes 81952 | tf_op jit(solution)/shard_map/ppermute | solution.py:756
  254.7 1.0 collective-permute-start.42
  256.4 1.2 collective-permute-start.43
  257.7 2.2 collective-permute-start.44
  260.5 4.7 %select_out.3 = f32[4,392,256]{2,1,0:T(8,128)} custom-call(s32[1]{0:T(128)} %bitcast.core_ref, s32[2,4,392,1]{3,2,1,0:T(8,128)} %constant.90.clone.picks_ref, bf16[416,256]{1,0:T(8,128)(2,1)} %bitcast.60, bf16[416,256]{1,0:T(8,128)(2,1)} %copy-done.27, bf16[416,256]{1,0:T(8,128)(2,1)} %copy-done.28, bf16[416,256]{1,0:T(8,128)(2,1)} %copy-done.29), custom_call_target="tpu_custom_call" | custom-call | flops 1 | bytes 1 | tf_op jit(solution)/shard_map/select_out/pallas_call | solution.py:731
  268.1 1.7 unpack.1
  (196 shorter events, 29.8 us)
Async XLA Ops:
  0.6 64.1 %copy-start = (s32[4,392]{1,0:T(4,128)S(1)}, s32[4,392]{1,0:T(4,128)}, u32[]{:S(2)}) copy-start(s32[4,392]{1,0:T(4,128)} %param.37) | copy-start | bytes 18820
  1.8 7.0 %collective-permute-start.1 = (bf16[1,1,1,64,768]{4,3,2,1,0:T(8,128)(2,1)S(1)}, bf16[1,1,1,64,768]{4,3,2,1,0:T(8,128)(2,1)S(1)}, u32[]{:S(2)}, u32[]{:S(2)}) collective-permute-start(bf16[1,1,1,64,768]{4,3,2,1,0:T(8,128)(2,1)S(1)} %reshape_reshape.3), channel_id=1, source_target_pairs={{0,8},{4,12},{8,0},{12,4},{16,24},{20,28},{24,16},{28,20},{1,9},{5... | collective-permute-start | bytes 294920 | tf_op jit(solution)/shard_map/ppermute | solution.py:756
  6.5 3.0 %collective-permute-start.2 = (f32[96,256]{1,0:T(8,128)}, f32[96,256]{1,0:T(8,128)S(1)}, u32[]{:S(2)}, u32[]{:S(2)}) collective-permute-start(f32[96,256]{1,0:T(8,128)} %pack.1.own_ref), channel_id=1, source_target_pairs={{0,1},{1,0},{2,3},{3,2},{4,5},{5,4},{6,7},{7,6},{8,9},{9,8},{10,11... | collective-permute-start | bytes 294920 | tf_op jit(solution)/shard_map/ppermute | solution.py:756
  9.5 18.4 %copy-start.14 = (bf16[1,4,392,256]{3,2,1,0:T(8,128)(2,1)S(1)}, bf16[1,4,392,256]{3,2,1,0:T(8,128)(2,1)}, u32[]{:S(2)}) copy-start(bf16[1,4,392,256]{3,2,1,0:T(8,128)(2,1)} %param.21) | copy-start | bytes 2408452
  9.5 23.3 %copy-start.33 = (bf16[64,1024]{1,0:T(8,128)(2,1)S(1)}, bf16[64,1024]{1,0:T(8,128)(2,1)}, u32[]{:S(2)}) copy-start(bf16[64,1024]{1,0:T(8,128)(2,1)} %param.32) | copy-start | bytes 393220
  9.5 23.3 %copy-start.37 = (bf16[256,64]{0,1:T(8,128)(2,1)S(1)}, bf16[256,64]{0,1:T(8,128)(2,1)}, u32[]{:S(2)}) copy-start(bf16[256,64]{0,1:T(8,128)(2,1)} %param.27) | copy-start | bytes 98308
  27.4 42.7 %collective-permute-start.11 = (bf16[16,208,512]{2,1,0:T(8,128)(2,1)}, bf16[16,208,512]{2,1,0:T(8,128)(2,1)S(1)}, u32[]{:S(2)}, u32[]{:S(2)}) collective-permute-start(bf16[16,208,512]{2,1,0:T(8,128)(2,1)} %table_lookup.1.own_ref), channel_id=1, source_target_pairs={{0,1},{1,0},{2,3},{3,2},{4,5},{5,4},{6,7},{7,6},{8,9},{9,8},{10,11... | collective-permute-start | bytes 10223624 | tf_op jit(solution)/shard_map/ppermute | solution.py:756
  28.7 16.3 %collective-permute-start = (bf16[800,256]{1,0:T(8,128)(2,1)}, bf16[800,256]{1,0:T(8,128)(2,1)}, u32[]{:S(2)}, u32[]{:S(2)}) collective-permute-start(bf16[800,256]{1,0:T(8,128)(2,1)} %bitcast.3), channel_id=1, source_target_pairs={{0,2},{2,0},{1,3},{3,1},{4,6},{6,4},{5,7},{7,5},{8,10},{10,8},{9,1... | collective-permute-start | bytes 1228808 | tf_op jit(solution)/shard_map/ppermute | solution.py:756
  30.2 12.1 %collective-permute-start.5 = (bf16[1,2,1,64,768]{4,3,2,1,0:T(8,128)(2,1)}, bf16[1,2,1,64,768]{4,3,2,1,0:T(8,128)(2,1)}, u32[]{:S(2)}, u32[]{:S(2)}) collective-permute-start(bf16[1,2,1,64,768]{4,3,2,1,0:T(8,128)(2,1)} %pad_maximum_fusion.9), channel_id=1, source_target_pairs={{0,16},{4,20},{8,24},{12,28},{16,0},{20,4},{24,8},{28,12},{1,17},{... | collective-permute-start | bytes 589832 | tf_op jit(solution)/shard_map/ppermute | solution.py:756
  33.5 12.5 %copy-start.32 = (bf16[1024,64]{0,1:T(8,128)(2,1)S(1)}, bf16[1024,64]{0,1:T(8,128)(2,1)}, u32[]{:S(2)}) copy-start(bf16[1024,64]{0,1:T(8,128)(2,1)} %param.34) | copy-start | bytes 393220
  33.5 11.4 %collective-permute-start.4 = (bf16[1,1,1,64,1280]{4,3,2,1,0:T(8,128)(2,1)}, bf16[1,1,1,64,1280]{4,3,2,1,0:T(8,128)(2,1)S(1)}, u32[]{:S(2)}, u32[]{:S(2)}) collective-permute-start(bf16[1,1,1,64,1280]{4,3,2,1,0:T(8,128)(2,1)} %maximum_bitcast_fusion), channel_id=1, source_target_pairs={{0,8},{4,12},{8,0},{12,4},{16,24},{20,28},{24,16},{28,20},{1,9},{5... | collective-permute-start | bytes 491528 | tf_op jit(solution)/shard_map/ppermute | solution.py:756
  43.3 12.6 %collective-permute-start.9 = (bf16[2,2,1,64,768]{4,3,2,1,0:T(8,128)(2,1)S(1)}, bf16[2,2,1,64,768]{4,3,2,1,0:T(8,128)(2,1)S(1)}, u32[]{:S(2)}, u32[]{:S(2)}) collective-permute-start(bf16[2,2,1,64,768]{4,3,2,1,0:T(8,128)(2,1)S(1)} %pad_maximum_fusion.6), channel_id=1, source_target_pairs={{0,4},{4,0},{8,12},{12,8},{16,20},{20,16},{24,28},{28,24},{1,5},{5... | collective-permute-start | bytes 1179656 | tf_op jit(solution)/shard_map/ppermute | solution.py:756
  45.9 16.6 %collective-permute-start.7 = (bf16[1,2,1,64,1280]{4,3,2,1,0:T(8,128)(2,1)S(1)}, bf16[1,2,1,64,1280]{4,3,2,1,0:T(8,128)(2,1)S(1)}, u32[]{:S(2)}, u32[]{:S(2)}) collective-permute-start(bf16[1,2,1,64,1280]{4,3,2,1,0:T(8,128)(2,1)S(1)} %pad_maximum_fusion.7), channel_id=1, source_target_pairs={{0,16},{4,20},{8,24},{12,28},{16,0},{20,4},{24,8},{28,12},{1,17},{... | collective-permute-start | bytes 983048 | tf_op jit(solution)/shard_map/ppermute | solution.py:756
  46.0 10.9 %collective-permute-start.8 = (bf16[1,1,1,64,1024]{4,3,2,1,0:T(8,128)(2,1)S(1)}, bf16[1,1,1,64,1024]{4,3,2,1,0:T(8,128)(2,1)S(1)}, u32[]{:S(2)}, u32[]{:S(2)}) collective-permute-start(bf16[1,1,1,64,1024]{4,3,2,1,0:T(8,128)(2,1)S(1)} %bitcast.70), channel_id=1, source_target_pairs={{0,8},{4,12},{8,0},{12,4},{16,24},{20,28},{24,16},{28,20},{1,9},{5... | collective-permute-start | bytes 393224 | tf_op jit(solution)/shard_map/ppermute | solution.py:756
  55.9 9.4 %collective-permute-start.6 = (bf16[2,400,256]{2,1,0:T(8,128)(2,1)}, bf16[2,400,256]{2,1,0:T(8,128)(2,1)}, u32[]{:S(2)}, u32[]{:S(2)}) collective-permute-start(bf16[2,400,256]{2,1,0:T(8,128)(2,1)} %get-tuple-element.210), channel_id=1, source_target_pairs={{0,1},{1,0},{2,3},{3,2},{4,5},{5,4},{6,7},{7,6},{8,9},{9,8},{10,11... | collective-permute-start | bytes 1228808 | tf_op jit(solution)/shard_map/ppermute | solution.py:756
  57.0 8.4 %collective-permute-start.10 = (bf16[512,768]{1,0:T(8,128)(2,1)}, bf16[512,768]{1,0:T(8,128)(2,1)}, u32[]{:S(2)}, u32[]{:S(2)}) collective-permute-start(bf16[512,768]{1,0:T(8,128)(2,1)} %bitcast.11.wm_ref), channel_id=1, source_target_pairs={{0,1},{1,0},{2,3},{3,2},{4,5},{5,4},{6,7},{7,6},{8,9},{9,8},{10,11... | collective-permute-start | bytes 2359304 | tf_op jit(solution)/shard_map/ppermute | solution.py:756
  64.2 25.0 %collective-permute-start.12 = (bf16[2,2,1,64,1280]{4,3,2,1,0:T(8,128)(2,1)}, bf16[2,2,1,64,1280]{4,3,2,1,0:T(8,128)(2,1)}, u32[]{:S(2)}, u32[]{:S(2)}) collective-permute-start(bf16[2,2,1,64,1280]{4,3,2,1,0:T(8,128)(2,1)} %pad_maximum_fusion.4), channel_id=1, source_target_pairs={{0,4},{4,0},{8,12},{12,8},{16,20},{20,16},{24,28},{28,24},{1,5},{5... | collective-permute-start | bytes 1966088 | tf_op jit(solution)/shard_map/ppermute | solution.py:756
  64.7 23.3 %collective-permute-start.13 = (bf16[1,2,1,64,1024]{4,3,2,1,0:T(8,128)(2,1)}, bf16[1,2,1,64,1024]{4,3,2,1,0:T(8,128)(2,1)}, u32[]{:S(2)}, u32[]{:S(2)}) collective-permute-start(bf16[1,2,1,64,1024]{4,3,2,1,0:T(8,128)(2,1)} %pad_maximum_fusion.8), channel_id=1, source_target_pairs={{0,16},{4,20},{8,24},{12,28},{16,0},{20,4},{24,8},{28,12},{1,17},{... | collective-permute-start | bytes 786440 | tf_op jit(solution)/shard_map/ppermute | solution.py:756
  90.6 3.2 %copy-start.3 = (bf16[2,2,2,64,1280]{4,3,2,1,0:T(8,128)(2,1)}, bf16[2,2,2,64,1280]{4,3,2,1,0:T(8,128)(2,1)S(1)}, u32[]{:S(2)}) copy-start(bf16[2,2,2,64,1280]{4,3,2,1,0:T(8,128)(2,1)S(1)} %pad_maximum_fusion) | copy-start | bytes 3932164
  90.6 3.2 %collective-permute-start.14 = (bf16[512,1280]{1,0:T(8,128)(2,1)S(1)}, bf16[512,1280]{1,0:T(8,128)(2,1)S(1)}, u32[]{:S(2)}, u32[]{:S(2)}) collective-permute-start(bf16[512,1280]{1,0:T(8,128)(2,1)S(1)} %bitcast.43), channel_id=1, source_target_pairs={{0,1},{1,0},{2,3},{3,2},{4,5},{5,4},{6,7},{7,6},{8,9},{9,8},{10,11... | collective-permute-start | bytes 3932168 | tf_op jit(solution)/shard_map/ppermute | solution.py:756
  91.9 11.4 %collective-permute-start.3 = (bf16[800,256]{1,0:T(8,128)(2,1)S(1)}, bf16[800,256]{1,0:T(8,128)(2,1)S(1)}, u32[]{:S(2)}, u32[]{:S(2)}) collective-permute-start(bf16[800,256]{1,0:T(8,128)(2,1)S(1)} %bitcast.65), channel_id=1, source_target_pairs={{0,2},{2,0},{1,3},{3,1},{4,6},{6,4},{5,7},{7,5},{8,10},{10,8},{9,1... | collective-permute-start | bytes 1228808 | tf_op jit(solution)/shard_map/ppermute | solution.py:756
  92.5 18.2 %collective-permute-start.16 = (bf16[2,2,1,64,1024]{4,3,2,1,0:T(8,128)(2,1)S(1)}, bf16[2,2,1,64,1024]{4,3,2,1,0:T(8,128)(2,1)S(1)}, u32[]{:S(2)}, u32[]{:S(2)}) collective-permute-start(bf16[2,2,1,64,1024]{4,3,2,1,0:T(8,128)(2,1)S(1)} %pad_maximum_fusion.5), channel_id=1, source_target_pairs={{0,4},{4,0},{8,12},{12,8},{16,20},{20,16},{24,28},{28,24},{1,5},{5... | collective-permute-start | bytes 1572872 | tf_op jit(solution)/shard_map/ppermute | solution.py:756
  110.8 3.3 %copy-start.7 = (bf16[2,2,2,64,1024]{4,3,2,1,0:T(8,128)(2,1)}, bf16[2,2,2,64,1024]{4,3,2,1,0:T(8,128)(2,1)S(1)}, u32[]{:S(2)}) copy-start(bf16[2,2,2,64,1024]{4,3,2,1,0:T(8,128)(2,1)S(1)} %pad_maximum_fusion.2) | copy-start | bytes 3145732
  110.8 3.3 %collective-permute-start.17 = (bf16[512,1024]{1,0:T(8,128)(2,1)S(1)}, bf16[512,1024]{1,0:T(8,128)(2,1)S(1)}, u32[]{:S(2)}, u32[]{:S(2)}) collective-permute-start(bf16[512,1024]{1,0:T(8,128)(2,1)S(1)} %bitcast.50), channel_id=1, source_target_pairs={{0,1},{1,0},{2,3},{3,2},{4,5},{5,4},{6,7},{7,6},{8,9},{9,8},{10,11... | collective-permute-start | bytes 3145736 | tf_op jit(solution)/shard_map/ppermute | solution.py:756
  111.0 3.2 %collective-permute-start.15 = (bf16[2,400,256]{2,1,0:T(8,128)(2,1)S(1)}, bf16[2,400,256]{2,1,0:T(8,128)(2,1)S(1)}, u32[]{:S(2)}, u32[]{:S(2)}) collective-permute-start(bf16[2,400,256]{2,1,0:T(8,128)(2,1)S(1)} %get-tuple-element.208), channel_id=1, source_target_pairs={{0,1},{1,0},{2,3},{3,2},{4,5},{5,4},{6,7},{7,6},{8,9},{9,8},{10,11... | collective-permute-start | bytes 1228808 | tf_op jit(solution)/shard_map/ppermute | solution.py:756
  138.5 16.3 %collective-permute-start.18 = (bf16[512,1024]{1,0:T(8,128)(2,1)S(1)}, bf16[512,1024]{1,0:T(8,128)(2,1)S(1)}, u32[]{:S(2)}, u32[]{:S(2)}) collective-permute-start(bf16[512,1024]{1,0:T(8,128)(2,1)S(1)} %get-tuple-element.203), channel_id=1, source_target_pairs={{0,1},{1,0},{2,3},{3,2},{4,5},{5,4},{6,7},{7,6},{8,9},{9,8},{10,11... | collective-permute-start | bytes 3145736 | tf_op jit(solution)/shard_map/ppermute | solution.py:756
  138.8 18.7 %collective-permute-start.19 = (bf16[512,1280]{1,0:T(8,128)(2,1)S(1)}, bf16[512,1280]{1,0:T(8,128)(2,1)}, u32[]{:S(2)}, u32[]{:S(2)}) collective-permute-start(bf16[512,1280]{1,0:T(8,128)(2,1)S(1)} %pad_maximum_fusion.1), channel_id=1, source_target_pairs={{0,1},{1,0},{2,3},{3,2},{4,5},{5,4},{6,7},{7,6},{8,9},{9,8},{10,11... | collective-permute-start | bytes 3932168 | tf_op jit(solution)/shard_map/ppermute | solution.py:756
  139.2 15.4 %copy-start.13 = (bf16[512,2304]{1,0:T(8,128)(2,1)S(1)}, bf16[512,2304]{1,0:T(8,128)(2,1)}, u32[]{:S(2)}) copy-start(bf16[512,2304]{1,0:T(8,128)(2,1)} %get-tuple-element.132) | copy-start | bytes 7077892
  156.0 4.8 %copy-start.20 = (bf16[2,400,256]{2,1,0:T(8,128)(2,1)S(1)}, bf16[2,400,256]{2,1,0:T(8,128)(2,1)}, u32[]{:S(2)}) copy-start(bf16[2,400,256]{2,1,0:T(8,128)(2,1)} %get-tuple-element.127) | copy-start | bytes 1228804
  156.0 4.8 %copy-start.21 = (bf16[2,400,256]{2,1,0:T(8,128)(2,1)S(1)}, bf16[2,400,256]{2,1,0:T(8,128)(2,1)}, u32[]{:S(2)}) copy-start(bf16[2,400,256]{2,1,0:T(8,128)(2,1)} %get-tuple-element.150) | copy-start | bytes 1228804
  156.0 26.2 %collective-permute-start.20 = (bf16[2,2,1,64,1024]{4,3,2,1,0:T(8,128)(2,1)}, bf16[2,2,1,64,1024]{4,3,2,1,0:T(8,128)(2,1)}, u32[]{:S(2)}, u32[]{:S(2)}) collective-permute-start(bf16[2,2,1,64,1024]{4,3,2,1,0:T(8,128)(2,1)} %constant_dynamic-slice_fusion.8), channel_id=1, source_target_pairs={{0,4},{4,0},{8,12},{12,8},{16,20},{20,16},{24,28},{28,24},{1,5},{5... | collective-permute-start | bytes 1572872 | tf_op jit(solution)/shard_map/ppermute | solution.py:756
  160.0 24.1 %collective-permute-start.21 = (bf16[2,2,2,32,1280]{4,3,2,1,0:T(8,128)(2,1)}, bf16[2,2,2,32,1280]{4,3,2,1,0:T(8,128)(2,1)}, u32[]{:S(2)}, u32[]{:S(2)}) collective-permute-start(bf16[2,2,2,32,1280]{4,3,2,1,0:T(8,128)(2,1)} %constant_dynamic-slice_fusion.7), channel_id=1, source_target_pairs={{0,2},{2,0},{1,3},{3,1},{4,6},{6,4},{5,7},{7,5},{8,10},{10,8},{9,1... | collective-permute-start | bytes 1966088 | tf_op jit(solution)/shard_map/ppermute | solution.py:756
  161.7 26.7 %collective-permute-start.23 = (bf16[416,256]{1,0:T(8,128)(2,1)}, bf16[416,256]{1,0:T(8,128)(2,1)}, u32[]{:S(2)}, u32[]{:S(2)}) collective-permute-start(bf16[416,256]{1,0:T(8,128)(2,1)} %bitcast.17), channel_id=1, source_target_pairs={{0,1},{1,0},{2,3},{3,2},{4,5},{5,4},{6,7},{7,6},{8,9},{9,8},{10,11... | collective-permute-start | bytes 638984 | tf_op jit(solution)/shard_map/ppermute | solution.py:756
  161.7 48.2 %collective-permute-start.30 = (bf16[8,208,512]{2,1,0:T(8,128)(2,1)}, bf16[8,208,512]{2,1,0:T(8,128)(2,1)S(1)}, u32[]{:S(2)}, u32[]{:S(2)}) collective-permute-start(bf16[8,208,512]{2,1,0:T(8,128)(2,1)} %get-tuple-element.159), channel_id=1, source_target_pairs={{0,1},{1,0},{2,3},{3,2},{4,5},{5,4},{6,7},{7,6},{8,9},{9,8},{10,11... | collective-permute-start | bytes 5111816 | tf_op jit(solution)/shard_map/ppermute | solution.py:756
  166.6 23.1 %collective-permute-start.22 = (bf16[512,768]{1,0:T(8,128)(2,1)}, bf16[512,768]{1,0:T(8,128)(2,1)S(1)}, u32[]{:S(2)}, u32[]{:S(2)}) collective-permute-start(bf16[512,768]{1,0:T(8,128)(2,1)} %side_grads.1), channel_id=1, source_target_pairs={{0,1},{1,0},{2,3},{3,2},{4,5},{5,4},{6,7},{7,6},{8,9},{9,8},{10,11... | collective-permute-start | bytes 2359304 | tf_op jit(solution)/shard_map/ppermute | solution.py:756
  182.2 26.3 %collective-permute-start.29 = (bf16[8,208,512]{2,1,0:T(8,128)(2,1)}, bf16[8,208,512]{2,1,0:T(8,128)(2,1)S(1)}, u32[]{:S(2)}, u32[]{:S(2)}) collective-permute-start(bf16[8,208,512]{2,1,0:T(8,128)(2,1)} %get-tuple-element.157), channel_id=1, source_target_pairs={{0,1},{1,0},{2,3},{3,2},{4,5},{5,4},{6,7},{7,6},{8,9},{9,8},{10,11... | collective-permute-start | bytes 5111816 | tf_op jit(solution)/shard_map/ppermute | solution.py:756
  184.1 20.6 %collective-permute-start.26 = (bf16[1,2,1,64,1024]{4,3,2,1,0:T(8,128)(2,1)S(1)}, bf16[1,2,1,64,1024]{4,3,2,1,0:T(8,128)(2,1)S(1)}, u32[]{:S(2)}, u32[]{:S(2)}) collective-permute-start(bf16[1,2,1,64,1024]{4,3,2,1,0:T(8,128)(2,1)S(1)} %constant_dynamic-slice_fusion.6), channel_id=1, source_target_pairs={{0,16},{4,20},{8,24},{12,28},{16,0},{20,4},{24,8},{28,12},{1,17},{... | collective-permute-start | bytes 786440 | tf_op jit(solution)/shard_map/ppermute | solution.py:756
  188.4 10.2 %collective-permute-start.24 = (bf16[416,256]{1,0:T(8,128)(2,1)}, bf16[416,256]{1,0:T(8,128)(2,1)S(1)}, u32[]{:S(2)}, u32[]{:S(2)}) collective-permute-start(bf16[416,256]{1,0:T(8,128)(2,1)} %bitcast.18), channel_id=1, source_target_pairs={{0,2},{2,0},{1,3},{3,1},{4,6},{6,4},{5,7},{7,5},{8,10},{10,8},{9,1... | collective-permute-start | bytes 638984 | tf_op jit(solution)/shard_map/ppermute | solution.py:756
  189.7 9.4 %collective-permute-start.25 = (bf16[416,256]{1,0:T(8,128)(2,1)}, bf16[416,256]{1,0:T(8,128)(2,1)S(1)}, u32[]{:S(2)}, u32[]{:S(2)}) collective-permute-start(bf16[416,256]{1,0:T(8,128)(2,1)} %bitcast.19), channel_id=1, source_target_pairs={{0,3},{1,2},{2,1},{3,0},{4,7},{5,6},{6,5},{7,4},{8,11},{9,10},{10,... | collective-permute-start | bytes 638984 | tf_op jit(solution)/shard_map/ppermute | solution.py:947
  198.5 6.1 %copy-start.18 = (bf16[512,768]{1,0:T(8,128)(2,1)S(1)}, bf16[512,768]{1,0:T(8,128)(2,1)}, u32[]{:S(2)}) copy-start(bf16[512,768]{1,0:T(8,128)(2,1)} %get-tuple-element.160) | copy-start | bytes 2359300
  198.6 9.8 %collective-permute-start.28 = (bf16[2,2,1,32,1280]{4,3,2,1,0:T(8,128)(2,1)S(1)}, bf16[2,2,1,32,1280]{4,3,2,1,0:T(8,128)(2,1)S(1)}, u32[]{:S(2)}, u32[]{:S(2)}) collective-permute-start(bf16[2,2,1,32,1280]{4,3,2,1,0:T(8,128)(2,1)S(1)} %constant_dynamic-slice_fusion.4), channel_id=1, source_target_pairs={{0,4},{4,0},{8,12},{12,8},{16,20},{20,16},{24,28},{28,24},{1,5},{5... | collective-permute-start | bytes 983048 | tf_op jit(solution)/shard_map/ppermute | solution.py:756
  204.7 16.6 %collective-permute-start.31 = (bf16[2,2,1,64,768]{4,3,2,1,0:T(8,128)(2,1)S(1)}, bf16[2,2,1,64,768]{4,3,2,1,0:T(8,128)(2,1)S(1)}, u32[]{:S(2)}, u32[]{:S(2)}) collective-permute-start(bf16[2,2,1,64,768]{4,3,2,1,0:T(8,128)(2,1)S(1)} %constant_dynamic-slice_fusion.3), channel_id=1, source_target_pairs={{0,4},{4,0},{8,12},{12,8},{16,20},{20,16},{24,28},{28,24},{1,5},{5... | collective-permute-start | bytes 1179656 | tf_op jit(solution)/shard_map/ppermute | solution.py:756
  206.3 15.2 %collective-permute-start.27 = (bf16[1,1,1,64,1024]{4,3,2,1,0:T(8,128)(2,1)S(1)}, bf16[1,1,1,64,1024]{4,3,2,1,0:T(8,128)(2,1)S(1)}, u32[]{:S(2)}, u32[]{:S(2)}) collective-permute-start(bf16[1,1,1,64,1024]{4,3,2,1,0:T(8,128)(2,1)S(1)} %constant_dynamic-slice_fusion.5), channel_id=1, source_target_pairs={{0,8},{4,12},{8,0},{12,4},{16,24},{20,28},{24,16},{28,20},{1,9},{5... | collective-permute-start | bytes 393224 | tf_op jit(solution)/shard_map/ppermute | solution.py:756
  208.4 48.1 %collective-permute-start.39 = (bf16[416,256]{1,0:T(8,128)(2,1)S(1)}, bf16[416,256]{1,0:T(8,128)(2,1)S(1)}, u32[]{:S(2)}, u32[]{:S(2)}) collective-permute-start(bf16[416,256]{1,0:T(8,128)(2,1)S(1)} %bitcast.69), channel_id=1, source_target_pairs={{0,1},{1,0},{2,3},{3,2},{4,5},{5,4},{6,7},{7,6},{8,9},{9,8},{10,11... | collective-permute-start | bytes 638984 | tf_op jit(solution)/shard_map/ppermute | solution.py:756
  208.5 49.2 %collective-permute-start.40 = (bf16[416,256]{1,0:T(8,128)(2,1)S(1)}, bf16[416,256]{1,0:T(8,128)(2,1)S(1)}, u32[]{:S(2)}, u32[]{:S(2)}) collective-permute-start(bf16[416,256]{1,0:T(8,128)(2,1)S(1)} %bitcast.68), channel_id=1, source_target_pairs={{0,2},{2,0},{1,3},{3,1},{4,6},{6,4},{5,7},{7,5},{8,10},{10,8},{9,1... | collective-permute-start | bytes 638984 | tf_op jit(solution)/shard_map/ppermute | solution.py:756
  209.9 11.5 %collective-permute-start.32 = (bf16[1,2,1,32,1280]{4,3,2,1,0:T(8,128)(2,1)S(1)}, bf16[1,2,1,32,1280]{4,3,2,1,0:T(8,128)(2,1)S(1)}, u32[]{:S(2)}, u32[]{:S(2)}) collective-permute-start(bf16[1,2,1,32,1280]{4,3,2,1,0:T(8,128)(2,1)S(1)} %constant_dynamic-slice_fusion.2), channel_id=1, source_target_pairs={{0,16},{4,20},{8,24},{12,28},{16,0},{20,4},{24,8},{28,12},{1,17},{... | collective-permute-start | bytes 491528 | tf_op jit(solution)/shard_map/ppermute | solution.py:756
  221.5 15.7 %collective-permute-start.48 = (bf16[64,1024]{1,0:T(8,128)(2,1)S(1)}, bf16[64,1024]{1,0:T(8,128)(2,1)S(1)}, u32[]{:S(2)}, u32[]{:S(2)}) collective-permute-start(bf16[64,1024]{1,0:T(8,128)(2,1)S(1)} %bitcast.64), channel_id=1, source_target_pairs={{0,2},{2,0},{1,3},{3,1},{4,6},{6,4},{5,7},{7,5},{8,10},{10,8},{9,1... | collective-permute-start | bytes 393224 | tf_op jit(solution)/shard_map/ppermute | solution.py:756
  222.4 14.8 %collective-permute-start.46 = (bf16[1,1,1,32,1280]{4,3,2,1,0:T(8,128)(2,1)S(1)}, bf16[1,1,1,32,1280]{4,3,2,1,0:T(8,128)(2,1)S(1)}, u32[]{:S(2)}, u32[]{:S(2)}) collective-permute-start(bf16[1,1,1,32,1280]{4,3,2,1,0:T(8,128)(2,1)S(1)} %constant_dynamic-slice_fusion.10), channel_id=1, source_target_pairs={{0,8},{4,12},{8,0},{12,4},{16,24},{20,28},{24,16},{28,20},{1,9},{5... | collective-permute-start | bytes 245768 | tf_op jit(solution)/shard_map/ppermute | solution.py:756
  223.4 13.8 %collective-permute-start.33 = (bf16[1,2,1,64,768]{4,3,2,1,0:T(8,128)(2,1)S(1)}, bf16[1,2,1,64,768]{4,3,2,1,0:T(8,128)(2,1)S(1)}, u32[]{:S(2)}, u32[]{:S(2)}) collective-permute-start(bf16[1,2,1,64,768]{4,3,2,1,0:T(8,128)(2,1)S(1)} %constant_dynamic-slice_fusion.1), channel_id=1, source_target_pairs={{0,16},{4,20},{8,24},{12,28},{16,0},{20,4},{24,8},{28,12},{1,17},{... | collective-permute-start | bytes 589832 | tf_op jit(solution)/shard_map/ppermute | solution.py:756
  237.3 1.9 collective-permute-start.34
  237.4 5.2 %collective-permute-start.38 = (bf16[1,1,1,64,768]{4,3,2,1,0:T(8,128)(2,1)S(1)}, bf16[1,1,1,64,768]{4,3,2,1,0:T(8,128)(2,1)S(1)}, u32[]{:S(2)}, u32[]{:S(2)}) collective-permute-start(bf16[1,1,1,64,768]{4,3,2,1,0:T(8,128)(2,1)S(1)} %constant_dynamic-slice_fusion), channel_id=1, source_target_pairs={{0,8},{4,12},{8,0},{12,4},{16,24},{20,28},{24,16},{28,20},{1,9},{5... | collective-permute-start | bytes 294920 | tf_op jit(solution)/shard_map/ppermute | solution.py:756
  240.1 4.9 %collective-permute-start.35 = (f32[96,256]{1,0:T(8,128)S(1)}, f32[96,256]{1,0:T(8,128)S(1)}, u32[]{:S(2)}, u32[]{:S(2)}) collective-permute-start(f32[96,256]{1,0:T(8,128)S(1)} %add.156), channel_id=1, source_target_pairs={{0,2},{2,0},{4,6},{6,4},{8,10},{10,8},{12,14},{14,12},{16,18},{18,... | collective-permute-start | bytes 294920 | tf_op jit(solution)/shard_map/ppermute | solution.py:837
  241.5 5.4 %collective-permute-start.36 = (f32[96,256]{1,0:T(8,128)S(1)}, f32[96,256]{1,0:T(8,128)S(1)}, u32[]{:S(2)}, u32[]{:S(2)}) collective-permute-start(f32[96,256]{1,0:T(8,128)S(1)} %add.156), channel_id=1, source_target_pairs={{0,4},{2,6},{4,0},{6,2},{8,12},{10,14},{12,8},{14,10},{16,20},{18,... | collective-permute-start | bytes 294920 | tf_op jit(solution)/shard_map/ppermute | solution.py:837
  242.6 5.8 %collective-permute-start.37 = (f32[96,256]{1,0:T(8,128)S(1)}, f32[96,256]{1,0:T(8,128)S(1)}, u32[]{:S(2)}, u32[]{:S(2)}) collective-permute-start(f32[96,256]{1,0:T(8,128)S(1)} %add.156), channel_id=1, source_target_pairs={{0,6},{2,4},{4,2},{6,0},{8,14},{10,12},{12,10},{14,8},{16,22},{18,... | collective-permute-start | bytes 294920 | tf_op jit(solution)/shard_map/ppermute | solution.py:837
  245.1 14.8 %collective-permute-start.41 = (bf16[416,256]{1,0:T(8,128)(2,1)S(1)}, bf16[416,256]{1,0:T(8,128)(2,1)S(1)}, u32[]{:S(2)}, u32[]{:S(2)}) collective-permute-start(bf16[416,256]{1,0:T(8,128)(2,1)S(1)} %bitcast.67), channel_id=1, source_target_pairs={{0,3},{1,2},{2,1},{3,0},{4,7},{5,6},{6,5},{7,4},{8,11},{9,10},{10,... | collective-permute-start | bytes 638984 | tf_op jit(solution)/shard_map/ppermute | solution.py:947
  246.8 7.8 %collective-permute-start.47 = (bf16[1,1,1,32,1280]{4,3,2,1,0:T(8,128)(2,1)S(1)}, bf16[1,1,1,32,1280]{4,3,2,1,0:T(8,128)(2,1)S(1)}, u32[]{:S(2)}, u32[]{:S(2)}) collective-permute-start(bf16[1,1,1,32,1280]{4,3,2,1,0:T(8,128)(2,1)S(1)} %add_convert_fusion.11), channel_id=1, source_target_pairs={{0,2},{2,0},{1,3},{3,1},{4,6},{6,4},{5,7},{7,5},{8,10},{10,8},{9,1... | collective-permute-start | bytes 245768 | tf_op jit(solution)/shard_map/ppermute | solution.py:756
  248.4 16.9 %collective-permute-start.45 = (bf16[64,768]{1,0:T(8,128)(2,1)S(1)}, bf16[64,768]{1,0:T(8,128)(2,1)S(1)}, u32[]{:S(2)}, u32[]{:S(2)}) collective-permute-start(bf16[64,768]{1,0:T(8,128)(2,1)S(1)} %bitcast.66), channel_id=1, source_target_pairs={{0,2},{2,0},{1,3},{3,1},{4,6},{6,4},{5,7},{7,5},{8,10},{10,8},{9,1... | collective-permute-start | bytes 294920 | tf_op jit(solution)/shard_map/ppermute | solution.py:756
  249.8 15.5 %copy-start.26 = (f32[96,256]{1,0:T(8,128)}, f32[96,256]{1,0:T(8,128)S(1)}, u32[]{:S(2)}) copy-start(f32[96,256]{1,0:T(8,128)S(1)} %add_add_fusion.a_ref) | copy-start | bytes 294916
  254.7 12.1 %collective-permute-start.42 = (f32[96,256]{1,0:T(8,128)S(1)}, f32[96,256]{1,0:T(8,128)S(1)}, u32[]{:S(2)}, u32[]{:S(2)}) collective-permute-start(f32[96,256]{1,0:T(8,128)S(1)} %add_add_fusion.a_ref), channel_id=1, source_target_pairs={{0,8},{2,10},{4,12},{6,14},{8,0},{10,2},{12,4},{14,6},{16,24},{18,... | collective-permute-start | bytes 294920 | tf_op jit(solution)/shard_map/ppermute | solution.py:837
  256.4 3.4 %copy-start.27 = (bf16[416,256]{1,0:T(8,128)(2,1)}, bf16[416,256]{1,0:T(8,128)(2,1)S(1)}, u32[]{:S(2)}) copy-start(bf16[416,256]{1,0:T(8,128)(2,1)S(1)} %collective-permute-done.39.beside_ref) | copy-start | bytes 638980
  256.4 10.3 %collective-permute-start.43 = (f32[96,256]{1,0:T(8,128)S(1)}, f32[96,256]{1,0:T(8,128)S(1)}, u32[]{:S(2)}, u32[]{:S(2)}) collective-permute-start(f32[96,256]{1,0:T(8,128)S(1)} %add_add_fusion.a_ref), channel_id=1, source_target_pairs={{0,16},{2,18},{4,20},{6,22},{8,24},{10,26},{12,28},{14,30},{16,0},... | collective-permute-start | bytes 294920 | tf_op jit(solution)/shard_map/ppermute | solution.py:837
  257.7 2.2 copy-start.28
  257.7 9.1 %collective-permute-start.44 = (f32[96,256]{1,0:T(8,128)S(1)}, f32[96,256]{1,0:T(8,128)S(1)}, u32[]{:S(2)}, u32[]{:S(2)}) collective-permute-start(f32[96,256]{1,0:T(8,128)S(1)} %add_add_fusion.a_ref), channel_id=1, source_target_pairs={{0,24},{2,26},{4,28},{6,30},{8,16},{10,18},{12,20},{14,22},{16,8},... | collective-permute-start | bytes 294920 | tf_op jit(solution)/shard_map/ppermute | solution.py:837
  260.5 9.3 %copy-start.1 = (s32[4,392]{1,0:T(4,128)S(1)}, s32[4,392]{1,0:T(4,128)}, u32[]{:S(2)}) copy-start(s32[4,392]{1,0:T(4,128)} %param.37) | copy-start | bytes 18820
  (23 other events, 24.4 us)
